TPU v7x, 32 devices: a whole 2x2x4 slice. The times are simulated.
32 devices in a mesh: seq: 16 (over z, y, core), img: 2 (over x).
Axes of the slice: x: 2, y: 2, z: 4, core: 2. Of those that a mesh axis runs over, the one named last changes fastest.
Arguments:
- pixels: int32 [16, 24, 128], P('img', None, 'seq'), may hold values from 0 to 255
- loss_mask: int32 [16, 24, 128], P('img', None, 'seq'), may hold values from 0 to 1, as said below
- tok_table: float32 [256, 256], P(None, 'seq'), may hold values from -1.2 to 1.2
- pos_table: float32 [67, 256], P(None, 'seq'), may hold values from -0.9 to 0.9
- attn_in: float32 [3, 256, 768], P(None, 'seq'), may hold values from -0.375 to 0.375
- attn_out: float32 [3, 256, 256], P(None, 'seq'), may hold values from -1.5 to 1.5
- ffn_in: float32 [3, 256, 512], P(None, 'seq'), may hold values from -0.375 to 0.375
- ffn_out: float32 [3, 512, 256], P(None, None, 'seq'), may hold values from -0.25 to 0.25
- head_table: float32 [256, 256], P('seq'), may hold values from -0.75 to 0.75
- norms: float32 [7, 2, 256], P(None, None, 'seq')
- tok_first: float32 [256, 256], P(None, 'seq')
- pos_first: float32 [67, 256], P(None, 'seq')
- in_first: float32 [3, 256, 768], P(None, 'seq')
- out_first: float32 [3, 256, 256], P(None, 'seq')
- up_first: float32 [3, 256, 512], P(None, 'seq')
- down_first: float32 [3, 512, 256], P(None, None, 'seq')
- head_first: float32 [256, 256], P('seq')
- norm_first: float32 [7, 2, 256], P(None, None, 'seq')
- tok_second: float32 [256, 256], P(None, 'seq')
- pos_second: float32 [67, 256], P(None, 'seq')
- in_second: float32 [3, 256, 768], P(None, 'seq')
- out_second: float32 [3, 256, 256], P(None, 'seq')
- up_second: float32 [3, 256, 512], P(None, 'seq')
- down_second: float32 [3, 512, 256], P(None, None, 'seq')
- head_second: float32 [256, 256], P('seq')
- norm_second: float32 [7, 2, 256], P(None, None, 'seq')
Outputs:
- loss_sum: float32 [], replicated
- loss_count: float32 [], replicated
- grad_norm: float32 [], replicated
- new_tok: float32 [256, 256], P(None, 'seq')
- new_pos: float32 [67, 256], P(None, 'seq')
- new_in: float32 [3, 256, 768], P(None, 'seq')
- new_out: float32 [3, 256, 256], P(None, 'seq')
- new_up: float32 [3, 256, 512], P(None, 'seq')
- new_down: float32 [3, 512, 256], P(None, None, 'seq')
- new_head: float32 [256, 256], P('seq')
- new_norms: float32 [7, 2, 256], P(None, None, 'seq')
- tok_first_new: float32 [256, 256], P(None, 'seq')
- pos_first_new: float32 [67, 256], P(None, 'seq')
- in_first_new: float32 [3, 256, 768], P(None, 'seq')
- out_first_new: float32 [3, 256, 256], P(None, 'seq')
- up_first_new: float32 [3, 256, 512], P(None, 'seq')
- down_first_new: float32 [3, 512, 256], P(None, None, 'seq')
- head_first_new: float32 [256, 256], P('seq')
- norm_first_new: float32 [7, 2, 256], P(None, None, 'seq')
- tok_second_new: float32 [256, 256], P(None, 'seq')
- pos_second_new: float32 [67, 256], P(None, 'seq')
- in_second_new: float32 [3, 256, 768], P(None, 'seq')
- out_second_new: float32 [3, 256, 256], P(None, 'seq')
- up_second_new: float32 [3, 256, 512], P(None, 'seq')
- down_second_new: float32 [3, 512, 256], P(None, None, 'seq')
- head_second_new: float32 [256, 256], P('seq')
- norm_second_new: float32 [7, 2, 256], P(None, None, 'seq')
Inputs may be any that keep to these rules, and one draw needn't show every extreme that they name: `loss_mask`: 0 or 1; position 0 of every image is supervised.
All inputs are finite; a program needn't handle non-finite values.
Results may differ from a plain program's by a relative error of at most 0.012.
Values may be sent and summed in bfloat16 or wider, within the bound.
A program may use at most 320 MiB of HBM per device.

v0:
```python
import jax
import jax.numpy as jnp
from jax import lax
from jax.sharding import PartitionSpec as P

D = 256
HEAD = 128
V = 256
STRIDE = 128
BLK = 24
LAYERS = 3
STEP = 10
SIDE = 32


HIGHEST = lax.Precision.HIGHEST
CLIP_NORM = 0.05
BETA_ONE = 0.9
BETA_TWO = 0.95
LEARN_RATE = 0.1
WEIGHT_DECAY = 0.1
ADAM_EPS = 1e-08
SMOOTHING = 0.1
NORM_EPS = 1e-05
WINDOW_FORMS = ("...brh,...bjh->...brj", "...brj,...bjh->...brh", "...brj,...brh->...bjh")
STRIDE_FORMS = ("...brh,...crh->...brc", "...brc,...crh->...brh", "...brc,...brh->...crh")


def shifted(x, axis, by):
    peers = lax.axis_size(axis)
    pairs = [(i, i + by) for i in range(peers) if 0 <= i + by < peers]
    return lax.ppermute(x, axis, pairs)


def shifted_2(x, axis, by):
    peers = lax.axis_size(axis)
    return lax.ppermute(x, axis, [(i, (i + by) % peers) for i in range(peers)])


def layer_norm(values, gain_pair):
    centre = values - jnp.mean(values, -1, keepdims=True)
    spread = jnp.mean(centre * centre, -1, keepdims=True)
    return centre * lax.rsqrt(spread + NORM_EPS) * (1.0 + gain_pair[0]) + gain_pair[1]


def norm_back(values, gain_pair, gradient):
    _, pull = jax.vjp(layer_norm, values, gain_pair)
    return pull(gradient)


def product(form, left, right):
    return jnp.einsum(form, left, right, preferred_element_type=jnp.float32)


def window_allowed(block_index, residues):
    key_index = jnp.arange(2 * STRIDE, dtype=jnp.int32)
    distance = STRIDE + residues[:, None] - key_index[None, :]
    nearby = (distance >= 0) & (distance < STRIDE)
    started = (block_index[:, None, None] > 0) | (key_index[None, None, :] >= STRIDE)
    return nearby[None] & started


def stride_allowed(blocks):
    block_index = jnp.arange(blocks, dtype=jnp.int32)
    return (block_index[:, None] >= block_index[None, :])[:, None, :]


def softmax_rows(query, key_rows, allowed, forms):
    raw = product(forms[0], query, key_rows)
    return jax.nn.softmax(jnp.where(allowed, raw * HEAD ** (-0.5), -1e30), axis=-1)


def attend_out(query, key_rows, value_rows, allowed, forms):
    probs = softmax_rows(query, key_rows, allowed, forms).astype(jnp.bfloat16)
    return product(forms[1], probs, value_rows)


def attend_back(query, key_rows, value_rows, allowed, grad_out, forms):
    probs = softmax_rows(query, key_rows, allowed, forms)
    d_probs = product(forms[0], grad_out, value_rows)
    centred = d_probs - jnp.sum(probs * d_probs, -1, keepdims=True)
    d_raw = (probs * centred * HEAD ** (-0.5)).astype(jnp.bfloat16)
    d_query = product(forms[1], d_raw, key_rows)
    d_key = product(forms[2], d_raw, query)
    d_value = product(forms[2], probs.astype(jnp.bfloat16), grad_out)
    return (d_query, d_key, d_value)


def block_joined(pairs):
    edge = shifted(pairs[-1:], "seq", 1)
    return jnp.concatenate([jnp.concatenate([edge, pairs[:-1]], 0), pairs], 1)


def split_heads(mixed, shape_four):
    pieces = jnp.split(mixed.reshape(shape_four + (6 * HEAD,)), 6, -1)
    return pieces


def layer_forward(state, w_in, w_out, w_up, w_down, pair_one, pair_two, masks, shape_four):
    row_count = state.shape[0]
    n_images, blocks, res_dev = shape_four
    hidden = layer_norm(state, pair_one).astype(jnp.bfloat16)
    mixed = jnp.dot(hidden, w_in, preferred_element_type=jnp.float32).astype(jnp.bfloat16)
    query0, query1, key0, key1, value0, value1 = split_heads(mixed, shape_four)
    stored_keys = None
    packed = jnp.concatenate([query0, key0, value0], -1).reshape(
        n_images * blocks, res_dev, 3 * HEAD
    )
    local = lax.all_to_all(packed, "seq", split_axis=0, concat_axis=1, tiled=True)
    joined = block_joined(local[..., HEAD:])
    out_local = attend_out(
        local[..., :HEAD], joined[..., :HEAD], joined[..., HEAD:], masks[2], WINDOW_FORMS
    )
    out0 = lax.all_to_all(
        out_local.astype(jnp.bfloat16), "seq", split_axis=1, concat_axis=0, tiled=True
    ).reshape(shape_four + (HEAD,))
    out1 = attend_out(query1, key1, value1, masks[1], STRIDE_FORMS)
    heads = (
        jnp.concatenate([out0.astype(jnp.float32), out1], -1)
        .reshape(row_count, 2 * HEAD)
        .astype(jnp.bfloat16)
    )
    middle = state + jnp.dot(heads, w_out, preferred_element_type=jnp.float32)
    hidden_two = layer_norm(middle, pair_two).astype(jnp.bfloat16)
    upper = jnp.dot(hidden_two, w_up, preferred_element_type=jnp.float32)
    active = jax.nn.gelu(upper).astype(jnp.bfloat16)
    result = middle + jnp.dot(active, w_down, preferred_element_type=jnp.float32)
    return (result, (state, mixed, stored_keys, heads, middle, upper, active))


def layer_backward(
    gradient, stored, w_in, w_out, w_up, w_down, pair_one, pair_two, masks, shape_four
):
    state, mixed, stored_keys, heads, middle, upper, active = stored
    row_count = state.shape[0]
    n_images, blocks, res_dev = shape_four
    grad_down = gradient.astype(jnp.bfloat16)
    g_down = product("rf,rd->fd", active, grad_down)
    d_active = product("rd,fd->rf", grad_down, w_down)
    _, gelu_pull = jax.vjp(jax.nn.gelu, upper)
    d_upper = gelu_pull(d_active)[0].astype(jnp.bfloat16)
    hidden_two = layer_norm(middle, pair_two).astype(jnp.bfloat16)
    g_up = product("rd,rf->df", hidden_two, d_upper)
    d_hidden_two = product("rf,df->rd", d_upper, w_up)
    d_middle, g_pair_two = norm_back(middle, pair_two, d_hidden_two)
    gradient = gradient + d_middle
    grad_out = gradient.astype(jnp.bfloat16)
    g_out = product("re,rd->ed", heads, grad_out)
    d_heads = (
        product("rd,ed->re", grad_out, w_out).astype(jnp.bfloat16).reshape(shape_four + (2 * HEAD,))
    )
    d_out0 = d_heads[..., :HEAD]
    d_out1 = d_heads[..., HEAD:]
    query0, query1, key0, key1, value0, value1 = split_heads(mixed, shape_four)
    packed = jnp.concatenate([query0, key0, value0, d_out0], -1).reshape(
        n_images * blocks, res_dev, 4 * HEAD
    )
    local = lax.all_to_all(packed, "seq", split_axis=0, concat_axis=1, tiled=True)
    joined = block_joined(local[..., HEAD : 3 * HEAD])
    d_query_local, d_key, d_value = attend_back(
        local[..., :HEAD],
        joined[..., :HEAD],
        joined[..., HEAD:],
        masks[2],
        local[..., 3 * HEAD :],
        WINDOW_FORMS,
    )
    both = jnp.concatenate([d_key, d_value], -1)
    earlier = both[:, :STRIDE]
    incoming = shifted(earlier[:1], "seq", -1)
    summed = both[:, STRIDE:] + jnp.concatenate([earlier[1:], incoming], 0)
    reply = jnp.concatenate([d_query_local, summed], -1).astype(jnp.bfloat16)
    back = lax.all_to_all(reply, "seq", split_axis=1, concat_axis=0, tiled=True).reshape(
        shape_four + (3 * HEAD,)
    )
    d_query0 = back[..., :HEAD]
    d_local = back[..., HEAD:]
    d_query1, d_key1, d_value1 = attend_back(query1, key1, value1, masks[1], d_out1, STRIDE_FORMS)
    d_mixed = jnp.concatenate(
        [
            d_query0.astype(jnp.float32),
            d_query1,
            d_local[..., :HEAD].astype(jnp.float32),
            d_key1,
            d_local[..., HEAD:].astype(jnp.float32),
            d_value1,
        ],
        -1,
    )
    d_mixed = d_mixed.reshape(row_count, 6 * HEAD).astype(jnp.bfloat16)
    hidden = layer_norm(state, pair_one).astype(jnp.bfloat16)
    g_in = product("rd,re->de", hidden, d_mixed)
    d_hidden = product("re,de->rd", d_mixed, w_in)
    d_state, g_pair_one = norm_back(state, pair_one, d_hidden)
    return (gradient + d_state, (g_in, g_out, g_up, g_down, g_pair_one, g_pair_two))


def position_rows(place):
    columns = jnp.arange(2 * SIDE + 3, dtype=jnp.int32)[None, :]
    hits = (columns == (place // (3 * SIDE))[:, None]) | (
        columns == (SIDE + place // 3 % SIDE)[:, None]
    )
    hits = hits | (columns == (2 * SIDE + place % 3)[:, None])
    return hits.astype(jnp.float32)


def adam_step(master, gradient, first, second, factor):
    gradient = gradient * factor
    first = BETA_ONE * first + (1.0 - BETA_ONE) * gradient
    second = BETA_TWO * second + (1.0 - BETA_TWO) * gradient * gradient
    moved = first / (1.0 - BETA_ONE**STEP) / (jnp.sqrt(second / (1.0 - BETA_TWO**STEP)) + ADAM_EPS)
    return (master - LEARN_RATE * (moved + WEIGHT_DECAY * master), first, second)


def on_device(
    pixels,
    loss_mask,
    tok_table,
    pos_table,
    attn_in,
    attn_out,
    ffn_in,
    ffn_out,
    head_table,
    norms,
    tok_first,
    pos_first,
    in_first,
    out_first,
    up_first,
    down_first,
    head_first,
    norm_first,
    tok_second,
    pos_second,
    in_second,
    out_second,
    up_second,
    down_second,
    head_second,
    norm_second,
):
    bfloat = jnp.bfloat16
    tok_w, pos_w, in_w, out_w, up_w, down_w, head_w, norm_w = (
        lax.all_gather(tok_table.astype(bfloat), "seq", axis=1, tiled=True),
        lax.all_gather(pos_table.astype(bfloat), "seq", axis=1, tiled=True),
        lax.all_gather(attn_in.astype(bfloat), "seq", axis=1, tiled=True),
        lax.all_gather(attn_out.astype(bfloat), "seq", axis=1, tiled=True),
        lax.all_gather(ffn_in.astype(bfloat), "seq", axis=1, tiled=True),
        lax.all_gather(ffn_out.astype(bfloat), "seq", axis=2, tiled=True),
        lax.all_gather(head_table.astype(bfloat), "seq", axis=0, tiled=True),
        lax.all_gather(norms.astype(bfloat), "seq", axis=2, tiled=True),
    )
    norm_float = norm_w.astype(jnp.float32)
    n_images, blocks, res_dev = pixels.shape
    shape_four = (n_images, blocks, res_dev)
    row_count = n_images * blocks * res_dev
    residues = lax.axis_index("seq") * res_dev + jnp.arange(res_dev, dtype=jnp.int32)
    carried = shifted_2(pixels[:, :, res_dev - 1], "seq", 1)
    earlier = jnp.concatenate([jnp.full((n_images, 1), -1, jnp.int32), carried[:, :-1]], 1)
    carried = jnp.where(lax.axis_index("seq") == 0, earlier, carried)
    input_ids = jnp.concatenate([carried[:, :, None], pixels[:, :, :-1]], 2).reshape(row_count)
    place = (jnp.arange(blocks, dtype=jnp.int32)[:, None] * STRIDE + residues[None, :]).reshape(-1)
    pos_hot = position_rows(place)
    tok_hot = (input_ids[:, None] == jnp.arange(V, dtype=jnp.int32)[None, :]).astype(jnp.float32)
    pos_part = jnp.dot(pos_hot.astype(bfloat), pos_w, preferred_element_type=jnp.float32)
    state = jnp.dot(tok_hot.astype(bfloat), tok_w, preferred_element_type=jnp.float32)
    state = (state.reshape(n_images, blocks * res_dev, D) + pos_part[None]).reshape(row_count, D)
    local_blocks = n_images * blocks // lax.axis_size("seq")
    block_in_image = (
        lax.axis_index("seq") * local_blocks + jnp.arange(local_blocks, dtype=jnp.int32)
    ) % BLK
    masks = (
        window_allowed(jnp.arange(blocks, dtype=jnp.int32), residues),
        stride_allowed(blocks),
        window_allowed(block_in_image, jnp.arange(STRIDE, dtype=jnp.int32)),
    )
    stored_all = []
    for layer_at in range(LAYERS):
        state, stored = layer_forward(
            state,
            in_w[layer_at],
            out_w[layer_at],
            up_w[layer_at],
            down_w[layer_at],
            norm_float[2 * layer_at],
            norm_float[2 * layer_at + 1],
            masks,
            shape_four,
        )
        stored_all.append(stored)
    final_pair = norm_float[2 * LAYERS]
    hidden = layer_norm(state, final_pair).astype(bfloat)
    logits = jnp.dot(hidden, head_w, preferred_element_type=jnp.float32)
    log_probs = jax.nn.log_softmax(logits, -1)
    target_hot = (
        pixels.reshape(row_count)[:, None] == jnp.arange(V, dtype=jnp.int32)[None, :]
    ).astype(jnp.float32)
    per_token = -(
        (1.0 - SMOOTHING) * jnp.sum(target_hot * log_probs, -1)
        + SMOOTHING * jnp.mean(log_probs, -1)
    )
    mask_rows = loss_mask.reshape(row_count).astype(jnp.float32)
    loss_sum, loss_count = lax.psum(
        (jnp.sum(mask_rows * per_token), jnp.sum(mask_rows)), ("seq", "img")
    )
    d_logits = (mask_rows / loss_count)[:, None] * (
        jnp.exp(log_probs) - (1.0 - SMOOTHING) * target_hot - SMOOTHING / V
    )
    d_logits = d_logits.astype(bfloat)
    g_head = product("rd,rv->dv", hidden, d_logits)
    d_hidden = product("rv,dv->rd", d_logits, head_w)
    gradient, g_final = norm_back(state, final_pair, d_hidden)
    layer_grads = [None] * LAYERS
    for layer_at in reversed(range(LAYERS)):
        gradient, layer_grads[layer_at] = layer_backward(
            gradient,
            stored_all[layer_at],
            in_w[layer_at],
            out_w[layer_at],
            up_w[layer_at],
            down_w[layer_at],
            norm_float[2 * layer_at],
            norm_float[2 * layer_at + 1],
            masks,
            shape_four,
        )
    g_tok = jnp.einsum("rv,rd->vd", tok_hot, gradient, precision=HIGHEST)
    summed_rows = jnp.sum(gradient.reshape(n_images, blocks * res_dev, D), 0)
    g_pos = jnp.einsum("rp,rd->pd", pos_hot, summed_rows, precision=HIGHEST)
    g_in = jnp.stack([item[0] for item in layer_grads])
    g_out = jnp.stack([item[1] for item in layer_grads])
    g_up = jnp.stack([item[2] for item in layer_grads])
    g_down = jnp.stack([item[3] for item in layer_grads])
    norm_rows = []
    for item in layer_grads:
        norm_rows.append(item[4])
        norm_rows.append(item[5])
    norm_rows.append(g_final)
    g_norm = jnp.stack(norm_rows)
    s_tok, s_pos, s_in, s_out, s_up, s_down, s_head, s_norm = lax.psum(
        (g_tok, g_pos, g_in, g_out, g_up, g_down, g_head, g_norm), "img"
    )
    shares = (
        lax.psum_scatter(s_tok, "seq", scatter_dimension=1, tiled=True),
        lax.psum_scatter(s_pos, "seq", scatter_dimension=1, tiled=True),
        lax.psum_scatter(s_in, "seq", scatter_dimension=1, tiled=True),
        lax.psum_scatter(s_out, "seq", scatter_dimension=1, tiled=True),
        lax.psum_scatter(s_up, "seq", scatter_dimension=1, tiled=True),
        lax.psum_scatter(s_down, "seq", scatter_dimension=2, tiled=True),
        lax.psum_scatter(s_head, "seq", scatter_dimension=0, tiled=True),
        lax.psum_scatter(s_norm, "seq", scatter_dimension=2, tiled=True),
    )
    squares = sum((jnp.sum(item * item) for item in shares))
    norm_total = jnp.sqrt(lax.psum(squares, "seq"))
    factor = jnp.minimum(1.0, CLIP_NORM / norm_total)
    masters = (tok_table, pos_table, attn_in, attn_out, ffn_in, ffn_out, head_table, norms)
    firsts = (
        tok_first,
        pos_first,
        in_first,
        out_first,
        up_first,
        down_first,
        head_first,
        norm_first,
    )
    seconds = (
        tok_second,
        pos_second,
        in_second,
        out_second,
        up_second,
        down_second,
        head_second,
        norm_second,
    )
    updated = [
        adam_step(masters[index], shares[index], firsts[index], seconds[index], factor)
        for index in range(8)
    ]
    return (
        loss_sum,
        loss_count,
        norm_total,
        updated[0][0],
        updated[1][0],
        updated[2][0],
        updated[3][0],
        updated[4][0],
        updated[5][0],
        updated[6][0],
        updated[7][0],
        updated[0][1],
        updated[1][1],
        updated[2][1],
        updated[3][1],
        updated[4][1],
        updated[5][1],
        updated[6][1],
        updated[7][1],
        updated[0][2],
        updated[1][2],
        updated[2][2],
        updated[3][2],
        updated[4][2],
        updated[5][2],
        updated[6][2],
        updated[7][2],
    )


def solution(mesh):
    placed = (
        P("img", None, "seq"),
        P("img", None, "seq"),
        P(None, "seq"),
        P(None, "seq"),
        P(None, "seq", None),
        P(None, "seq", None),
        P(None, "seq", None),
        P(None, None, "seq"),
        P("seq", None),
        P(None, None, "seq"),
        P(None, "seq"),
        P(None, "seq"),
        P(None, "seq", None),
        P(None, "seq", None),
        P(None, "seq", None),
        P(None, None, "seq"),
        P("seq", None),
        P(None, None, "seq"),
        P(None, "seq"),
        P(None, "seq"),
        P(None, "seq", None),
        P(None, "seq", None),
        P(None, "seq", None),
        P(None, None, "seq"),
        P("seq", None),
        P(None, None, "seq"),
    )
    return jax.shard_map(
        on_device,
        mesh=mesh,
        in_specs=placed,
        out_specs=(
            P(),
            P(),
            P(),
            P(None, "seq"),
            P(None, "seq"),
            P(None, "seq", None),
            P(None, "seq", None),
            P(None, "seq", None),
            P(None, None, "seq"),
            P("seq", None),
            P(None, None, "seq"),
            P(None, "seq"),
            P(None, "seq"),
            P(None, "seq", None),
            P(None, "seq", None),
            P(None, "seq", None),
            P(None, None, "seq"),
            P("seq", None),
            P(None, None, "seq"),
            P(None, "seq"),
            P(None, "seq"),
            P(None, "seq", None),
            P(None, "seq", None),
            P(None, "seq", None),
            P(None, None, "seq"),
            P("seq", None),
            P(None, None, "seq"),
        ),
        check_vma=False,
    )
```

profile of v0, /device:TPU:0, one launch (start us, length us, event | category | flops | bytes accessed | tf_op | source)
XLA Modules:
  0.0 1627.0 jit_solution(1218189318970780900)
XLA Ops:
  12.9 23.1 %all_gather.26 = bf16[7,2,256]{0,1,2:T(2,128)(2,1)S(1)} all-gather(bf16[7,2,16]{0,1,2:T(2,128)(2,1)S(1)} %copy.393), channel_id=1, replica_groups=mesh['seq'=16,'img'=2] {'seq'}, dimensions={2}, use_global_device_ids=true | all-gather | bytes 7616 | tf_op jit(solution)/shard_map/all_gather | solution.py:252
  99.8 36.8 %all_gather.28 = bf16[3,256,256]{2,1,0:T(8,128)(2,1)S(1)} all-gather(bf16[3,16,256]{2,1,0:T(8,128)(2,1)S(1)} %convert_element_type.305), channel_id=1, replica_groups=mesh['seq'=16,'img'=2] {'seq'}, dimensions={1}, use_global_device_ids=true | all-gather | bytes 417792 | tf_op jit(solution)/shard_map/all_gather | solution.py:248
  138.0 25.7 %all_gather.30 = bf16[3,512,256]{1,2,0:T(8,128)(2,1)} all-gather(bf16[3,512,16]{1,2,0:T(8,128)(2,1)S(1)} %convert_element_type.309), channel_id=1, replica_groups=mesh['seq'=16,'img'=2] {'seq'}, dimensions={2}, use_global_device_ids=true | all-gather | bytes 835584 | tf_op jit(solution)/shard_map/all_gather | solution.py:250
  163.6 21.0 %all_gather.29 = bf16[3,256,512]{2,1,0:T(8,128)(2,1)} all-gather(bf16[3,16,512]{2,1,0:T(8,128)(2,1)S(1)} %convert_element_type.307), channel_id=1, replica_groups=mesh['seq'=16,'img'=2] {'seq'}, dimensions={1}, use_global_device_ids=true | all-gather | bytes 835584 | tf_op jit(solution)/shard_map/all_gather | solution.py:249
  233.3 33.4 %all_to_all.180 = bf16[192,8,384]{2,1,0:T(8,128)(2,1)S(1)} all-to-all(bf16[192,8,384]{2,1,0:T(8,128)(2,1)S(1)} %bitcast.375), channel_id=1, replica_groups=mesh['seq'=16,'img'=2] {'seq'}, dimensions={0} | all-to-all | bytes 2359296 | tf_op jit(solution)/shard_map/all_to_all | solution.py:109
  314.1 33.4 %all_to_all.181 = bf16[192,8,384]{2,1,0:T(8,128)(2,1)S(1)} all-to-all(bf16[192,8,384]{2,1,0:T(8,128)(2,1)S(1)} %bitcast.376), channel_id=1, replica_groups=mesh['seq'=16,'img'=2] {'seq'}, dimensions={0} | all-to-all | bytes 2359296 | tf_op jit(solution)/shard_map/all_to_all | solution.py:109
  358.1 20.8 %all_gather.31 = bf16[256,256]{1,0:T(8,128)(2,1)} all-gather(bf16[16,256]{1,0:T(8,128)(2,1)} %convert_element_type.331), channel_id=1, replica_groups=mesh['seq'=16,'img'=2] {'seq'}, dimensions={0}, use_global_device_ids=true | all-gather | bytes 139264 | tf_op jit(solution)/shard_map/all_gather | solution.py:251
  429.1 40.0 %all-reduce.16 = (f32[]{:T(128)}, f32[]{:T(128)}) all-reduce(f32[]{:T(128)} %get-tuple-element.173, f32[]{:T(128)} %get-tuple-element.172), channel_id=1, replica_groups=mesh['seq'=16,'img'=2] {'seq','img'}, use_global_device_ids=true, to_apply=%region_31.32 | all-reduce | flops 2 | bytes 16 | tf_op jit(solution)/shard_map/psum | solution.py:304
  490.2 41.0 %all_to_all.182 = bf16[192,8,512]{2,1,0:T(8,128)(2,1)S(1)} all-to-all(bf16[192,8,512]{2,1,0:T(8,128)(2,1)S(1)} %bitcast.364), channel_id=1, replica_groups=mesh['seq'=16,'img'=2] {'seq'}, dimensions={0} | all-to-all | bytes 3145728 | tf_op jit(solution)/shard_map/all_to_all | solution.py:158
  589.6 29.6 %all-to-all-done.7 = bf16[12,128,384]{2,0,1:T(8,128)(2,1)} async-done(((bf16[12,128,384]{2,0,1:T(8,128)(2,1)}), bf16[12,128,384]{2,0,1:T(8,128)(2,1)}, u32[]{:S(2)}, u32[]{:S(2)}) %all-to-all-start.7) | async-done | bytes 1179680 | tf_op jit(solution)/shard_map/all_to_all | solution.py:173
  661.6 45.0 %all_to_all.183 = bf16[192,8,512]{2,1,0:T(8,128)(2,1)S(1)} all-to-all(bf16[192,8,512]{2,1,0:T(8,128)(2,1)S(1)} %bitcast.365), channel_id=1, replica_groups=mesh['seq'=16,'img'=2] {'seq'}, dimensions={0} | all-to-all | bytes 3145728 | tf_op jit(solution)/shard_map/all_to_all | solution.py:158
  763.7 29.7 %all-to-all-done.9 = bf16[12,128,384]{2,0,1:T(8,128)(2,1)} async-done(((bf16[12,128,384]{2,0,1:T(8,128)(2,1)}), bf16[12,128,384]{2,0,1:T(8,128)(2,1)}, u32[]{:S(2)}, u32[]{:S(2)}) %all-to-all-start.9) | async-done | bytes 1179680 | tf_op jit(solution)/shard_map/all_to_all | solution.py:173
  834.5 45.0 %all_to_all.184 = bf16[192,8,512]{2,1,0:T(8,128)(2,1)S(1)} all-to-all(bf16[192,8,512]{2,1,0:T(8,128)(2,1)S(1)} %bitcast.366), channel_id=1, replica_groups=mesh['seq'=16,'img'=2] {'seq'}, dimensions={0} | all-to-all | bytes 3145728 | tf_op jit(solution)/shard_map/all_to_all | solution.py:158
  1029.4 21.9 %reduce-scatter.22.cloned.1.call-done = f32[16,14]{1,0:T(8,128)} async-done(((f32[256,14]{1,0:T(8,128)}), f32[16,14]{1,0:T(8,128)}) %reduce-scatter.22.cloned.1.call-update) | async-done | bytes 912
  1052.8 56.4 %reduce-scatter.20.cloned.1.call-done = f32[16,256]{1,0:T(8,128)} async-done(((f32[256,256]{1,0:T(8,128)}), f32[16,256]{1,0:T(8,128)}) %reduce-scatter.20.cloned.1.call-update) | async-done | bytes 16400 | tf_op jit(solution)/shard_map/reduce_scatter | solution.py:351
  1109.2 58.9 %reduce-scatter.16.cloned.1.call-done = f32[3,16,256]{2,1,0:T(8,128)} async-done(((f32[3,256,256]{2,1,0:T(8,128)}), f32[3,16,256]{2,1,0:T(8,128)}) %reduce-scatter.16.cloned.1.call-update) | async-done | bytes 49168 | tf_op jit(solution)/shard_map/reduce_scatter | solution.py:348
  1168.1 58.4 %reduce-scatter.12.cloned.1.call-done = f32[67,16]{0,1:T(8,128)} async-done(((f32[67,256]{0,1:T(8,128)}), f32[67,16]{0,1:T(8,128)}) %reduce-scatter.12.cloned.1.call-update) | async-done | bytes 4304 | tf_op jit(solution)/shard_map/reduce_scatter | solution.py:346
  1226.5 58.2 %reduce-scatter.10.cloned.1.call-done = f32[256,16]{0,1:T(8,128)} async-done(((f32[256,256]{0,1:T(8,128)}), f32[256,16]{0,1:T(8,128)}) %reduce-scatter.10.cloned.1.call-update) | async-done | bytes 16400 | tf_op jit(solution)/shard_map/reduce_scatter | solution.py:345
  1299.4 86.1 %all-reduce.23.cloned.1.call-done = f32[3,512,256]{1,0,2:T(4,128)} async-done(((f32[3,512,256]{1,0,2:T(4,128)}), f32[3,512,256]{1,0,2:T(4,128)}) %all-reduce.23.cloned.1.call-update) | async-done | bytes 1572880
  1387.1 22.4 %all-reduce.25.cloned.1.call-done = (f32[256,16]{0,1:T(8,128)}, f32[67,16]{0,1:T(8,128)}, f32[3,16,256]{2,1,0:T(8,128)}, f32[16,256]{1,0:T(8,128)}, f32[7,2,16]{2,1,0:T(2,128)}) async-done(((f32[256,16]{0,1:T(8,128)}, f32[67,16]{0,1:T(8,128)}, f32[3,16,256]{2,1,0:T(8,128)}, f32[16,256]{1,0:T(8,128)}, f32[7,2,16]{2,1,0:T(2,128)}), (f32[256,16]{0,1:T(8,128)}, f32[67,16]{0,1:T(8,128)}, ...) | async-done | bytes 87120 | tf_op jit(solution)/shard_map/psum | solution.py:341
  1410.9 61.9 %reduce-scatter.18.cloned.1.call-done = f32[3,16,512]{2,1,0:T(8,128)} async-done(((f32[3,256,512]{2,1,0:T(8,128)}), f32[3,16,512]{2,1,0:T(8,128)}) %reduce-scatter.18.cloned.1.call-update) | async-done | bytes 98320 | tf_op jit(solution)/shard_map/reduce_scatter | solution.py:349
  1472.7 66.1 %reduce-scatter.14.cloned.1.call-done = f32[3,16,768]{2,1,0:T(8,128)} async-done(((f32[3,256,768]{2,1,0:T(8,128)}), f32[3,16,768]{2,1,0:T(8,128)}) %reduce-scatter.14.cloned.1.call-update) | async-done | bytes 147472 | tf_op jit(solution)/shard_map/reduce_scatter | solution.py:347
  1545.5 20.4 %all-reduce.27.cloned.1.call-done = (f32[3,16,768]{2,1,0:T(8,128)}, f32[3,16,512]{2,1,0:T(8,128)}, f32[3,512,16]{1,2,0:T(8,128)}) async-done(((f32[3,16,768]{2,1,0:T(8,128)}, f32[3,16,512]{2,1,0:T(8,128)}, f32[3,512,16]{1,2,0:T(8,128)}), (f32[3,16,768]{2,1,0:T(8,128)}, f32[3,16,512]{2,1,0:T(8,128)}, f32[3,512,16]{1,2,0:T(8,128)})) %all-reduce.27.cloned.1.call-update) | async-done | bytes 344080 | tf_op jit(solution)/shard_map/psum | solution.py:341
  1574.5 33.8 %psum.87 = f32[]{:T(128)} all-reduce(f32[]{:T(128)S(6)} %add.758), channel_id=1, replica_groups=mesh['seq'=16,'img'=2] {'seq'}, use_global_device_ids=true, to_apply=%region_99.100 | all-reduce | flops 1 | bytes 8 | tf_op jit(solution)/shard_map/psum | solution.py:355
  (908 shorter events, 632.8 us)
Async XLA Ops:
  7.2 83.2 %all-gather.2.cloned.1.call-start = ((), (), s32[]{:S(2)}) async-start(), calls=%async_computation.19 | async-start | bytes 1253376 | tf_op jit(solution)/shard_map/all_gather | solution.py:247
  8.0 79.2 %collective-permute-start = (s32[8,24]{1,0:T(8,128)S(1)}, s32[8,24]{1,0:T(8,128)S(1)}, u32[]{:S(2)}, u32[]{:S(2)}) collective-permute-start(s32[8,24]{1,0:T(8,128)S(1)} %bitcast.420), channel_id=1, source_target_pairs={{0,2},{2,4},{4,6},{6,8},{8,10},{10,12},{12,14},{14,16},{16,18},{18... | collective-permute-start | bytes 2312 | tf_op jit(solution)/shard_map/ppermute | solution.py:37
  95.8 88.8 %all-to-all-start = ((bf16[192,8,384]{2,1,0:T(8,128)(2,1)}), bf16[192,8,384]{2,1,0:T(8,128)(2,1)S(1)}, u32[]{:S(2)}, u32[]{:S(2)}) async-start(bf16[192,8,384]{2,1,0:T(8,128)(2,1)} %bitcast.372), calls=%async_computation | async-start | bytes 2359296 | tf_op jit(solution)/shard_map/all_to_all | solution.py:109
  202.9 20.1 %all-to-all-start.1 = ((bf16[12,128,128]{2,0,1:T(8,128)(2,1)}), bf16[12,128,128]{2,0,1:T(8,128)(2,1)S(1)}, u32[]{:S(2)}, u32[]{:S(2)}) async-start(bf16[12,128,128]{2,0,1:T(8,128)(2,1)} %copy.395), calls=%async_computation.1 | async-start | bytes 1048576 | tf_op jit(solution)/shard_map/all_to_all | solution.py:114
  282.6 20.7 %all-to-all-start.3 = ((bf16[12,128,128]{2,0,1:T(8,128)(2,1)}), bf16[12,128,128]{2,0,1:T(8,128)(2,1)S(1)}, u32[]{:S(2)}, u32[]{:S(2)}) async-start(bf16[12,128,128]{2,0,1:T(8,128)(2,1)} %copy.404), calls=%async_computation.3 | async-start | bytes 1048576 | tf_op jit(solution)/shard_map/all_to_all | solution.py:114
  349.4 30.7 %collective-permute-start.3 = (bf16[1,128,256]{2,1,0:T(8,128)(2,1)}, bf16[1,128,256]{2,1,0:T(8,128)(2,1)}, u32[]{:S(2)}, u32[]{:S(2)}) collective-permute-start(bf16[1,128,256]{2,1,0:T(8,128)(2,1)} %slice.502), channel_id=1, source_target_pairs={{0,2},{2,4},{4,6},{6,8},{8,10},{10,12},{12,14},{14,16},{16,18},{18... | collective-permute-start | bytes 196616 | tf_op jit(solution)/shard_map/ppermute | solution.py:32
  395.6 18.7 %all-to-all-start.5 = ((bf16[12,128,128]{2,0,1:T(8,128)(2,1)}), bf16[12,128,128]{2,0,1:T(8,128)(2,1)}, u32[]{:S(2)}, u32[]{:S(2)}) async-start(bf16[12,128,128]{2,0,1:T(8,128)(2,1)} %copy.413), calls=%async_computation.5 | async-start | bytes 1048576 | tf_op jit(solution)/shard_map/all_to_all | solution.py:114
  569.4 3.8 collective-permute-start.5
  577.5 41.7 %all-to-all-start.7 = ((bf16[12,128,384]{2,0,1:T(8,128)(2,1)}), bf16[12,128,384]{2,0,1:T(8,128)(2,1)}, u32[]{:S(2)}, u32[]{:S(2)}) async-start(bf16[12,128,384]{2,0,1:T(8,128)(2,1)} %copy.425), calls=%async_computation.7 | async-start | bytes 3145728 | tf_op jit(solution)/shard_map/all_to_all | solution.py:173
  743.7 3.8 collective-permute-start.7
  751.7 41.7 %all-to-all-start.9 = ((bf16[12,128,384]{2,0,1:T(8,128)(2,1)}), bf16[12,128,384]{2,0,1:T(8,128)(2,1)}, u32[]{:S(2)}, u32[]{:S(2)}) async-start(bf16[12,128,384]{2,0,1:T(8,128)(2,1)} %copy.443), calls=%async_computation.9 | async-start | bytes 3145728 | tf_op jit(solution)/shard_map/all_to_all | solution.py:173
  879.6 3.6 collective-permute-start.8
  918.0 3.8 collective-permute-start.9
  924.2 41.5 %all-to-all-start.11 = ((bf16[12,128,384]{2,0,1:T(8,128)(2,1)}), bf16[12,128,384]{2,0,1:T(8,128)(2,1)S(1)}, u32[]{:S(2)}, u32[]{:S(2)}) async-start(bf16[12,128,384]{2,0,1:T(8,128)(2,1)} %copy.461), calls=%async_computation.11 | async-start | bytes 3145728 | tf_op jit(solution)/shard_map/all_to_all | solution.py:173
  933.7 117.6 %reduce-scatter.22.cloned.1.call-start = ((), (), s32[]{:S(2)}) async-start(), calls=%async_computation.26 | async-start | bytes 139264
  991.6 117.6 %reduce-scatter.20.cloned.1.call-start = ((), (), s32[]{:S(2)}) async-start(), calls=%async_computation.25 | async-start | bytes 278528 | tf_op jit(solution)/shard_map/reduce_scatter | solution.py:351
  993.7 174.4 %reduce-scatter.16.cloned.1.call-start = ((), (), s32[]{:S(2)}) async-start(), calls=%async_computation.23 | async-start | bytes 835584 | tf_op jit(solution)/shard_map/reduce_scatter | solution.py:348
  1001.3 225.2 %reduce-scatter.12.cloned.1.call-start = ((), (), s32[]{:S(2)}) async-start(), calls=%async_computation.21 | async-start | bytes 139264 | tf_op jit(solution)/shard_map/reduce_scatter | solution.py:346
  1008.2 276.5 %reduce-scatter.10.cloned.1.call-start = ((), (), s32[]{:S(2)}) async-start(), calls=%async_computation.20 | async-start | bytes 278528 | tf_op jit(solution)/shard_map/reduce_scatter | solution.py:345
  1012.2 373.3 %all-reduce.23.cloned.1.call-start = ((), (), s32[]{:S(2)}) async-start(), calls=%async_computation.27 | async-start | bytes 4194304
  1020.2 389.3 %all-reduce.25.cloned.1.call-start = ((), (), s32[]{:S(2)}) async-start(), calls=%async_computation.28 | async-start | bytes 194560 | tf_op jit(solution)/shard_map/psum | solution.py:341
  1284.7 188.1 %reduce-scatter.18.cloned.1.call-start = ((), (), s32[]{:S(2)}) async-start(), calls=%async_computation.24 | async-start | bytes 1671168 | tf_op jit(solution)/shard_map/reduce_scatter | solution.py:349
  1287.4 251.5 %reduce-scatter.14.cloned.1.call-start = ((), (), s32[]{:S(2)}) async-start(), calls=%async_computation.22 | async-start | bytes 2506752 | tf_op jit(solution)/shard_map/reduce_scatter | solution.py:347
  1297.7 268.2 %all-reduce.27.cloned.1.call-start = ((), (), s32[]{:S(2)}) async-start(), calls=%async_computation.29 | async-start | bytes 688128 | tf_op jit(solution)/shard_map/psum | solution.py:341
  (261 other events, 10311.5 us)
Sparse Core Ops, SparseCore 0:
  10.9 41.2 all-gather.1
  991.7 59.5 reduce-scatter.21
  1054.8 54.2 reduce-scatter.19
  1112.6 55.4 reduce-scatter.15
  1172.3 54.0 reduce-scatter.11
  1230.3 54.3 reduce-scatter.9
  1288.6 96.8 all-reduce.22
  1388.6 20.8 all-reduce.24
  1413.2 59.4 reduce-scatter.17
  1476.8 61.9 reduce-scatter.13
  1541.8 24.0 all-reduce.26
where the time goes:
time: 1640 us; the launch traced here: 1630 us
  waiting for transfers between devices  621 us (38%)
  blocking collectives  436 us (27%)
  matrix products  272 us (17%)
  local copies, waits for them, and re-layouts  112 us (7%)
  other arithmetic  90.7 us (6%)
  starting transfers between devices  70.9 us (4%)
  between operations  25.4 us (2%)
    dot_general x62, matrix products, product(): return jnp.einsum(form, left, right, preferred_element_type=jnp.float32)  226 us
    all_to_all x3, blocking collectives, layer_backward(): lax.all_to_all(packed, 'seq', split_axis=0, concat_axis=1, tiled=True)  131 us
    unnamed x13, waiting for transfers between devices  108 us
    all_to_all x3, waiting for transfers between devices, layer_backward(): lax.all_to_all(reply, 'seq', split_axis=1, concat_axis=0, tiled=True)  78.1 us
    all_to_all x2, blocking collectives, layer_forward(): lax.all_to_all(packed, 'seq', split_axis=0, concat_axis=1, tiled=True)  66.8 us
    reduce_scatter x1, waiting for transfers between devices, on_device(): lax.psum_scatter(s_in, 'seq', scatter_dimension=1, tiled=True)  66.1 us
    reduce_scatter x1, waiting for transfers between devices, on_device(): lax.psum_scatter(s_up, 'seq', scatter_dimension=1, tiled=True)  61.9 us
    reduce_scatter x1, waiting for transfers between devices, on_device(): lax.psum_scatter(s_out, 'seq', scatter_dimension=1, tiled=True)  58.9 us
  transfers between devices with their start and end apart: 28, of which 23 were waited for; matrix products, arithmetic and copies ran while one was open for 8% of the time, Pallas kernels for 0%

commit v1 on v0

v1 whole, which is shorter than its diff:
```python
import functools
import math

import jax
import jax.numpy as jnp
from jax import lax
from jax.experimental import pallas as pl
from jax.experimental.pallas import tpu as pltpu
from jax.sharding import PartitionSpec as P

D = 256
HEAD = 128
FF = 512
V = 256
STRIDE = 128
LAYERS = 3
NORMS = 2 * LAYERS + 1
STEP = 10
SIDE = 32
POS = 2 * SIDE + 3
CLIP_NORM = 0.05
BETA_ONE = 0.9
BETA_TWO = 0.95
LEARN_RATE = 0.1
WEIGHT_DECAY = 0.1
ADAM_EPS = 1e-08
SMOOTHING = 0.1
NORM_EPS = 1e-05
SCALE = HEAD ** (-0.5)

C_IN, C_OUT, C_UP, C_DOWN = (0, 768), (768, 1024), (1024, 1536), (1536, 2048)
C_LAYER = 2048
C_TOK, C_POS, C_HEAD, C_NORM = (0, 256), (256, 384), (384, 640), (640, 768)
C_REST = 768

BF = jnp.bfloat16
F32 = jnp.float32
VMEM_LIMIT = 64 * 1024 * 1024


def dot(a, b):
    return lax.dot_general(a, b, (((1,), (0,)), ((), ())), preferred_element_type=F32)


def dot_nt(a, b):
    return lax.dot_general(a, b, (((1,), (1,)), ((), ())), preferred_element_type=F32)


def dot_tn(a, b):
    return lax.dot_general(a, b, (((0,), (0,)), ((), ())), preferred_element_type=F32)


class Geometry:
    def __init__(self, n, m, images, blocks):
        self.n, self.m, self.images, self.blocks = n, m, images, blocks
        self.depth = n // 4
        self.rows = D // n
        self.group = n // images
        self.res = STRIDE // self.group
        self.own = STRIDE // n

    def place(self):
        me = lax.axis_index("seq")
        return me // 4, me // 2 % 2, me % 2


def seq_id(z, y, core):
    return {"seq": z * 4 + y * 2 + core}


def greet(devices):
    barrier = pltpu.get_barrier_semaphore()
    for device in devices:
        pl.semaphore_signal(barrier, inc=1, device_id=device, device_id_type=pl.DeviceIdType.MESH)
    pl.semaphore_wait(barrier, len(devices))


def push(src, dst, send_sem, recv_sem, device):
    return pltpu.make_async_remote_copy(
        src_ref=src,
        dst_ref=dst,
        send_sem=send_sem,
        recv_sem=recv_sem,
        device_id=device,
        device_id_type=pl.DeviceIdType.MESH,
    )


def gather_kernel(
    geo, pixels, mask, tok, pos, w_in, w_out, w_up, w_down, head, norms, px, rest, layers, send, recv
):
    z, y, core = geo.place()
    depth = geo.depth
    px[z, y, core, : geo.images] = pixels[...]
    px[z, y, core, geo.images :] = mask[...]
    rest[z, y, core, :, C_TOK[0] : C_TOK[1]] = tok[...].astype(BF)
    rest[z, y, core, :, C_POS[0] : C_POS[1]] = pos[...].astype(BF)
    rest[z, y, core, :, C_HEAD[0] : C_HEAD[1]] = head[...].astype(BF)
    rest[z, y, core, :, C_NORM[0] : C_NORM[1]] = norms[...].astype(BF)
    for l in range(LAYERS):
        layers[l, z, y, core, :, C_IN[0] : C_IN[1]] = w_in[l].astype(BF)
        layers[l, z, y, core, :, C_OUT[0] : C_OUT[1]] = w_out[l].astype(BF)
        layers[l, z, y, core, :, C_UP[0] : C_UP[1]] = w_up[l].astype(BF)
        layers[l, z, y, core, :, C_DOWN[0] : C_DOWN[1]] = w_down[l].astype(BF)
    peers = [seq_id(lax.rem(z + k, depth), y, core) for k in range(1, depth)]
    beside, sibling = seq_id(z, 1 - y, core), seq_id(z, y, 1 - core)
    greet(peers + [beside, sibling])
    arrays = [px, rest] + [layers.at[l] for l in range(LAYERS)]
    first, second, third = [], [], []
    for a, array in enumerate(arrays):
        mine = array.at[z, y, core]
        copies = [push(mine, mine, send.at[a, k], recv.at[a, k], peers[k]) for k in range(depth - 1)]
        for copy in copies:
            copy.start()
        first.append(copies)
    for a, array in enumerate(arrays):
        for copy in first[a]:
            copy.wait_recv()
        column = array.at[pl.ds(0, depth), y, core]
        copy = push(column, column, send.at[a, depth - 1], recv.at[a, depth - 1], beside)
        copy.start()
        second.append(copy)
    for a, array in enumerate(arrays):
        second[a].wait_recv()
        half = array.at[pl.ds(0, depth), pl.ds(0, 2), core]
        copy = push(half, half, send.at[a, depth], recv.at[a, depth], sibling)
        copy.start()
        third.append(copy)
    for a in range(len(arrays)):
        third[a].wait()
        second[a].wait_send()
        for copy in first[a]:
            copy.wait_send()


def normalise(x):
    centre = x - jnp.mean(x, -1, keepdims=True)
    spread = jnp.mean(centre * centre, -1, keepdims=True)
    rstd = lax.rsqrt(spread + NORM_EPS)
    return centre * rstd, rstd


def fold(x):
    return jnp.sum(x.reshape(x.shape[0] // 8, 8, x.shape[1]), 0)


def normalise_back(dy, unit, rstd, gain):
    dxh = dy * (1.0 + gain)
    mean_one = jnp.mean(dxh, -1, keepdims=True)
    mean_two = jnp.mean(dxh * unit, -1, keepdims=True)
    return rstd * (dxh - mean_one - unit * mean_two), fold(dy * unit), fold(dy)


def gelu_both(u):
    c = math.sqrt(2.0 / math.pi)
    square = u * u
    t = jnp.tanh(c * u * (1.0 + 0.044715 * square))
    half = 0.5 * (1.0 + t)
    slope = half + 0.5 * u * (1.0 - t * t) * (c * (1.0 + 3.0 * 0.044715 * square))
    return u * half, slope


def softmax(scores):
    e = jnp.exp(scores - jnp.max(scores, -1, keepdims=True))
    return e * (1.0 / jnp.sum(e, -1, keepdims=True))


def step_kernel(
    geo, chunk, px, rest, layers, g_rest, g_layers, stats,
    x_s, x1_s, q0_s, kv_s, qkv1_s, p0_s, p1_s, o_s, a_s, slope_s, stage, o1_s, do0_s, dq0_s, acc, back,
    dx_s, ids_s, tgt_s, msk_s, prev_s, bias0, bias1, norm_s, gnorm, wide, send, recv,
):
    z, y, core = geo.place()
    me = lax.axis_index("seq")
    depth, group, res, blocks, own = geo.depth, geo.group, geo.res, geo.blocks, geo.own
    image, part = me // group, me % group
    siblings = [{"seq": image * group + lax.rem(part + k, group)} for k in range(1, group)]
    greet(siblings)
    rows = chunk * res
    chunks = blocks // chunk
    n_groups = res // 8

    def table(ref, cols):
        piece = ref[..., cols[0] : cols[1]]
        width = cols[1] - cols[0]
        if geo.rows % 16:
            return piece.astype(F32).reshape(D, width).astype(BF)
        return piece.reshape(D, width)

    def layer_table(l, cols):
        return table(layers.at[l], cols)

    def add_to(ref, cols, value):
        shape = (depth, 2, 2, geo.rows, cols[1] - cols[0])
        ref[..., cols[0] : cols[1]] += value.reshape(shape)

    for ref in (ids_s, tgt_s, msk_s, prev_s, wide):
        ref[...] = jnp.zeros_like(ref)
    span = depth // group
    for j in range(geo.images):
        slot = (part * span + j // 4, j // 2 % 2, j % 2)
        tgt_s[j * own : (j + 1) * own, :blocks] = px[(*slot, image)].astype(F32)
        msk_s[j * own : (j + 1) * own, :blocks] = px[(*slot, geo.images + image)].astype(F32)
    before = px[lax.rem(part * span + depth - 1, depth), 1, 1, image].astype(F32)
    prev_s[:own, :blocks] = before
    prev = prev_s[...]
    lane = lax.broadcasted_iota(jnp.int32, prev.shape, 1)
    moved = jnp.where(lane == 0, -1.0, pltpu.roll(prev, 1, 1))
    prev = jnp.where(part == 0, moved, prev)
    ids_s[0:1, :] = prev[own - 1 : own, :]
    ids_s[1:res, :] = tgt_s[0 : res - 1, :]

    norm_s[...] = jnp.transpose(table(rest, C_NORM).astype(F32))[:16].reshape(16, 1, D)

    qi = part * res + lax.broadcasted_iota(jnp.int32, (res, 2 * STRIDE), 0)
    kj = lax.broadcasted_iota(jnp.int32, (res, 2 * STRIDE), 1)
    seen = (kj > qi) & (kj <= qi + STRIDE)
    bias0[0] = jnp.where(seen & (kj >= STRIDE), 0.0, -1e30)
    bias0[1] = jnp.where(seen, 0.0, -1e30)
    side = 8 * blocks
    ri = lax.broadcasted_iota(jnp.int32, (side, side), 0)
    ci = lax.broadcasted_iota(jnp.int32, (side, side), 1)
    bias1[...] = jnp.where(((ri & 7) == (ci & 7)) & (ri >= ci), 0.0, -1e30)

    g_rest[...] = jnp.zeros_like(g_rest)
    g_layers[...] = jnp.zeros_like(g_layers)
    gnorm[...] = jnp.zeros_like(gnorm)

    def spread(ref, b0):
        values = ref[...].astype(BF)
        at = lax.broadcasted_iota(jnp.int32, (128, 128), 0)
        return jnp.concatenate(
            [dot(values, (at == b0 + j).astype(F32).astype(BF)) for j in range(chunk)], 0
        )

    def one_hot(ref, b0):
        value = spread(ref, b0)
        lane = lax.broadcasted_iota(jnp.int32, (rows, 128), 1).astype(F32)
        return jnp.concatenate([(value == lane).astype(F32), (value == lane + 128.0).astype(F32)], 1)

    def place_hot(b0):
        r = lax.broadcasted_iota(jnp.int32, (rows, 128), 0)
        lane = lax.broadcasted_iota(jnp.int32, (rows, 128), 1).astype(F32)
        p = ((b0 + r // res) * STRIDE + part * res + r % res).astype(F32)
        third = jnp.floor((p + 0.5) * (1.0 / 3.0))
        line = jnp.floor((third + 0.5) * (1.0 / SIDE))
        hits = (lane == line) | (lane == SIDE + third - SIDE * line)
        return (hits | (lane == 2 * SIDE + p - 3.0 * third)).astype(F32)

    def loop(count, body):
        lax.fori_loop(0, count, lambda i, carry: (body(i), carry)[1], 0)

    def embed(i):
        b0 = i * chunk
        hot = jnp.concatenate([one_hot(ids_s, b0), place_hot(b0)], 1).astype(BF)
        x = dot_nt(hot, table(rest, (C_TOK[0], C_POS[1])))
        x_s[0, pl.ds(b0, chunk)] = x.reshape(chunk, res, D)

    loop(chunks, embed)

    def exchange(l, k):
        mine = kv_s.at[l, pl.ds(1, blocks), part]
        return push(mine, mine, send.at[k], recv.at[l, k], siblings[k])

    def forward(l):
        def mix(i):
            b0 = i * chunk
            unit, _ = normalise(x_s[l, pl.ds(b0, chunk)].reshape(rows, D))
            h = (unit * (1.0 + norm_s[4 * l]) + norm_s[4 * l + 1]).astype(BF)
            qkv = dot(h, layer_table(l, C_IN)).reshape(chunk, res, 6 * HEAD)
            q0_s[l, pl.ds(b0, chunk)] = qkv[..., :HEAD].astype(BF)
            kv_s[l, pl.ds(b0 + 1, chunk), part, :, :HEAD] = qkv[..., 2 * HEAD : 3 * HEAD].astype(BF)
            kv_s[l, pl.ds(b0 + 1, chunk), part, :, HEAD:] = qkv[..., 4 * HEAD : 5 * HEAD].astype(BF)
            stage[pl.ds(b0, chunk), :, :HEAD] = qkv[..., HEAD : 2 * HEAD]
            stage[pl.ds(b0, chunk), :, HEAD : 2 * HEAD] = qkv[..., 3 * HEAD : 4 * HEAD]
            stage[pl.ds(b0, chunk), :, 2 * HEAD :] = qkv[..., 5 * HEAD :]

        kv_s[l, 0] = jnp.zeros((group, res, 2 * HEAD), BF)
        loop(chunks, mix)
        copies = [exchange(l, k) for k in range(group - 1)]
        for copy in copies:
            copy.start()

        def strided(g):
            at = pl.ds(pl.multiple_of(8 * g, 8), 8)
            qkv = stage[:, at, :].reshape(8 * blocks, 3 * HEAD).astype(BF)
            qkv1_s[l, g] = qkv
            scores = dot_nt(qkv[:, :HEAD], qkv[:, HEAD : 2 * HEAD]) * SCALE + bias1[...]
            probs = softmax(scores).astype(BF)
            p1_s[l, g] = probs
            o1_s[:, at, :] = dot(probs, qkv[:, 2 * HEAD :]).reshape(blocks, 8, HEAD)

        loop(n_groups, strided)
        for copy in copies:
            copy.wait()

        def window(b):
            kv = kv_s[l, pl.ds(b, 2)].reshape(2 * STRIDE, 2 * HEAD)
            scores = dot_nt(q0_s[l, b], kv[:, :HEAD]) * SCALE + bias0[jnp.minimum(b, 1)]
            probs = softmax(scores).astype(BF)
            p0_s[l, b] = probs
            o_s[l, b, :, :HEAD] = dot(probs, kv[:, HEAD:]).astype(BF)

        loop(blocks, window)

        def feed(i):
            b0 = i * chunk
            at = pl.ds(b0, chunk)
            o_s[l, at, :, HEAD:] = o1_s[at].astype(BF)
            x1 = x_s[l, at].reshape(rows, D) + dot(o_s[l, at].reshape(rows, D), layer_table(l, C_OUT))
            x1_s[l, at] = x1.reshape(chunk, res, D)
            unit, _ = normalise(x1)
            h = (unit * (1.0 + norm_s[4 * l + 2]) + norm_s[4 * l + 3]).astype(BF)
            a, slope = gelu_both(dot(h, layer_table(l, C_UP)))
            a = a.astype(BF)
            a_s[l, at] = a.reshape(chunk, res, FF)
            slope_s[l, at] = slope.astype(BF).reshape(chunk, res, FF)
            x2 = x1 + dot_nt(a, layer_table(l, C_DOWN))
            x_s[l + 1, at] = x2.reshape(chunk, res, D)

        loop(chunks, feed)

    loop(LAYERS, forward)

    def finish(i, loss):
        b0 = i * chunk
        at = pl.ds(b0, chunk)
        unit, rstd = normalise(x_s[LAYERS, at].reshape(rows, D))
        gain = norm_s[4 * LAYERS]
        h = (unit * (1.0 + gain) + norm_s[4 * LAYERS + 1]).astype(BF)
        head = table(rest, C_HEAD)
        logits = dot(h, head)
        hot = one_hot(tgt_s, b0)
        shift = logits - jnp.max(logits, -1, keepdims=True)
        e = jnp.exp(shift)
        total = jnp.sum(e, -1, keepdims=True)
        weight = spread(msk_s, b0)
        per = (
            jnp.log(total)
            - (1.0 - SMOOTHING) * jnp.sum(hot * shift, -1, keepdims=True)
            - SMOOTHING * jnp.mean(shift, -1, keepdims=True)
        )
        loss = loss + jnp.sum(weight[:, :1] * per, 0, keepdims=True)
        weight = jnp.concatenate([weight, weight], 1)
        d_logits = weight * (e * (1.0 / total) - (1.0 - SMOOTHING) * hot - SMOOTHING / V)
        d_logits = d_logits.astype(BF)
        add_to(g_rest, C_HEAD, dot_tn(h, d_logits))
        dx, g_gain, g_bias = normalise_back(dot_nt(d_logits, head), unit, rstd, gain)
        gnorm[4 * LAYERS] += g_gain
        gnorm[4 * LAYERS + 1] += g_bias
        dx_s[at] = dx.reshape(chunk, res, D)
        return loss

    loss = lax.fori_loop(0, chunks, finish, jnp.zeros((1, 1), F32))
    count = jnp.sum(jnp.sum(msk_s[...], 0, keepdims=True), 1, keepdims=True)
    line = lax.broadcasted_iota(jnp.int32, (8, 128), 0)
    stats[...] = jnp.where(line == 0, loss, jnp.where(line == 1, count, 0.0))

    def give(l, slot, k):
        other = lax.rem(part + k + 1, group)
        return push(
            acc.at[pl.ds(1, blocks), other], back.at[slot, k], send.at[k], recv.at[LAYERS + l, k], siblings[k]
        )

    def backward(step):
        l = LAYERS - 1 - step
        slot = step % 2

        def feed(i):
            b0 = i * chunk
            at = pl.ds(b0, chunk)
            dx2 = dx_s[at].reshape(rows, D)
            g2 = dx2.astype(BF)
            a = a_s[l, at].reshape(rows, FF)
            add_to(g_layers.at[l], C_DOWN, dot_tn(g2, a))
            du = slope_s[l, at].reshape(rows, FF).astype(F32) * dot(g2, layer_table(l, C_DOWN))
            du = du.astype(BF)
            unit, rstd = normalise(x1_s[l, at].reshape(rows, D))
            gain = norm_s[4 * l + 2]
            h = (unit * (1.0 + gain) + norm_s[4 * l + 3]).astype(BF)
            add_to(g_layers.at[l], C_UP, dot_tn(h, du))
            dh = dot_nt(du, layer_table(l, C_UP))
            dx, g_gain, g_bias = normalise_back(dh, unit, rstd, gain)
            gnorm[4 * l + 2] += g_gain
            gnorm[4 * l + 3] += g_bias
            dx = dx + dx2
            dx_s[at] = dx.reshape(chunk, res, D)
            g1 = dx.astype(BF)
            add_to(g_layers.at[l], C_OUT, dot_tn(o_s[l, at].reshape(rows, D), g1))
            do = dot_nt(g1, layer_table(l, C_OUT)).reshape(chunk, res, D)
            do0_s[at] = do[..., :HEAD].astype(BF)
            o1_s[at] = do[..., HEAD:]

        loop(chunks, feed)
        acc[...] = jnp.zeros_like(acc)

        def window(b):
            kv = kv_s[l, pl.ds(b, 2)].reshape(2 * STRIDE, 2 * HEAD)
            probs = p0_s[l, b]
            do = do0_s[b]
            dp = dot_nt(do, kv[:, HEAD:])
            wide_p = probs.astype(F32)
            ds = (wide_p * (dp - jnp.sum(wide_p * dp, -1, keepdims=True)) * SCALE).astype(BF)
            dq0_s[b] = dot(ds, kv[:, :HEAD]).astype(BF)
            dkv = jnp.concatenate([dot_tn(ds, q0_s[l, b]), dot_tn(probs, do)], 1)
            acc[pl.ds(b, 2)] += dkv.reshape(2, group, res, 2 * HEAD)

        loop(blocks, window)
        copies = [give(l, slot, k) for k in range(group - 1)]
        for copy in copies:
            copy.start()

        def strided(g):
            at = pl.ds(pl.multiple_of(8 * g, 8), 8)
            qkv = qkv1_s[l, g]
            probs = p1_s[l, g]
            do = o1_s[:, at, :].reshape(8 * blocks, HEAD).astype(BF)
            dp = dot_nt(do, qkv[:, 2 * HEAD :])
            wide_p = probs.astype(F32)
            ds = (wide_p * (dp - jnp.sum(wide_p * dp, -1, keepdims=True)) * SCALE).astype(BF)
            dq = dot(ds, qkv[:, HEAD : 2 * HEAD])
            dk = dot_tn(ds, qkv[:, :HEAD])
            dv = dot_tn(probs, do)
            stage[:, at, :] = jnp.concatenate([dq, dk, dv], 1).reshape(blocks, 8, 3 * HEAD)

        loop(n_groups, strided)
        for copy in copies:
            copy.wait()

        def mix(i):
            b0 = i * chunk
            at = pl.ds(b0, chunk)
            dkv = acc[pl.ds(b0 + 1, chunk), part]
            for k in range(group - 1):
                dkv = dkv + back[slot, k, at]
            d1 = stage[at]
            dqkv = jnp.concatenate(
                [
                    dq0_s[at],
                    d1[..., :HEAD].astype(BF),
                    dkv[..., :HEAD].astype(BF),
                    d1[..., HEAD : 2 * HEAD].astype(BF),
                    dkv[..., HEAD:].astype(BF),
                    d1[..., 2 * HEAD :].astype(BF),
                ],
                -1,
            ).reshape(rows, 6 * HEAD)
            unit, rstd = normalise(x_s[l, at].reshape(rows, D))
            gain = norm_s[4 * l]
            h = (unit * (1.0 + gain) + norm_s[4 * l + 1]).astype(BF)
            add_to(g_layers.at[l], C_IN, dot_tn(h, dqkv))
            dh = dot_nt(dqkv, layer_table(l, C_IN))
            dx, g_gain, g_bias = normalise_back(dh, unit, rstd, gain)
            gnorm[4 * l] += g_gain
            gnorm[4 * l + 1] += g_bias
            dx_s[at] += dx.reshape(chunk, res, D)

        loop(chunks, mix)

    loop(LAYERS, backward)

    def embed_back(i):
        b0 = i * chunk
        hot = jnp.concatenate([one_hot(ids_s, b0), place_hot(b0)], 1).astype(BF)
        dx = dx_s[pl.ds(b0, chunk)].reshape(rows, D)
        high = dx.astype(BF)
        low = (dx - high.astype(F32)).astype(BF)
        add_to(g_rest, (C_TOK[0], C_POS[1]), dot_tn(high, hot) + dot_tn(low, hot))

    loop(chunks, embed_back)
    for i in range(2 * NORMS):
        wide[i : i + 1, :] = jnp.sum(gnorm[i], 0, keepdims=True)
    add_to(g_rest, C_NORM, jnp.transpose(wide[...]))


def adam(master, gradient, first, second):
    first = BETA_ONE * first + (1.0 - BETA_ONE) * gradient
    second = BETA_TWO * second + (1.0 - BETA_TWO) * gradient * gradient
    moved = first / (1.0 - BETA_ONE**STEP) / (jnp.sqrt(second / (1.0 - BETA_TWO**STEP)) + ADAM_EPS)
    return master - LEARN_RATE * (moved + WEIGHT_DECAY * master), first, second


def update_kernel(geo, *refs):
    g_rest, g_layers, stats = refs[:3]
    masters, firsts, seconds = refs[3:11], refs[11:19], refs[19:27]
    totals = refs[27]
    outs = (refs[28:36], refs[36:44], refs[44:52])
    (s1_rest, s1_layers, r1_rest, r1_layers, s2_rest, s2_layers, r2_rest, r2_layers,
     s3_rest, s3_layers, r3_rest, r3_layers, r4_rest, r4_layers, sum_rest, sum_layers,
     st_img, st_core, st_y, st_z, st_send, send, recv, st_send_sem, st_recv_sem) = refs[52:]
    z, y, core = geo.place()
    x = lax.axis_index("img")
    depth, m = geo.depth, geo.m
    peers = [seq_id(lax.rem(z + k, depth), y, core) for k in range(1, depth)]
    beside, sibling = seq_id(z, 1 - y, core), seq_id(z, y, 1 - core)
    across = [{"img": lax.rem(x + k, m)} for k in range(1, m)]
    greet(peers + [beside, sibling] + across)

    def sections(a, b):
        return [a] + [b.at[l] for l in range(LAYERS)]

    grads = sections(g_rest, g_layers)
    s1, r1 = sections(s1_rest, s1_layers), sections(r1_rest, r1_layers)
    s2, r2 = sections(s2_rest, s2_layers), sections(r2_rest, r2_layers)
    s3, r3 = sections(s3_rest, s3_layers), sections(r3_rest, r3_layers)
    r4 = sections(r4_rest, r4_layers)
    sums = sections(sum_rest, sum_layers)
    order = list(range(1 + LAYERS))
    every = pl.ds(0, depth)

    st_img[x] = stats[...]
    st_copies = [
        push(st_img.at[x], st_img.at[x], st_send_sem.at[k], st_recv_sem.at[k], across[k]) for k in range(m - 1)
    ]
    for copy in st_copies:
        copy.start()
    one, two, three, four = {}, {}, {}, {}
    for a in order:
        s1[a][...] = grads[a][every, pl.ds(0, 2), 1 - core].astype(BF)
        one[a] = push(s1[a], r1[a], send.at[a, 0], recv.at[a, 0], sibling)
        one[a].start()
    for a in order:
        one[a].wait()
        s2[a][...] = (grads[a][every, 1 - y, core] + r1[a][every, 1 - y].astype(F32)).astype(BF)
        two[a] = push(s2[a], r2[a], send.at[a, 1], recv.at[a, 1], beside)
        two[a].start()
    for a in order:
        two[a].wait()
        total = grads[a][every, y, core] + r1[a][every, y].astype(F32) + r2[a][...].astype(F32)
        s3[a][...] = total.astype(BF)
        three[a] = [
            push(s3[a].at[lax.rem(z + k, depth)], r3[a].at[k - 1], send.at[a, 1 + k], recv.at[a, 1 + k], peers[k - 1])
            for k in range(1, depth)
        ]
        for copy in three[a]:
            copy.start()
    for a in order:
        for copy in three[a]:
            copy.wait()
        total = s3[a][z].astype(F32)
        for k in range(1, depth):
            total = total + r3[a][k - 1].astype(F32)
        r4[a][x] = total.astype(BF)
        four[a] = [
            push(r4[a].at[x], r4[a].at[x], send.at[a, depth + 1 + k], recv.at[a, depth + 1 + k], across[k])
            for k in range(m - 1)
        ]
        for copy in four[a]:
            copy.start()
    squares = jnp.zeros((1, 1), F32)
    for a in order:
        for copy in four[a]:
            copy.wait()
        total = r4[a][0].astype(F32)
        for k in range(1, m):
            total = total + r4[a][k].astype(F32)
        sums[a][...] = total
        squares = squares + jnp.sum(jnp.sum(total * total, 0, keepdims=True), 1, keepdims=True)
    for copy in st_copies:
        copy.wait()
    told = st_img[0]
    for k in range(1, m):
        told = told + st_img[k]
    line = lax.broadcasted_iota(jnp.int32, (8, 128), 0)
    told = jnp.where(line == 2, squares, told)
    base = m - 1

    def swap(told, buffer, index, where, device):
        buffer[where] = told
        copy = push(buffer.at[where], buffer.at[where], st_send_sem.at[base + index], st_recv_sem.at[base + index], device)
        copy.start()
        copy.wait()
        return buffer[0] + buffer[1]

    told = swap(told, st_core, 0, core, sibling)
    told = swap(told, st_y, 1, y, beside)
    st_z[z] = told
    copies = [
        push(st_z.at[z], st_z.at[z], st_send_sem.at[base + 1 + k], st_recv_sem.at[base + 1 + k], peers[k - 1])
        for k in range(1, depth)
    ]
    for copy in copies:
        copy.start()
    for copy in copies:
        copy.wait()
    told = st_z[0]
    for k in range(1, depth):
        told = told + st_z[k]
    count = told[1:2, :1]
    norm = jnp.sqrt(told[2:3, :1]) / count
    totals[...] = jnp.where(line == 2, norm, told)
    factor = jnp.minimum(1.0, CLIP_NORM / norm) / count

    def put(index, at, gradient):
        gradient = gradient * factor
        result = adam(masters[index][at], gradient, firsts[index][at], seconds[index][at])
        for k in range(3):
            outs[k][index][at] = result[k]

    put(0, ..., sum_rest[:, C_TOK[0] : C_TOK[1]])
    put(1, ..., sum_rest[:, C_POS[0] : C_POS[1]])
    put(6, ..., sum_rest[:, C_HEAD[0] : C_HEAD[1]])
    put(7, ..., sum_rest[:, C_NORM[0] : C_NORM[1]])
    for l in range(LAYERS):
        put(2, l, sum_layers[l, :, C_IN[0] : C_IN[1]])
        put(3, l, sum_layers[l, :, C_OUT[0] : C_OUT[1]])
        put(4, l, sum_layers[l, :, C_UP[0] : C_UP[1]])
        put(5, l, sum_layers[l, :, C_DOWN[0] : C_DOWN[1]])


def packed(tok, pos, w_in, w_out, w_up, w_down, head, norms):
    rows = head.shape[0]
    pos = jnp.pad(pos.T, ((0, 0), (0, 128 - POS)))
    norms = jnp.pad(norms.reshape(2 * NORMS, rows).T, ((0, 0), (0, 128 - 2 * NORMS)))
    return (tok.T, pos, w_in, w_out, w_up, jnp.swapaxes(w_down, 1, 2), head, norms)


def unpacked(tok, pos, w_in, w_out, w_up, w_down, head, norms):
    norms = norms[:, : 2 * NORMS].T.reshape(NORMS, 2, head.shape[0])
    return (tok.T, pos[:, :POS].T, w_in, w_out, w_up, jnp.swapaxes(w_down, 1, 2), head, norms)


def on_device(geo, pixels, loss_mask, *weights):
    masters, firsts, seconds = (packed(*weights[k : k + 8]) for k in (0, 8, 16))
    n_rows, depth, blocks, res, group = geo.rows, geo.depth, geo.blocks, geo.res, geo.group
    vmem = pl.BlockSpec(memory_space=pltpu.VMEM)
    px, rest, layers = pl.pallas_call(
        functools.partial(gather_kernel, geo),
        out_shape=(
            jax.ShapeDtypeStruct((depth, 2, 2, 2 * geo.images, geo.own, blocks), jnp.int32),
            jax.ShapeDtypeStruct((depth, 2, 2, n_rows, C_REST), BF),
            jax.ShapeDtypeStruct((LAYERS, depth, 2, 2, n_rows, C_LAYER), BF),
        ),
        in_specs=[vmem] * 10,
        out_specs=(vmem, vmem, vmem),
        scratch_shapes=[
            pltpu.SemaphoreType.DMA((2 + LAYERS, depth + 1)),
            pltpu.SemaphoreType.DMA((2 + LAYERS, depth + 1)),
        ],
        compiler_params=pltpu.CompilerParams(
            collective_id=0, has_side_effects=True, vmem_limit_bytes=VMEM_LIMIT
        ),
        name="gather",
    )(jnp.swapaxes(pixels, 1, 2), jnp.swapaxes(loss_mask, 1, 2), *masters)

    chunk = 4
    n_groups = res // 8
    side = 8 * blocks
    g_rest, g_layers, stats = pl.pallas_call(
        functools.partial(step_kernel, geo, chunk),
        out_shape=(
            jax.ShapeDtypeStruct((depth, 2, 2, n_rows, C_REST), F32),
            jax.ShapeDtypeStruct((LAYERS, depth, 2, 2, n_rows, C_LAYER), F32),
            jax.ShapeDtypeStruct((8, 128), F32),
        ),
        in_specs=[vmem] * 3,
        out_specs=(vmem,) * 3,
        scratch_shapes=[
            pltpu.VMEM((LAYERS + 1, blocks, res, D), F32),
            pltpu.VMEM((LAYERS, blocks, res, D), F32),
            pltpu.VMEM((LAYERS, blocks, res, HEAD), BF),
            pltpu.VMEM((LAYERS, blocks + 1, group, res, 2 * HEAD), BF),
            pltpu.VMEM((LAYERS, n_groups, side, 3 * HEAD), BF),
            pltpu.VMEM((LAYERS, blocks, res, 2 * STRIDE), BF),
            pltpu.VMEM((LAYERS, n_groups, side, side), BF),
            pltpu.VMEM((LAYERS, blocks, res, D), BF),
            pltpu.VMEM((LAYERS, blocks, res, FF), BF),
            pltpu.VMEM((LAYERS, blocks, res, FF), BF),
            pltpu.VMEM((blocks, res, 3 * HEAD), F32),
            pltpu.VMEM((blocks, res, HEAD), F32),
            pltpu.VMEM((blocks, res, HEAD), BF),
            pltpu.VMEM((blocks, res, HEAD), BF),
            pltpu.VMEM((blocks + 1, group, res, 2 * HEAD), F32),
            pltpu.VMEM((2, group - 1, blocks, res, 2 * HEAD), F32),
            pltpu.VMEM((blocks, res, D), F32),
            pltpu.VMEM((res, 128), F32),
            pltpu.VMEM((res, 128), F32),
            pltpu.VMEM((res, 128), F32),
            pltpu.VMEM((8, 128), F32),
            pltpu.VMEM((2, res, 2 * STRIDE), F32),
            pltpu.VMEM((side, side), F32),
            pltpu.VMEM((16, 1, D), F32),
            pltpu.VMEM((2 * NORMS, 8, D), F32),
            pltpu.VMEM((128, D), F32),
            pltpu.SemaphoreType.DMA((group - 1,)),
            pltpu.SemaphoreType.DMA((2 * LAYERS, group - 1)),
        ],
        compiler_params=pltpu.CompilerParams(
            collective_id=1, has_side_effects=True, vmem_limit_bytes=VMEM_LIMIT
        ),
        name="step",
    )(px, rest, layers)

    def both(lead, dtype):
        return [
            pltpu.VMEM((*lead, n_rows, C_REST), dtype),
            pltpu.VMEM((LAYERS, *lead, n_rows, C_LAYER), dtype),
        ]

    stat = jax.ShapeDtypeStruct((8, 128), F32)
    shapes = [jax.ShapeDtypeStruct(item.shape, F32) for item in masters]
    m = geo.m
    outs = pl.pallas_call(
        functools.partial(update_kernel, geo),
        out_shape=[stat] + shapes * 3,
        in_specs=[vmem] * 27,
        out_specs=[vmem] * 25,
        scratch_shapes=[
            *both((depth, 2), BF), *both((depth, 2), BF),
            *both((depth,), BF), *both((depth,), BF),
            *both((depth,), BF), *both((depth - 1,), BF),
            *both((m,), BF), *both((), F32),
            pltpu.VMEM((m, 8, 128), F32),
            pltpu.VMEM((2, 8, 128), F32),
            pltpu.VMEM((2, 8, 128), F32),
            pltpu.VMEM((depth, 8, 128), F32),
            pltpu.VMEM((8, 128), F32),
            pltpu.SemaphoreType.DMA((1 + LAYERS, depth + m)),
            pltpu.SemaphoreType.DMA((1 + LAYERS, depth + m)),
            pltpu.SemaphoreType.DMA((m + depth,)),
            pltpu.SemaphoreType.DMA((m + depth,)),
        ],
        compiler_params=pltpu.CompilerParams(
            collective_id=2, has_side_effects=True, vmem_limit_bytes=VMEM_LIMIT
        ),
        name="update",
    )(g_rest, g_layers, stats, *masters, *firsts, *seconds)
    totals = outs[0]
    return (
        totals[0, 0],
        totals[1, 0],
        totals[2, 0],
        *unpacked(*outs[1:9]),
        *unpacked(*outs[9:17]),
        *unpacked(*outs[17:25]),
    )


def solution(mesh):
    pixels = P("img", None, "seq")
    weights = (
        P(None, "seq"),
        P(None, "seq"),
        P(None, "seq", None),
        P(None, "seq", None),
        P(None, "seq", None),
        P(None, None, "seq"),
        P("seq", None),
        P(None, None, "seq"),
    )

    def body(pixels, loss_mask, *rest):
        geo = Geometry(mesh.shape["seq"], mesh.shape["img"], pixels.shape[0], pixels.shape[1])
        return on_device(geo, pixels, loss_mask, *rest)

    return jax.shard_map(
        body,
        mesh=mesh,
        in_specs=(pixels, pixels) + weights * 3,
        out_specs=(P(), P(), P()) + weights * 3,
        check_vma=False,
    )
```

time: 1640 us -> 302 us (0.18)
  waiting for transfers between devices: 621 us -> 0 us
  blocking collectives: 436 us -> 0 us
  matrix products: 272 us -> 0 us
  Pallas kernels: 0 us -> 258 us
  other arithmetic: 90.7 us -> 0 us
  starting transfers between devices: 70.9 us -> 0 us
  local copies, waits for them, and re-layouts: 112 us -> 41.6 us
  between operations: 25.4 us -> 0.71 us
    reduce_scatter x6 -> x0, waiting for transfers between devices: 360 us -> none  [the longest x1 66.1 us: on_device(): lax.psum_scatter(s_in, 'seq', scatter_dimension=1, tiled=True)]
    pallas_call x0 -> x3, Pallas kernels: none -> 258 us  [the longest x1 162 us: on_device(): pl.pallas_call(functools.partial(step_kernel, geo, chunk), out_shape=(jax...]
    dot_general x79 -> x0, matrix products: 254 us -> none  [the longest x62 226 us: product(): return jnp.einsum(form, left, right, preferred_element_type=jnp.float32)]
    all_to_all x5 -> x0, blocking collectives: 198 us -> none  [the longest x3 131 us: layer_backward(): lax.all_to_all(packed, 'seq', split_axis=0, concat_axis=1, tiled=True)]
    all_gather x7 -> x0, blocking collectives: 164 us -> none  [the longest x1 36.8 us: on_device(): lax.all_gather(attn_out.astype(bfloat), 'seq', axis=1, tiled=True)]
    unnamed x13 -> x0, waiting for transfers between devices: 108 us -> none
    all_to_all x7 -> x0, waiting for transfers between devices: 101 us -> none  [the longest x3 78.1 us: layer_backward(): lax.all_to_all(reply, 'seq', split_axis=1, concat_axis=0, tiled=True)]
    psum x2 -> x0, blocking collectives: 73.8 us -> none  [the longest x1 40 us: on_device(): lax.psum((jnp.sum(mask_rows * per_token), jnp.sum(mask_rows)), ('seq', 'i...]
  transfers between devices with their start and end apart: 28 -> 0, of which waited for: 23 -> 0; matrix products, arithmetic and copies ran while one was open for 8% -> 0% of each run, Pallas kernels for 0% -> 0%
where the time goes in v1:
time: 302 us; the launch traced here: 300 us
  Pallas kernels  258 us (85%)
  local copies, waits for them, and re-layouts  41.6 us (14%)
    pallas_call x1, Pallas kernels, on_device(): pl.pallas_call(functools.partial(step_kernel, geo, chunk), out_shape=(jax...  162 us
    pallas_call x1, Pallas kernels, on_device(): pl.pallas_call(functools.partial(update_kernel, geo), out_shape=[stat] +...  49.6 us
    pallas_call x1, Pallas kernels, on_device(): pl.pallas_call(functools.partial(gather_kernel, geo), out_shape=(jax.Shap...  46.6 us
    unnamed x18, local copies, waits for them, and re-layouts  26.2 us

profile of v1, /device:TPU:0, one launch (start us, length us, event | category | flops | bytes accessed | tf_op | source)
XLA Modules:
  0.0 300.2 jit_solution(15351238179875235709)
XLA Ops:
  2.1 1.3 pad.20.pos.refs_4_
  3.4 46.6 %gather.1 = (s32[4,2,2,16,8,24]{5,4,3,2,1,0:T(8,128)}, bf16[4,2,2,16,768]{4,3,2,1,0:T(8,128)(2,1)}, bf16[3,4,2,2,16,2048]{5,4,3,2,1,0:T(8,128)(2,1)}) custom-call(s32[8,8,24]{2,1,0:T(8,128)} %bitcast.44, s32[8,8,24]{2,1,0:T(8,128)} %bitcast.45, f32[16,256]{1,0:T(8,128)} %bitcast.42, f32[16,128]{1,0:T(8,128)} %pad.20.pos.refs_4_, f32[3,16,768]{2,1,0:T(8,128)} %refs_5_.1, ...), custom_call_target="tpu_custom_call" | custom-call | tf_op jit(solution)/shard_map/gather/pallas_call | solution.py:627
  49.9 161.7 %step.1 = (f32[4,2,2,16,768]{4,3,2,1,0:T(8,128)}, f32[3,4,2,2,16,2048]{5,4,3,2,1,0:T(8,128)}, f32[8,128]{1,0:T(8,128)}) custom-call(s32[4,2,2,16,8,24]{5,4,3,2,1,0:T(8,128)} %get-tuple-element.58.px, bf16[4,2,2,16,768]{4,3,2,1,0:T(8,128)(2,1)} %get-tuple-element.59.rest, bf16[3,4,2,2,16,2048]{5,4,3,2,1,0:T(8,128)(2,1)} %get-tuple-element.60.layers), custom_call_target="tpu_custom_call" | custom-call | tf_op jit(solution)/shard_map/step/pallas_call | solution.py:649
  217.1 49.6 %update.1 = (f32[8,128]{1,0:T(8,128)}, f32[16,256]{1,0:T(8,128)}, f32[16,128]{1,0:T(8,128)}, f32[3,16,768]{2,1,0:T(8,128)}, f32[3,16,256]{2,1,0:T(8,128)}, /*ind...) custom-call(f32[4,2,2,16,768]{4,3,2,1,0:T(8,128)} %get-tuple-element, ...), custom_call_target="tpu_custom_call" | custom-call | tf_op jit(solution)/shard_map/update/pallas_call | solution.py:703
  268.7 1.3 slice_bitcast_fusion.1
  270.1 1.3 fusion
  274.1 1.3 copy.83
  275.4 1.6 copy.84
  277.0 1.4 copy.85
  278.4 1.5 copy.86
  279.9 1.5 copy.87
  281.5 1.3 copy.88
  282.8 1.3 copy.89
  284.1 1.6 copy.90
  285.7 1.4 copy.91
  287.1 1.5 copy.92
  288.6 1.5 copy.93
  290.2 1.3 copy.94
  291.5 1.3 copy.95
  292.8 1.6 copy.96
  294.4 1.4 copy.97
  295.8 1.5 copy.98
  297.4 1.5 copy.99
  298.9 1.3 copy.100
  (20 shorter events, 11.6 us)

commit v2 on v1

v2 whole, which is shorter than its diff:
```python
import functools
import math

import jax
import jax.numpy as jnp
from jax import lax
from jax.experimental import pallas as pl
from jax.experimental.pallas import tpu as pltpu
from jax.sharding import PartitionSpec as P

D = 256
HEAD = 128
FF = 512
V = 256
STRIDE = 128
LAYERS = 3
NORMS = 2 * LAYERS + 1
STEP = 10
SIDE = 32
POS = 2 * SIDE + 3
CLIP_NORM = 0.05
BETA_ONE = 0.9
BETA_TWO = 0.95
LEARN_RATE = 0.1
WEIGHT_DECAY = 0.1
ADAM_EPS = 1e-08
SMOOTHING = 0.1
NORM_EPS = 1e-05
SCALE = HEAD ** (-0.5)

C_IN, C_OUT, C_UP, C_DOWN = (0, 768), (768, 1024), (1024, 1536), (1536, 2048)
C_LAYER = 2048
C_TOK, C_POS, C_NORM, C_HEAD = (0, 256), (256, 384), (384, 512), (512, 768)
C_REST = 768
C_ALL = LAYERS * C_LAYER + C_REST

BF = jnp.bfloat16
F32 = jnp.float32
VMEM_LIMIT = 64 * 1024 * 1024


def dot(a, b):
    return lax.dot_general(a, b, (((1,), (0,)), ((), ())), preferred_element_type=F32)


def dot_nt(a, b):
    return lax.dot_general(a, b, (((1,), (1,)), ((), ())), preferred_element_type=F32)


def dot_tn(a, b):
    return lax.dot_general(a, b, (((0,), (0,)), ((), ())), preferred_element_type=F32)


class Geometry:
    def __init__(self, n, m, images, blocks):
        self.n, self.m, self.images, self.blocks = n, m, images, blocks
        self.depth = n // 4
        self.rows = D // n
        self.group = n // images
        self.res = STRIDE // self.group
        self.own = STRIDE // n
        self.wide = -(-images * blocks // 128) * 128

    def place(self):
        me = lax.axis_index("seq")
        return me // 4, me // 2 % 2, me % 2


def seq_id(z, y, core):
    return {"seq": z * 4 + y * 2 + core}


def greet(devices):
    barrier = pltpu.get_barrier_semaphore()
    for device in devices:
        pl.semaphore_signal(barrier, inc=1, device_id=device, device_id_type=pl.DeviceIdType.MESH)
    pl.semaphore_wait(barrier, len(devices))


def push(src, dst, send_sem, recv_sem, device):
    return pltpu.make_async_remote_copy(
        src_ref=src,
        dst_ref=dst,
        send_sem=send_sem,
        recv_sem=recv_sem,
        device_id=device,
        device_id_type=pl.DeviceIdType.MESH,
    )


def normalise(x):
    centre = x - jnp.mean(x, -1, keepdims=True)
    spread = jnp.mean(centre * centre, -1, keepdims=True)
    rstd = lax.rsqrt(spread + NORM_EPS)
    return centre * rstd, rstd


def fold(x):
    return jnp.sum(x.reshape(x.shape[0] // 8, 8, x.shape[1]), 0)


def normalise_back(dy, unit, rstd, gain):
    dxh = dy * (1.0 + gain)
    mean_one = jnp.mean(dxh, -1, keepdims=True)
    mean_two = jnp.mean(dxh * unit, -1, keepdims=True)
    return rstd * (dxh - mean_one - unit * mean_two), fold(dy * unit), fold(dy)


def gelu_both(u):
    c = math.sqrt(2.0 / math.pi)
    square = u * u
    t = jnp.tanh(c * u * (1.0 + 0.044715 * square))
    half = 0.5 * (1.0 + t)
    slope = half + 0.5 * u * (1.0 - t * t) * (c * (1.0 + 3.0 * 0.044715 * square))
    return u * half, slope


def softmax(scores):
    e = jnp.exp(scores - jnp.max(scores, -1, keepdims=True))
    return e * (1.0 / jnp.sum(e, -1, keepdims=True))


def step_kernel(
    geo, chunk, batch,
    pixels, mask, tok, pos, w_in, w_out, w_up, w_down, head, norms,
    sums, totals,
    px, rest, layers, g_rest, g_layers,
    x_s, x1_s, q0_s, kv_s, qkv1_s, p0_s, p1_s, o_s, a_s, slope_s, stage, o1_s, do0_s, dq0_s,
    own_s, away_s, back_s, edge_s, dx_s, ids_s, tgt_s, msk_s, prev_s, pack_s, bias0, bias1, norm_s, gnorm, wide,
    s1, r1, s2, r2, s3, r3, r4, st_img, st_core, st_y, st_z,
    g_send, g_recv, kv_send, kv_recv, rs_send, rs_recv, st_send, st_recv,
):
    z, y, core = geo.place()
    me, x_img = lax.axis_index("seq"), lax.axis_index("img")
    depth, group, res, blocks, own, m = geo.depth, geo.group, geo.res, geo.blocks, geo.own, geo.m
    image, part = me // group, me % group
    siblings = [{"seq": image * group + lax.rem(part + k, group)} for k in range(1, group)]
    peers = [seq_id(lax.rem(z + k, depth), y, core) for k in range(1, depth)]
    beside, sibling = seq_id(z, 1 - y, core), seq_id(z, y, 1 - core)
    across = [{"img": lax.rem(x_img + k, m)} for k in range(1, m)]
    rows = chunk * res
    chunks = blocks // chunk
    n_groups = res // 8
    every, pair = pl.ds(0, depth), pl.ds(0, 2)

    rest[z, y, core, :, C_TOK[0] : C_TOK[1]] = tok[...].astype(BF)
    wide[...] = jnp.zeros_like(wide)
    wide[: geo.rows, :POS] = pos[...]
    rest[z, y, core, :, C_POS[0] : C_POS[1]] = wide[: geo.rows, :128].astype(BF)
    wide[...] = jnp.zeros_like(wide)
    for i in range(NORMS):
        wide[2 * i : 2 * i + 2, : geo.rows] = norms[i]
    rest[z, y, core, :, C_NORM[0] : C_NORM[1]] = jnp.transpose(wide[:, :128])[: geo.rows].astype(BF)
    rest[z, y, core, :, C_HEAD[0] : C_HEAD[1]] = head[...].astype(BF)
    for l in range(LAYERS):
        layers[l, z, y, core, :, C_IN[0] : C_IN[1]] = w_in[l].astype(BF)
        layers[l, z, y, core, :, C_OUT[0] : C_OUT[1]] = w_out[l].astype(BF)
        layers[l, z, y, core, :, C_UP[0] : C_UP[1]] = w_up[l].astype(BF)
        layers[l, z, y, core, :, C_DOWN[0] : C_DOWN[1]] = w_down[l].astype(BF)
    pack_s[...] = jnp.zeros_like(pack_s)
    pack_s[:, :own, :blocks] = pixels[...].astype(F32)
    pack_s[:, own:, :blocks] = mask[...].astype(F32)
    at = lax.broadcasted_iota(jnp.int32, (128, geo.wide), 0)
    to = lax.broadcasted_iota(jnp.int32, (128, geo.wide), 1)
    packed = jnp.zeros((2 * own, geo.wide), F32)
    for i in range(geo.images):
        spot = ((to == at + i * blocks) & (at < blocks)).astype(F32).astype(BF)
        packed = packed + dot(pack_s[i].astype(BF), spot)
    px[z, y, core] = packed.astype(BF)

    others = peers + [beside] + across
    others = others + (siblings if group > 2 else [sibling])
    if group > 2:
        others = [d for d in others if d is not beside]
    greet(others)

    parts = [px, rest.at[..., 0 : C_NORM[1]], layers.at[0, ..., 0 : C_IN[1]], layers.at[0, ..., C_OUT[0] : C_LAYER]]
    parts += [layers.at[1], rest.at[..., C_HEAD[0] : C_HEAD[1]], layers.at[2]]

    def gather_z(a, k):
        mine = parts[a].at[z, y, core]
        return push(mine, mine, g_send.at[a, k], g_recv.at[a, k], peers[k])

    def gather_y(a):
        column = parts[a].at[every, y, core]
        return push(column, column, g_send.at[a, depth - 1], g_recv.at[a, depth - 1], beside)

    def gather_core(a):
        half = parts[a].at[every, pair, core]
        return push(half, half, g_send.at[a, depth], g_recv.at[a, depth], sibling)

    def to_y(a):
        for k in range(depth - 1):
            gather_z(a, k).wait_recv()
        gather_y(a).start()

    def to_core(a):
        gather_y(a).wait_recv()
        gather_core(a).start()

    def arrived(a):
        gather_core(a).wait_recv()

    for a in range(len(parts)):
        for k in range(depth - 1):
            gather_z(a, k).start()

    def table(ref, cols):
        piece = ref[..., cols[0] : cols[1]]
        width = cols[1] - cols[0]
        if geo.rows % 16:
            return piece.astype(F32).reshape(D, width).astype(BF)
        return piece.reshape(D, width)

    def layer_table(l, cols):
        return table(layers.at[l], cols)

    def add_to(ref, cols, value):
        shape = (depth, 2, 2, geo.rows, cols[1] - cols[0])
        ref[..., cols[0] : cols[1]] += value.reshape(shape)

    for ref in (ids_s, tgt_s, msk_s, prev_s, wide, g_rest, g_layers, gnorm):
        ref[...] = jnp.zeros_like(ref)
    for l in range(LAYERS):
        kv_s[l, 0] = jnp.zeros((group, res, 2 * HEAD), BF)

    qi = part * res + lax.broadcasted_iota(jnp.int32, (res, 2 * STRIDE), 0)
    kj = lax.broadcasted_iota(jnp.int32, (res, 2 * STRIDE), 1)
    kj = kj // STRIDE * STRIDE + (kj % STRIDE + part * res) % STRIDE
    seen = (kj > qi) & (kj <= qi + STRIDE)
    bias0[0] = jnp.where(seen & (kj >= STRIDE), 0.0, -1e30)
    bias0[1] = jnp.where(seen, 0.0, -1e30)
    side = 8 * blocks
    ri = lax.broadcasted_iota(jnp.int32, (side, side), 0)
    ci = lax.broadcasted_iota(jnp.int32, (side, side), 1)
    bias1[...] = jnp.where(((ri & 7) == (ci & 7)) & (ri >= ci), 0.0, -1e30)

    to_y(0)
    to_y(1)
    to_y(2)
    to_core(0)
    to_core(1)
    to_y(3)
    to_core(2)
    arrived(0)

    span = depth // group
    at = lax.broadcasted_iota(jnp.int32, (geo.wide, 128), 0)
    to = lax.broadcasted_iota(jnp.int32, (geo.wide, 128), 1)
    spot = ((at == to + image * blocks) & (to < blocks)).astype(F32).astype(BF)
    for j in range(geo.images):
        piece = dot(px[part * span + j // 4, j // 2 % 2, j % 2], spot)
        tgt_s[j * own : (j + 1) * own, :] = piece[:own]
        msk_s[j * own : (j + 1) * own, :] = piece[own:]
    prev = dot(px[lax.rem(part * span + depth - 1, depth), 1, 1], spot)[:own]
    lane = lax.broadcasted_iota(jnp.int32, prev.shape, 1)
    moved = jnp.where(lane == 0, -1.0, pltpu.roll(prev, 1, 1))
    prev = jnp.where(part == 0, moved, prev)
    ids_s[0:1, :] = prev[own - 1 : own, :]
    ids_s[1:res, :] = tgt_s[0 : res - 1, :]

    arrived(1)
    norm_s[...] = jnp.transpose(table(rest, C_NORM).astype(F32))[:16].reshape(16, 1, D)

    def spread(ref, b0):
        values = ref[...].astype(BF)
        at = lax.broadcasted_iota(jnp.int32, (128, 128), 0)
        return jnp.concatenate(
            [dot(values, (at == b0 + j).astype(F32).astype(BF)) for j in range(chunk)], 0
        )

    def one_hot(ref, b0):
        value = spread(ref, b0)
        lane = lax.broadcasted_iota(jnp.int32, (rows, 128), 1).astype(F32)
        return jnp.concatenate([(value == lane).astype(F32), (value == lane + 128.0).astype(F32)], 1)

    def place_hot(b0):
        r = lax.broadcasted_iota(jnp.int32, (rows, 128), 0)
        lane = lax.broadcasted_iota(jnp.int32, (rows, 128), 1).astype(F32)
        p = ((b0 + r // res) * STRIDE + part * res + r % res).astype(F32)
        third = jnp.floor((p + 0.5) * (1.0 / 3.0))
        line = jnp.floor((third + 0.5) * (1.0 / SIDE))
        hits = (lane == line) | (lane == SIDE + third - SIDE * line)
        return (hits | (lane == 2 * SIDE + p - 3.0 * third)).astype(F32)

    def loop(count, body):
        lax.fori_loop(0, count, lambda i, carry: (body(i), carry)[1], 0)

    def embed(i):
        b0 = i * chunk
        hot = jnp.concatenate([one_hot(ids_s, b0), place_hot(b0)], 1).astype(BF)
        x = dot_nt(hot, table(rest, (C_TOK[0], C_POS[1])))
        x_s[0, pl.ds(b0, chunk)] = x.reshape(chunk, res, D)

    loop(chunks, embed)

    def exchange(l, k):
        mine = kv_s.at[l, pl.ds(1, blocks), 0]
        there = kv_s.at[l, pl.ds(1, blocks), group - 1 - k]
        return push(mine, there, kv_send.at[k], kv_recv.at[l, k], siblings[k])

    def forward(l):
        def mix(i):
            b0 = i * chunk
            at = pl.ds(b0, chunk)
            unit, _ = normalise(x_s[l, at].reshape(rows, D))
            h = (unit * (1.0 + norm_s[4 * l]) + norm_s[4 * l + 1]).astype(BF)
            qkv = dot(h, layer_table(l, C_IN)).reshape(chunk, res, 6 * HEAD)
            q0_s[l, at] = qkv[..., :HEAD].astype(BF)
            kv_s[l, pl.ds(b0 + 1, chunk), 0, :, :HEAD] = qkv[..., 2 * HEAD : 3 * HEAD].astype(BF)
            kv_s[l, pl.ds(b0 + 1, chunk), 0, :, HEAD:] = qkv[..., 4 * HEAD : 5 * HEAD].astype(BF)
            stage[at, :, :HEAD] = qkv[..., HEAD : 2 * HEAD]
            stage[at, :, HEAD : 2 * HEAD] = qkv[..., 3 * HEAD : 4 * HEAD]
            stage[at, :, 2 * HEAD :] = qkv[..., 5 * HEAD :]

        def strided(g):
            at = pl.ds(pl.multiple_of(8 * g, 8), 8)
            qkv = stage[:, at, :].reshape(8 * blocks, 3 * HEAD).astype(BF)
            qkv1_s[l, g] = qkv
            scores = dot_nt(qkv[:, :HEAD], qkv[:, HEAD : 2 * HEAD]) * SCALE + bias1[...]
            probs = softmax(scores).astype(BF)
            p1_s[l, g] = probs
            o1_s[:, at, :] = dot(probs, qkv[:, 2 * HEAD :]).reshape(blocks, 8, HEAD)

        def window(i):
            b0 = i * batch
            kv = kv_s[l, pl.ds(b0, batch + 1)].reshape((batch + 1) * STRIDE, 2 * HEAD)
            raw = [
                dot_nt(q0_s[l, b0 + j], kv[j * STRIDE : (j + 2) * STRIDE, :HEAD]) * SCALE
                + bias0[jnp.minimum(b0 + j, 1)]
                for j in range(batch)
            ]
            probs = softmax(jnp.concatenate(raw, 0)).astype(BF)
            p0_s[l, pl.ds(b0, batch)] = probs.reshape(batch, res, 2 * STRIDE)
            for j in range(batch):
                value = dot(probs[j * res : (j + 1) * res], kv[j * STRIDE : (j + 2) * STRIDE, HEAD:])
                o_s[l, b0 + j, :, :HEAD] = value.astype(BF)

        def feed(i):
            b0 = i * chunk
            at = pl.ds(b0, chunk)
            o_s[l, at, :, HEAD:] = o1_s[at].astype(BF)
            x1 = x_s[l, at].reshape(rows, D) + dot(o_s[l, at].reshape(rows, D), layer_table(l, C_OUT))
            x1_s[l, at] = x1.reshape(chunk, res, D)
            unit, _ = normalise(x1)
            h = (unit * (1.0 + norm_s[4 * l + 2]) + norm_s[4 * l + 3]).astype(BF)
            a, slope = gelu_both(dot(h, layer_table(l, C_UP)))
            a = a.astype(BF)
            a_s[l, at] = a.reshape(chunk, res, FF)
            slope_s[l, at] = slope.astype(BF).reshape(chunk, res, FF)
            x2 = x1 + dot_nt(a, layer_table(l, C_DOWN))
            x_s[l + 1, at] = x2.reshape(chunk, res, D)

        arrived((2, 4, 6)[l])
        loop(chunks, mix)
        copies = [exchange(l, k) for k in range(group - 1)]
        for copy in copies:
            copy.start()
        if l == 0:
            to_core(3)
            to_y(4)
        if l == 1:
            to_core(5)
            to_core(6)
        loop(n_groups, strided)
        for copy in copies:
            copy.wait()
        loop(blocks // batch, window)
        if l == 0:
            arrived(3)
            to_y(5)
        loop(chunks, feed)
        if l == 0:
            to_core(4)
            to_y(6)

    for l in range(LAYERS):
        forward(l)
    arrived(5)

    def finish(i, loss):
        b0 = i * chunk
        at = pl.ds(b0, chunk)
        unit, rstd = normalise(x_s[LAYERS, at].reshape(rows, D))
        gain = norm_s[4 * LAYERS]
        h = (unit * (1.0 + gain) + norm_s[4 * LAYERS + 1]).astype(BF)
        table_head = table(rest, C_HEAD)
        logits = dot(h, table_head)
        hot = one_hot(tgt_s, b0)
        shift = logits - jnp.max(logits, -1, keepdims=True)
        e = jnp.exp(shift)
        total = jnp.sum(e, -1, keepdims=True)
        weight = spread(msk_s, b0)
        per = (
            jnp.log(total)
            - (1.0 - SMOOTHING) * jnp.sum(hot * shift, -1, keepdims=True)
            - SMOOTHING * jnp.mean(shift, -1, keepdims=True)
        )
        loss = loss + jnp.sum(weight[:, :1] * per, 0, keepdims=True)
        weight = jnp.concatenate([weight, weight], 1)
        d_logits = weight * (e * (1.0 / total) - (1.0 - SMOOTHING) * hot - SMOOTHING / V)
        d_logits = d_logits.astype(BF)
        add_to(g_rest, C_HEAD, dot_tn(h, d_logits))
        dx, g_gain, g_bias = normalise_back(dot_nt(d_logits, table_head), unit, rstd, gain)
        gnorm[4 * LAYERS] += g_gain
        gnorm[4 * LAYERS + 1] += g_bias
        dx_s[at] = dx.reshape(chunk, res, D)
        return loss

    loss = lax.fori_loop(0, chunks, finish, jnp.zeros((1, 1), F32))
    count = jnp.sum(jnp.sum(msk_s[...], 0, keepdims=True), 1, keepdims=True)
    line = lax.broadcasted_iota(jnp.int32, (8, 128), 0)
    st_img[x_img] = jnp.where(line == 0, loss, jnp.where(line == 1, count, 0.0))
    st_across = [
        push(st_img.at[x_img], st_img.at[x_img], st_send.at[k], st_recv.at[k], across[k]) for k in range(m - 1)
    ]
    for copy in st_across:
        copy.start()

    def give(l, k):
        return push(
            away_s.at[k, pl.ds(1, blocks)], back_s.at[l % 2, k], kv_send.at[k], kv_recv.at[LAYERS + l, k], siblings[k]
        )

    def backward(l, after_feed, after_window, after_strided):
        grads = g_layers.at[l % 2]

        def feed(i):
            b0 = i * chunk
            at = pl.ds(b0, chunk)
            dx2 = dx_s[at].reshape(rows, D)
            g2 = dx2.astype(BF)
            a = a_s[l, at].reshape(rows, FF)
            add_to(grads, C_DOWN, dot_tn(g2, a))
            du = slope_s[l, at].reshape(rows, FF).astype(F32) * dot(g2, layer_table(l, C_DOWN))
            du = du.astype(BF)
            unit, rstd = normalise(x1_s[l, at].reshape(rows, D))
            gain = norm_s[4 * l + 2]
            h = (unit * (1.0 + gain) + norm_s[4 * l + 3]).astype(BF)
            add_to(grads, C_UP, dot_tn(h, du))
            dh = dot_nt(du, layer_table(l, C_UP))
            dx, g_gain, g_bias = normalise_back(dh, unit, rstd, gain)
            gnorm[4 * l + 2] += g_gain
            gnorm[4 * l + 3] += g_bias
            dx = dx + dx2
            dx_s[at] = dx.reshape(chunk, res, D)
            g1 = dx.astype(BF)
            add_to(grads, C_OUT, dot_tn(o_s[l, at].reshape(rows, D), g1))
            do = dot_nt(g1, layer_table(l, C_OUT)).reshape(chunk, res, D)
            do0_s[at] = do[..., :HEAD].astype(BF)
            o1_s[at] = do[..., HEAD:]

        def window(i):
            b0 = i * batch
            at = pl.ds(b0, batch)
            kv = kv_s[l, pl.ds(b0, batch + 1)].reshape((batch + 1) * STRIDE, 2 * HEAD)
            probs = p0_s[l, at].reshape(batch * res, 2 * STRIDE)
            do = [do0_s[b0 + j] for j in range(batch)]
            keys = [kv[j * STRIDE : (j + 2) * STRIDE, :HEAD] for j in range(batch)]
            dp = jnp.concatenate(
                [dot_nt(do[j], kv[j * STRIDE : (j + 2) * STRIDE, HEAD:]) for j in range(batch)], 0
            )
            wide_p = probs.astype(F32)
            ds = (wide_p * (dp - jnp.sum(wide_p * dp, -1, keepdims=True)) * SCALE).astype(BF)
            carry = edge_s[...]
            for j in range(batch):
                cut = slice(j * res, (j + 1) * res)
                dq0_s[b0 + j] = dot(ds[cut], keys[j]).astype(BF)
                dkv = jnp.concatenate([dot_tn(ds[cut], q0_s[l, b0 + j]), dot_tn(probs[cut], do[j])], 1)
                done = (carry + dkv[:STRIDE]).reshape(group, res, 2 * HEAD)
                own_s[b0 + j] = done[0]
                for k in range(group - 1):
                    away_s[k, b0 + j] = done[k + 1].astype(BF)
                carry = dkv[STRIDE:]
            edge_s[...] = carry

        def strided(g):
            at = pl.ds(pl.multiple_of(8 * g, 8), 8)
            qkv = qkv1_s[l, g]
            probs = p1_s[l, g]
            do = o1_s[:, at, :].reshape(8 * blocks, HEAD).astype(BF)
            dp = dot_nt(do, qkv[:, 2 * HEAD :])
            wide_p = probs.astype(F32)
            ds = (wide_p * (dp - jnp.sum(wide_p * dp, -1, keepdims=True)) * SCALE).astype(BF)
            dq = dot(ds, qkv[:, HEAD : 2 * HEAD])
            dk = dot_tn(ds, qkv[:, :HEAD])
            dv = dot_tn(probs, do)
            stage[:, at, :] = jnp.concatenate([dq, dk, dv], 1).reshape(blocks, 8, 3 * HEAD)

        def mix(i):
            b0 = i * chunk
            at = pl.ds(b0, chunk)
            dkv = own_s[pl.ds(b0 + 1, chunk)]
            for k in range(group - 1):
                dkv = dkv + back_s[l % 2, k, at].astype(F32)
            d1 = stage[at]
            dqkv = jnp.concatenate(
                [
                    dq0_s[at],
                    d1[..., :HEAD].astype(BF),
                    dkv[..., :HEAD].astype(BF),
                    d1[..., HEAD : 2 * HEAD].astype(BF),
                    dkv[..., HEAD:].astype(BF),
                    d1[..., 2 * HEAD :].astype(BF),
                ],
                -1,
            ).reshape(rows, 6 * HEAD)
            unit, rstd = normalise(x_s[l, at].reshape(rows, D))
            gain = norm_s[4 * l]
            h = (unit * (1.0 + gain) + norm_s[4 * l + 1]).astype(BF)
            add_to(grads, C_IN, dot_tn(h, dqkv))
            dh = dot_nt(dqkv, layer_table(l, C_IN))
            dx, g_gain, g_bias = normalise_back(dh, unit, rstd, gain)
            gnorm[4 * l] += g_gain
            gnorm[4 * l + 1] += g_bias
            dx_s[at] += dx.reshape(chunk, res, D)

        loop(chunks, feed)
        after_feed()
        edge_s[...] = jnp.zeros_like(edge_s)
        loop(blocks // batch, window)
        last = edge_s[...].reshape(group, res, 2 * HEAD)
        own_s[blocks] = last[0]
        for k in range(group - 1):
            away_s[k, blocks] = last[k + 1].astype(BF)
        copies = [give(l, k) for k in range(group - 1)]
        for copy in copies:
            copy.start()
        after_window()
        loop(n_groups, strided)
        after_strided()
        for copy in copies:
            copy.wait()
        loop(chunks, mix)

    def section(index, ref, cols, base):
        width = cols[1] - cols[0]
        cut = slice(base, base + width)
        grad = ref.at[..., cols[0] : cols[1]]
        first = push(s1.at[..., cut], r1.at[..., cut], rs_send.at[index, 0], rs_recv.at[index, 0], sibling)
        second = push(s2.at[..., cut], r2.at[..., cut], rs_send.at[index, 1], rs_recv.at[index, 1], beside)
        third = [
            push(
                s3.at[lax.rem(z + k, depth), :, cut],
                r3.at[k - 1, :, cut],
                rs_send.at[index, 1 + k],
                rs_recv.at[index, 1 + k],
                peers[k - 1],
            )
            for k in range(1, depth)
        ]
        fourth = [
            push(
                r4.at[x_img, :, cut],
                r4.at[x_img, :, cut],
                rs_send.at[index, depth + 1 + k],
                rs_recv.at[index, depth + 1 + k],
                across[k],
            )
            for k in range(m - 1)
        ]

        def go_core():
            s1[..., cut] = grad[every, pair, 1 - core].astype(BF)
            first.start()

        def go_y():
            first.wait()
            total = grad[every, 1 - y, core] + r1[every, 1 - y, :, cut].astype(F32)
            s2[..., cut] = total.astype(BF)
            second.start()

        def go_z():
            second.wait()
            total = grad[every, y, core] + r1[every, y, :, cut].astype(F32) + r2[..., cut].astype(F32)
            s3[..., cut] = total.astype(BF)
            for copy in third:
                copy.start()

        def go_img():
            for copy in third:
                copy.wait()
            total = s3[z, :, cut].astype(F32)
            for k in range(1, depth):
                total = total + r3[k - 1, :, cut].astype(F32)
            r4[x_img, :, cut] = total.astype(BF)
            for copy in fourth:
                copy.start()

        def end():
            for copy in fourth:
                copy.wait()
            total = r4[0, :, cut].astype(F32)
            for k in range(1, m):
                total = total + r4[k, :, cut].astype(F32)
            sums[:, cut] = total
            return jnp.sum(jnp.sum(total * total, 0, keepdims=True), 1, keepdims=True)

        return go_core, go_y, go_z, go_img, end

    two = section(0, g_layers.at[0], (0, C_LAYER), 2 * C_LAYER)
    one = section(1, g_layers.at[1], (0, C_LAYER), C_LAYER)
    zero_rest = section(2, g_layers.at[0], (C_OUT[0], C_LAYER), C_OUT[0])
    zero_in = section(3, g_layers.at[0], C_IN, 0)
    other = section(4, g_rest, (0, C_REST), LAYERS * C_LAYER)

    def run(*steps):
        def inner():
            for step in steps:
                step()

        return inner

    nothing = run()
    backward(2, nothing, nothing, nothing)
    two[0]()
    backward(1, two[1], two[2], two[3])
    squares = two[4]()
    one[0]()
    g_layers[0] = jnp.zeros(g_layers.shape[1:], F32)
    backward(0, run(zero_rest[0], one[1]), run(zero_rest[1], one[2]), run(zero_rest[2], one[3]))
    zero_in[0]()
    zero_rest[3]()
    squares = squares + one[4]()

    def embed_back(i):
        b0 = i * chunk
        hot = jnp.concatenate([one_hot(ids_s, b0), place_hot(b0)], 1).astype(BF)
        dx = dx_s[pl.ds(b0, chunk)].reshape(rows, D)
        high = dx.astype(BF)
        low = (dx - high.astype(F32)).astype(BF)
        add_to(g_rest, (C_TOK[0], C_POS[1]), dot_tn(high, hot) + dot_tn(low, hot))

    loop(chunks, embed_back)
    for i in range(2 * NORMS):
        wide[i : i + 1, :] = jnp.sum(gnorm[i], 0, keepdims=True)
    add_to(g_rest, C_NORM, jnp.transpose(wide[...]))
    other[0]()
    zero_in[1]()
    other[1]()
    zero_in[2]()
    other[2]()
    squares = squares + zero_rest[4]()
    zero_in[3]()
    other[3]()
    squares = squares + zero_in[4]()
    squares = squares + other[4]()

    for copy in st_across:
        copy.wait()
    told = st_img[0]
    for k in range(1, m):
        told = told + st_img[k]
    told = jnp.where(line == 2, squares, told)
    base = m - 1

    def swap(told, buffer, index, where, device):
        buffer[where] = told
        copy = push(buffer.at[where], buffer.at[where], st_send.at[base + index], st_recv.at[base + index], device)
        copy.start()
        copy.wait()
        return buffer[0] + buffer[1]

    told = swap(told, st_core, 0, core, sibling)
    told = swap(told, st_y, 1, y, beside)
    st_z[z] = told
    copies = [
        push(st_z.at[z], st_z.at[z], st_send.at[base + 1 + k], st_recv.at[base + 1 + k], peers[k - 1])
        for k in range(1, depth)
    ]
    for copy in copies:
        copy.start()
    for a in range(len(parts)):
        for k in range(depth - 1):
            gather_z(a, k).wait_send()
        gather_y(a).wait_send()
        gather_core(a).wait_send()
    for copy in copies:
        copy.wait()
    told = st_z[0]
    for k in range(1, depth):
        told = told + st_z[k]
    count = told[1:2, :1]
    norm = jnp.sqrt(told[2:3, :1]) / count
    factor = jnp.minimum(1.0, CLIP_NORM / norm) / count
    totals[...] = jnp.where(line == 2, norm, jnp.where(line == 3, factor, told))


def adam(master, gradient, first, second):
    first = BETA_ONE * first + (1.0 - BETA_ONE) * gradient
    second = BETA_TWO * second + (1.0 - BETA_TWO) * gradient * gradient
    moved = first / (1.0 - BETA_ONE**STEP) / (jnp.sqrt(second / (1.0 - BETA_TWO**STEP)) + ADAM_EPS)
    return master - LEARN_RATE * (moved + WEIGHT_DECAY * master), first, second


def update_kernel(rows, *refs):
    sums, totals = refs[:2]
    masters, firsts, seconds = refs[2:10], refs[10:18], refs[18:26]
    outs = (refs[26:34], refs[34:42], refs[42:50])
    turned = refs[50]
    factor = totals[3:4, :1]

    def put(index, at, gradient):
        result = adam(masters[index][at], gradient * factor, firsts[index][at], seconds[index][at])
        for k in range(3):
            outs[k][index][at] = result[k]

    base = LAYERS * C_LAYER
    put(0, ..., sums[:, base + C_TOK[0] : base + C_TOK[1]])
    put(1, ..., sums[:, base + C_POS[0] : base + C_POS[0] + POS])
    put(6, ..., sums[:, base + C_HEAD[0] : base + C_HEAD[1]])
    turned[...] = jnp.transpose(sums[:, base + C_NORM[0] : base + C_NORM[1]])
    for i in range(NORMS):
        put(7, i, turned[2 * i : 2 * i + 2, :])
    for l in range(LAYERS):
        for index, cols in ((2, C_IN), (3, C_OUT), (4, C_UP), (5, C_DOWN)):
            put(index, l, sums[:, l * C_LAYER + cols[0] : l * C_LAYER + cols[1]])


def turned(tok, pos, w_in, w_out, w_up, w_down, head, norms):
    return (tok.T, pos.T, w_in, w_out, w_up, jnp.swapaxes(w_down, 1, 2), head, norms)


def on_device(geo, pixels, loss_mask, *weights):
    masters, firsts, seconds = (turned(*weights[k : k + 8]) for k in (0, 8, 16))
    n_rows, depth, blocks, res, group = geo.rows, geo.depth, geo.blocks, geo.res, geo.group
    m = geo.m
    vmem = pl.BlockSpec(memory_space=pltpu.VMEM)
    chunk = 4
    batch = 4
    n_groups = res // 8
    side = 8 * blocks
    sums, totals = pl.pallas_call(
        functools.partial(step_kernel, geo, chunk, batch),
        out_shape=(
            jax.ShapeDtypeStruct((n_rows, C_ALL), F32),
            jax.ShapeDtypeStruct((8, 128), F32),
        ),
        in_specs=[vmem] * 10,
        out_specs=(vmem,) * 2,
        scratch_shapes=[
            pltpu.VMEM((depth, 2, 2, 2 * geo.own, geo.wide), BF),
            pltpu.VMEM((depth, 2, 2, n_rows, C_REST), BF),
            pltpu.VMEM((LAYERS, depth, 2, 2, n_rows, C_LAYER), BF),
            pltpu.VMEM((depth, 2, 2, n_rows, C_REST), F32),
            pltpu.VMEM((2, depth, 2, 2, n_rows, C_LAYER), F32),
            pltpu.VMEM((LAYERS + 1, blocks, res, D), F32),
            pltpu.VMEM((LAYERS, blocks, res, D), F32),
            pltpu.VMEM((LAYERS, blocks, res, HEAD), BF),
            pltpu.VMEM((LAYERS, blocks + 1, group, res, 2 * HEAD), BF),
            pltpu.VMEM((LAYERS, n_groups, side, 3 * HEAD), BF),
            pltpu.VMEM((LAYERS, blocks, res, 2 * STRIDE), BF),
            pltpu.VMEM((LAYERS, n_groups, side, side), BF),
            pltpu.VMEM((LAYERS, blocks, res, D), BF),
            pltpu.VMEM((LAYERS, blocks, res, FF), BF),
            pltpu.VMEM((LAYERS, blocks, res, FF), BF),
            pltpu.VMEM((blocks, res, 3 * HEAD), F32),
            pltpu.VMEM((blocks, res, HEAD), F32),
            pltpu.VMEM((blocks, res, HEAD), BF),
            pltpu.VMEM((blocks, res, HEAD), BF),
            pltpu.VMEM((blocks + 1, res, 2 * HEAD), F32),
            pltpu.VMEM((group - 1, blocks + 1, res, 2 * HEAD), BF),
            pltpu.VMEM((2, group - 1, blocks, res, 2 * HEAD), BF),
            pltpu.VMEM((STRIDE, 2 * HEAD), F32),
            pltpu.VMEM((blocks, res, D), F32),
            pltpu.VMEM((res, 128), F32),
            pltpu.VMEM((res, 128), F32),
            pltpu.VMEM((res, 128), F32),
            pltpu.VMEM((8, 128), F32),
            pltpu.VMEM((geo.images, 2 * geo.own, 128), F32),
            pltpu.VMEM((2, res, 2 * STRIDE), F32),
            pltpu.VMEM((side, side), F32),
            pltpu.VMEM((16, 1, D), F32),
            pltpu.VMEM((2 * NORMS, 8, D), F32),
            pltpu.VMEM((128, D), F32),
            pltpu.VMEM((depth, 2, n_rows, C_ALL), BF),
            pltpu.VMEM((depth, 2, n_rows, C_ALL), BF),
            pltpu.VMEM((depth, n_rows, C_ALL), BF),
            pltpu.VMEM((depth, n_rows, C_ALL), BF),
            pltpu.VMEM((depth, n_rows, C_ALL), BF),
            pltpu.VMEM((depth - 1, n_rows, C_ALL), BF),
            pltpu.VMEM((m, n_rows, C_ALL), BF),
            pltpu.VMEM((m, 8, 128), F32),
            pltpu.VMEM((2, 8, 128), F32),
            pltpu.VMEM((2, 8, 128), F32),
            pltpu.VMEM((depth, 8, 128), F32),
            pltpu.SemaphoreType.DMA((4 + LAYERS, depth + 1)),
            pltpu.SemaphoreType.DMA((4 + LAYERS, depth + 1)),
            pltpu.SemaphoreType.DMA((group - 1,)),
            pltpu.SemaphoreType.DMA((2 * LAYERS, group - 1)),
            pltpu.SemaphoreType.DMA((5, depth + m)),
            pltpu.SemaphoreType.DMA((5, depth + m)),
            pltpu.SemaphoreType.DMA((m + depth,)),
            pltpu.SemaphoreType.DMA((m + depth,)),
        ],
        compiler_params=pltpu.CompilerParams(
            collective_id=0, has_side_effects=True, vmem_limit_bytes=VMEM_LIMIT
        ),
        name="step",
    )(jnp.swapaxes(pixels, 1, 2), jnp.swapaxes(loss_mask, 1, 2), *masters)

    shapes = [jax.ShapeDtypeStruct(item.shape, F32) for item in masters]
    outs = pl.pallas_call(
        functools.partial(update_kernel, n_rows),
        out_shape=shapes * 3,
        in_specs=[vmem] * 26,
        out_specs=[vmem] * 24,
        scratch_shapes=[pltpu.VMEM((128, n_rows), F32)],
        name="update",
    )(sums, totals, *masters, *firsts, *seconds)
    return (
        totals[0, 0],
        totals[1, 0],
        totals[2, 0],
        *turned(*outs[:8]),
        *turned(*outs[8:16]),
        *turned(*outs[16:]),
    )


def solution(mesh):
    pixels = P("img", None, "seq")
    weights = (
        P(None, "seq"),
        P(None, "seq"),
        P(None, "seq", None),
        P(None, "seq", None),
        P(None, "seq", None),
        P(None, None, "seq"),
        P("seq", None),
        P(None, None, "seq"),
    )

    def body(pixels, loss_mask, *rest):
        geo = Geometry(mesh.shape["seq"], mesh.shape["img"], pixels.shape[0], pixels.shape[1])
        return on_device(geo, pixels, loss_mask, *rest)

    return jax.shard_map(
        body,
        mesh=mesh,
        in_specs=(pixels, pixels) + weights * 3,
        out_specs=(P(), P(), P()) + weights * 3,
        check_vma=False,
    )
```

time: 302 us -> 172 us (0.57)
  Pallas kernels: 258 us -> 170 us
  local copies, waits for them, and re-layouts: 41.6 us -> 1.31 us
    pallas_call x3 -> x2, Pallas kernels: 258 us -> 170 us  [the longest x1 167 us: on_device(): pl.pallas_call(functools.partial(step_kernel, geo, chunk, batch), out_sha...]
    unnamed x18 -> x0, local copies, waits for them, and re-layouts: 26.2 us -> none
    pad x6 -> x0, local copies, waits for them, and re-layouts: 5.71 us -> none  [the longest x3 3.89 us: packed(): pos = jnp.pad(pos.T, ((0, 0), (0, 128 - POS)))]
    transpose x7 -> x0, local copies, waits for them, and re-layouts: 4.28 us -> none  [the longest x2 2.61 us: unpacked(): pos[:, :POS]]
    reshape x9 -> x0, local copies, waits for them, and re-layouts: 4.18 us -> none  [the longest x6 2.36 us: packed(): norms.reshape(2 * NORMS, rows)]
where the time goes in v2:
time: 172 us
  Pallas kernels  170 us (99%)
    pallas_call x1, Pallas kernels, on_device(): pl.pallas_call(functools.partial(step_kernel, geo, chunk, batch), out_sha...  167 us

profile of v2, /device:TPU:0, one launch (start us, length us, event | category | flops | bytes accessed | tf_op | source)
XLA Modules:
  0.0 172.0 jit_solution(1920222279376190379)
XLA Ops:
  0.7 167.1 %step.1 = (f32[16,6912]{1,0:T(8,128)}, f32[8,128]{1,0:T(8,128)}) custom-call(s32[8,8,24]{2,1,0:T(8,128)} %bitcast.31, s32[8,8,24]{2,1,0:T(8,128)} %bitcast.32, f32[16,256]{1,0:T(8,128)} %bitcast.27, f32[16,67]{1,0:T(8,128)} %bitcast.29, f32[3,16,768]{2,1,0:T(8,128)} %refs_4_.1, f32[3,16,256]{2,1,0:T(8,128)} %refs_5_.1, f32[3,16,512]{2,1,0:T(8,128)} %refs_6_.1, ...), custom_call_target="tpu_custom_call" | custom-call | tf_op jit(solution)/shard_map/step/pallas_call | solution.py:733
  167.7 2.9 %update.1 = (f32[16,256]{1,0:T(8,128)}, f32[16,67]{1,0:T(8,128)}, f32[3,16,768]{2,1,0:T(8,128)}, f32[3,16,256]{2,1,0:T(8,128)}, f32[3,16,512]{2,1,0:T(8,128)}, /...) custom-call(f32[16,6912]{1,0:T(8,128)} %get-tuple-element.54.refs_0_, ...), custom_call_target="tpu_custom_call" | custom-call | tf_op jit(solution)/shard_map/update/pallas_call | solution.py:803
  170.7 1.3 fusion

commit v3 on v2

--- a/solution.py
+++ b/solution.py
@@ -108,11 +108,10 @@
 
 def gelu_both(u):
     c = math.sqrt(2.0 / math.pi)
-    square = u * u
-    t = jnp.tanh(c * u * (1.0 + 0.044715 * square))
-    half = 0.5 * (1.0 + t)
-    slope = half + 0.5 * u * (1.0 - t * t) * (c * (1.0 + 3.0 * 0.044715 * square))
-    return u * half, slope
+    w = c + (0.044715 * c) * (u * u)
+    half = 0.5 + 0.5 * jnp.tanh(u * w)
+    a = u * half
+    return a, half + a * (1.0 - half) * (6.0 * w - 4.0 * c)
 
 
 def softmax(scores):
@@ -121,12 +120,12 @@
 
 
 def step_kernel(
-    geo, chunk, batch,
+    geo, chunk, batch, pack,
     pixels, mask, tok, pos, w_in, w_out, w_up, w_down, head, norms,
     sums, totals,
     px, rest, layers, g_rest, g_layers,
     x_s, x1_s, q0_s, kv_s, qkv1_s, p0_s, p1_s, o_s, a_s, slope_s, stage, o1_s, do0_s, dq0_s,
-    own_s, away_s, back_s, edge_s, dx_s, ids_s, tgt_s, msk_s, prev_s, pack_s, bias0, bias1, norm_s, gnorm, wide,
+    away_s, back_s, edge_s, ids_s, tgt_s, msk_s, prev_s, pack_s, bias0, bias1, norm_s, gnorm, wide,
     s1, r1, s2, r2, s3, r3, r4, st_img, st_core, st_y, st_z,
     g_send, g_recv, kv_send, kv_recv, rs_send, rs_recv, st_send, st_recv,
 ):
@@ -313,14 +312,20 @@
             stage[at, :, HEAD : 2 * HEAD] = qkv[..., 3 * HEAD : 4 * HEAD]
             stage[at, :, 2 * HEAD :] = qkv[..., 5 * HEAD :]
 
-        def strided(g):
-            at = pl.ds(pl.multiple_of(8 * g, 8), 8)
-            qkv = stage[:, at, :].reshape(8 * blocks, 3 * HEAD).astype(BF)
-            qkv1_s[l, g] = qkv
-            scores = dot_nt(qkv[:, :HEAD], qkv[:, HEAD : 2 * HEAD]) * SCALE + bias1[...]
-            probs = softmax(scores).astype(BF)
-            p1_s[l, g] = probs
-            o1_s[:, at, :] = dot(probs, qkv[:, 2 * HEAD :]).reshape(blocks, 8, HEAD)
+        def strided(i):
+            qkvs = []
+            for j in range(pack):
+                at = pl.ds(pl.multiple_of(8 * (i * pack + j), 8), 8)
+                qkv = stage[:, at, :].reshape(side, 3 * HEAD).astype(BF)
+                qkv1_s[l, i * pack + j] = qkv
+                qkvs.append(qkv)
+            raw = [dot_nt(qkv[:, :HEAD], qkv[:, HEAD : 2 * HEAD]) * SCALE + bias1[...] for qkv in qkvs]
+            probs = softmax(jnp.concatenate(raw, 0)).astype(BF)
+            p1_s[l, pl.ds(i * pack, pack)] = probs.reshape(pack, side, side)
+            for j in range(pack):
+                at = pl.ds(pl.multiple_of(8 * (i * pack + j), 8), 8)
+                value = dot(probs[j * side : (j + 1) * side], qkvs[j][:, 2 * HEAD :])
+                o1_s[:, at, :] = value.reshape(blocks, 8, HEAD)
 
         def window(i):
             b0 = i * batch
@@ -362,7 +367,7 @@
         if l == 1:
             to_core(5)
             to_core(6)
-        loop(n_groups, strided)
+        loop(n_groups // pack, strided)
         for copy in copies:
             copy.wait()
         loop(blocks // batch, window)
@@ -377,6 +382,8 @@
     for l in range(LAYERS):
         forward(l)
     arrived(5)
+
+    dx_s = x_s.at[LAYERS]
 
     def finish(i, loss):
         b0 = i * chunk
@@ -424,6 +431,7 @@
 
     def backward(l, after_feed, after_window, after_strided):
         grads = g_layers.at[l % 2]
+        own_s = x1_s.at[l]
 
         def feed(i):
             b0 = i * chunk
@@ -474,18 +482,20 @@
                 carry = dkv[STRIDE:]
             edge_s[...] = carry
 
-        def strided(g):
-            at = pl.ds(pl.multiple_of(8 * g, 8), 8)
-            qkv = qkv1_s[l, g]
-            probs = p1_s[l, g]
-            do = o1_s[:, at, :].reshape(8 * blocks, HEAD).astype(BF)
-            dp = dot_nt(do, qkv[:, 2 * HEAD :])
+        def strided(i):
+            probs = p1_s[l, pl.ds(i * pack, pack)].reshape(pack * side, side)
+            qkvs = [qkv1_s[l, i * pack + j] for j in range(pack)]
+            ats = [pl.ds(pl.multiple_of(8 * (i * pack + j), 8), 8) for j in range(pack)]
+            dos = [o1_s[:, at, :].reshape(side, HEAD).astype(BF) for at in ats]
+            dp = jnp.concatenate([dot_nt(do, qkv[:, 2 * HEAD :]) for do, qkv in zip(dos, qkvs)], 0)
             wide_p = probs.astype(F32)
             ds = (wide_p * (dp - jnp.sum(wide_p * dp, -1, keepdims=True)) * SCALE).astype(BF)
-            dq = dot(ds, qkv[:, HEAD : 2 * HEAD])
-            dk = dot_tn(ds, qkv[:, :HEAD])
-            dv = dot_tn(probs, do)
-            stage[:, at, :] = jnp.concatenate([dq, dk, dv], 1).reshape(blocks, 8, 3 * HEAD)
+            for j in range(pack):
+                cut = slice(j * side, (j + 1) * side)
+                dq = dot(ds[cut], qkvs[j][:, HEAD : 2 * HEAD])
+                dk = dot_tn(ds[cut], qkvs[j][:, :HEAD])
+                dv = dot_tn(probs[cut], dos[j])
+                stage[:, ats[j], :] = jnp.concatenate([dq, dk, dv], 1).reshape(blocks, 8, 3 * HEAD)
 
         def mix(i):
             b0 = i * chunk
@@ -527,7 +537,7 @@
         for copy in copies:
             copy.start()
         after_window()
-        loop(n_groups, strided)
+        loop(n_groups // pack, strided)
         after_strided()
         for copy in copies:
             copy.wait()
@@ -726,12 +736,13 @@
     n_rows, depth, blocks, res, group = geo.rows, geo.depth, geo.blocks, geo.res, geo.group
     m = geo.m
     vmem = pl.BlockSpec(memory_space=pltpu.VMEM)
-    chunk = 4
-    batch = 4
+    chunk = 12
+    batch = 12
+    pack = 4
     n_groups = res // 8
     side = 8 * blocks
     sums, totals = pl.pallas_call(
-        functools.partial(step_kernel, geo, chunk, batch),
+        functools.partial(step_kernel, geo, chunk, batch, pack),
         out_shape=(
             jax.ShapeDtypeStruct((n_rows, C_ALL), F32),
             jax.ShapeDtypeStruct((8, 128), F32),
@@ -745,7 +756,7 @@
             pltpu.VMEM((depth, 2, 2, n_rows, C_REST), F32),
             pltpu.VMEM((2, depth, 2, 2, n_rows, C_LAYER), F32),
             pltpu.VMEM((LAYERS + 1, blocks, res, D), F32),
-            pltpu.VMEM((LAYERS, blocks, res, D), F32),
+            pltpu.VMEM((LAYERS, blocks + 1, res, D), F32),
             pltpu.VMEM((LAYERS, blocks, res, HEAD), BF),
             pltpu.VMEM((LAYERS, blocks + 1, group, res, 2 * HEAD), BF),
             pltpu.VMEM((LAYERS, n_groups, side, 3 * HEAD), BF),
@@ -758,11 +769,9 @@
             pltpu.VMEM((blocks, res, HEAD), F32),
             pltpu.VMEM((blocks, res, HEAD), BF),
             pltpu.VMEM((blocks, res, HEAD), BF),
-            pltpu.VMEM((blocks + 1, res, 2 * HEAD), F32),
             pltpu.VMEM((group - 1, blocks + 1, res, 2 * HEAD), BF),
             pltpu.VMEM((2, group - 1, blocks, res, 2 * HEAD), BF),
             pltpu.VMEM((STRIDE, 2 * HEAD), F32),
-            pltpu.VMEM((blocks, res, D), F32),
             pltpu.VMEM((res, 128), F32),
             pltpu.VMEM((res, 128), F32),
             pltpu.VMEM((res, 128), F32),

time: 172 us -> 142 us (0.83)
  Pallas kernels: 170 us -> 139 us
    pallas_call x1, Pallas kernels: 167 us -> 136 us  [on_device(): pl.pallas_call(functools.partial(step_kernel, geo, chunk, batch, pack), o...]
where the time goes in v3:
time: 142 us; the launch traced here: 141 us
  Pallas kernels  139 us (98%)
    pallas_call x1, Pallas kernels, on_device(): pl.pallas_call(functools.partial(step_kernel, geo, chunk, batch, pack), o...  136 us
    pallas_call x1, Pallas kernels, on_device(): pl.pallas_call(functools.partial(update_kernel, n_rows), out_shape=shapes...  2.95 us

profile of v3, /device:TPU:0, one launch (start us, length us, event | category | flops | bytes accessed | tf_op | source)
XLA Modules:
  0.0 141.3 jit_solution(5037426664364369147)
XLA Ops:
  0.7 136.4 %step.1 = (f32[16,6912]{1,0:T(8,128)}, f32[8,128]{1,0:T(8,128)}) custom-call(s32[8,8,24]{2,1,0:T(8,128)} %bitcast.31, s32[8,8,24]{2,1,0:T(8,128)} %bitcast.32, f32[16,256]{1,0:T(8,128)} %bitcast.27, f32[16,67]{1,0:T(8,128)} %bitcast.29, f32[3,16,768]{2,1,0:T(8,128)} %refs_4_.1, f32[3,16,256]{2,1,0:T(8,128)} %refs_5_.1, f32[3,16,512]{2,1,0:T(8,128)} %refs_6_.1, ...), custom_call_target="tpu_custom_call" | custom-call | tf_op jit(solution)/shard_map/step/pallas_call | solution.py:744
  137.1 2.9 %update.1 = (f32[16,256]{1,0:T(8,128)}, f32[16,67]{1,0:T(8,128)}, f32[3,16,768]{2,1,0:T(8,128)}, f32[3,16,256]{2,1,0:T(8,128)}, f32[3,16,512]{2,1,0:T(8,128)}, /...) custom-call(f32[16,6912]{1,0:T(8,128)} %get-tuple-element.54.refs_0_, ...), custom_call_target="tpu_custom_call" | custom-call | tf_op jit(solution)/shard_map/update/pallas_call | solution.py:812
  140.0 1.3 fusion

commit v4 on v3

--- a/solution.py
+++ b/solution.py
@@ -30,8 +30,8 @@
 
 C_IN, C_OUT, C_UP, C_DOWN = (0, 768), (768, 1024), (1024, 1536), (1536, 2048)
 C_LAYER = 2048
-C_TOK, C_POS, C_NORM, C_HEAD = (0, 256), (256, 384), (384, 512), (512, 768)
-C_REST = 768
+C_TOK, C_POS, C_HEAD = (0, 256), (256, 384), (384, 640)
+C_REST = 640
 C_ALL = LAYERS * C_LAYER + C_REST
 
 BF = jnp.bfloat16
@@ -74,7 +74,10 @@
     barrier = pltpu.get_barrier_semaphore()
     for device in devices:
         pl.semaphore_signal(barrier, inc=1, device_id=device, device_id_type=pl.DeviceIdType.MESH)
-    pl.semaphore_wait(barrier, len(devices))
+
+
+def greeted(devices):
+    pl.semaphore_wait(pltpu.get_barrier_semaphore(), len(devices))
 
 
 def push(src, dst, send_sem, recv_sem, device):
@@ -125,8 +128,8 @@
     sums, totals,
     px, rest, layers, g_rest, g_layers,
     x_s, x1_s, q0_s, kv_s, qkv1_s, p0_s, p1_s, o_s, a_s, slope_s, stage, o1_s, do0_s, dq0_s,
-    away_s, back_s, edge_s, ids_s, tgt_s, msk_s, prev_s, pack_s, bias0, bias1, norm_s, gnorm, wide,
-    s1, r1, s2, r2, s3, r3, r4, st_img, st_core, st_y, st_z,
+    away_s, back_s, edge_s, ids_s, tgt_s, msk_s, prev_s, pack_s, bias0, bias1, norm_s, gnorm, wide, squares,
+    s1, r1, r2, r4, st_img, st_core, st_plane,
     g_send, g_recv, kv_send, kv_recv, rs_send, rs_recv, st_send, st_recv,
 ):
     z, y, core = geo.place()
@@ -136,26 +139,19 @@
     siblings = [{"seq": image * group + lax.rem(part + k, group)} for k in range(1, group)]
     peers = [seq_id(lax.rem(z + k, depth), y, core) for k in range(1, depth)]
     beside, sibling = seq_id(z, 1 - y, core), seq_id(z, y, 1 - core)
+    columns = 2 * depth
+    column = z * 2 + y
+    plane = [lax.rem(column + k, columns) for k in range(1, columns)]
     across = [{"img": lax.rem(x_img + k, m)} for k in range(1, m)]
+    others = [seq_id(q // 2, q % 2, core) for q in plane] + across + [sibling]
+    if group > 2:
+        others.append(seq_id(z, 1 - y, 1 - core))
+    greet(others)
     rows = chunk * res
     chunks = blocks // chunk
     n_groups = res // 8
     every, pair = pl.ds(0, depth), pl.ds(0, 2)
 
-    rest[z, y, core, :, C_TOK[0] : C_TOK[1]] = tok[...].astype(BF)
-    wide[...] = jnp.zeros_like(wide)
-    wide[: geo.rows, :POS] = pos[...]
-    rest[z, y, core, :, C_POS[0] : C_POS[1]] = wide[: geo.rows, :128].astype(BF)
-    wide[...] = jnp.zeros_like(wide)
-    for i in range(NORMS):
-        wide[2 * i : 2 * i + 2, : geo.rows] = norms[i]
-    rest[z, y, core, :, C_NORM[0] : C_NORM[1]] = jnp.transpose(wide[:, :128])[: geo.rows].astype(BF)
-    rest[z, y, core, :, C_HEAD[0] : C_HEAD[1]] = head[...].astype(BF)
-    for l in range(LAYERS):
-        layers[l, z, y, core, :, C_IN[0] : C_IN[1]] = w_in[l].astype(BF)
-        layers[l, z, y, core, :, C_OUT[0] : C_OUT[1]] = w_out[l].astype(BF)
-        layers[l, z, y, core, :, C_UP[0] : C_UP[1]] = w_up[l].astype(BF)
-        layers[l, z, y, core, :, C_DOWN[0] : C_DOWN[1]] = w_down[l].astype(BF)
     pack_s[...] = jnp.zeros_like(pack_s)
     pack_s[:, :own, :blocks] = pixels[...].astype(F32)
     pack_s[:, own:, :blocks] = mask[...].astype(F32)
@@ -166,15 +162,19 @@
         spot = ((to == at + i * blocks) & (at < blocks)).astype(F32).astype(BF)
         packed = packed + dot(pack_s[i].astype(BF), spot)
     px[z, y, core] = packed.astype(BF)
-
-    others = peers + [beside] + across
-    others = others + (siblings if group > 2 else [sibling])
-    if group > 2:
-        others = [d for d in others if d is not beside]
-    greet(others)
-
-    parts = [px, rest.at[..., 0 : C_NORM[1]], layers.at[0, ..., 0 : C_IN[1]], layers.at[0, ..., C_OUT[0] : C_LAYER]]
-    parts += [layers.at[1], rest.at[..., C_HEAD[0] : C_HEAD[1]], layers.at[2]]
+    rest[z, y, core, :, C_TOK[0] : C_TOK[1]] = tok[...].astype(BF)
+    wide[...] = jnp.zeros_like(wide)
+    for i in range(NORMS):
+        wide[POS + 2 * i : POS + 2 * i + 2, : geo.rows] = norms[i]
+    flipped = jnp.transpose(wide[:, :128])[: geo.rows]
+    wide[: geo.rows, :128] = flipped
+    wide[: geo.rows, :POS] = pos[...]
+    rest[z, y, core, :, C_POS[0] : C_POS[1]] = wide[: geo.rows, :128].astype(BF)
+
+    parts = [px, rest.at[..., 0 : C_POS[1]]]
+    for l in range(LAYERS):
+        parts += [layers.at[l, ..., 0 : C_IN[1]], layers.at[l, ..., C_OUT[0] : C_LAYER]]
+    parts += [rest.at[..., C_HEAD[0] : C_HEAD[1]]]
 
     def gather_z(a, k):
         mine = parts[a].at[z, y, core]
@@ -200,9 +200,22 @@
     def arrived(a):
         gather_core(a).wait_recv()
 
-    for a in range(len(parts)):
+    def to_z(a):
         for k in range(depth - 1):
             gather_z(a, k).start()
+
+    greeted(others)
+    to_z(0)
+    to_z(1)
+    for l in range(LAYERS):
+        layers[l, z, y, core, :, C_IN[0] : C_IN[1]] = w_in[l].astype(BF)
+        to_z(2 + 2 * l)
+        layers[l, z, y, core, :, C_OUT[0] : C_OUT[1]] = w_out[l].astype(BF)
+        layers[l, z, y, core, :, C_UP[0] : C_UP[1]] = w_up[l].astype(BF)
+        layers[l, z, y, core, :, C_DOWN[0] : C_DOWN[1]] = w_down[l].astype(BF)
+        to_z(3 + 2 * l)
+    rest[z, y, core, :, C_HEAD[0] : C_HEAD[1]] = head[...].astype(BF)
+    to_z(8)
 
     def table(ref, cols):
         piece = ref[..., cols[0] : cols[1]]
@@ -239,8 +252,6 @@
     to_y(2)
     to_core(0)
     to_core(1)
-    to_y(3)
-    to_core(2)
     arrived(0)
 
     span = depth // group
@@ -259,7 +270,11 @@
     ids_s[1:res, :] = tgt_s[0 : res - 1, :]
 
     arrived(1)
-    norm_s[...] = jnp.transpose(table(rest, C_NORM).astype(F32))[:16].reshape(16, 1, D)
+    wide[...] = jnp.transpose(table(rest, C_POS).astype(F32))
+    for i in range(2 * NORMS):
+        norm_s[i] = wide[POS + i : POS + i + 1, :]
+    wide[...] = jnp.zeros_like(wide)
+    to_y(3)
 
     def spread(ref, b0):
         values = ref[...].astype(BF)
@@ -282,8 +297,14 @@
         hits = (lane == line) | (lane == SIDE + third - SIDE * line)
         return (hits | (lane == 2 * SIDE + p - 3.0 * third)).astype(F32)
 
-    def loop(count, body):
-        lax.fori_loop(0, count, lambda i, carry: (body(i), carry)[1], 0)
+    def loop(count, body, between=()):
+        def inner(i, carry):
+            if between:
+                pl.when(i == count - 1)(lambda: [step() for step in between] and None)
+            body(i)
+            return carry
+
+        lax.fori_loop(0, count, inner, 0)
 
     def embed(i):
         b0 = i * chunk
@@ -292,6 +313,8 @@
         x_s[0, pl.ds(b0, chunk)] = x.reshape(chunk, res, D)
 
     loop(chunks, embed)
+    to_core(2)
+    to_y(4)
 
     def exchange(l, k):
         mine = kv_s.at[l, pl.ds(1, blocks), 0]
@@ -356,32 +379,37 @@
             x2 = x1 + dot_nt(a, layer_table(l, C_DOWN))
             x_s[l + 1, at] = x2.reshape(chunk, res, D)
 
-        arrived((2, 4, 6)[l])
+        arrived(2 + 2 * l)
         loop(chunks, mix)
         copies = [exchange(l, k) for k in range(group - 1)]
         for copy in copies:
             copy.start()
+        if l == 1:
+            to_core(5)
+            to_y(7)
+        loop(n_groups // pack, strided)
         if l == 0:
             to_core(3)
-            to_y(4)
+            to_y(5)
         if l == 1:
-            to_core(5)
             to_core(6)
-        loop(n_groups // pack, strided)
+        if l == 2:
+            to_core(8)
         for copy in copies:
             copy.wait()
         loop(blocks // batch, window)
         if l == 0:
-            arrived(3)
-            to_y(5)
-        loop(chunks, feed)
-        if l == 0:
             to_core(4)
-            to_y(6)
+        if l == 1:
+            to_y(8)
+        arrived(3 + 2 * l)
+        loop(chunks, feed, [lambda: to_y(6)] if l == 0 else [])
+        if l == 1:
+            to_core(7)
 
     for l in range(LAYERS):
         forward(l)
-    arrived(5)
+    arrived(8)
 
     dx_s = x_s.at[LAYERS]
 
@@ -429,7 +457,7 @@
             away_s.at[k, pl.ds(1, blocks)], back_s.at[l % 2, k], kv_send.at[k], kv_recv.at[LAYERS + l, k], siblings[k]
         )
 
-    def backward(l, after_feed, after_window, after_strided):
+    def backward(l, points):
         grads = g_layers.at[l % 2]
         own_s = x1_s.at[l]
 
@@ -497,14 +525,13 @@
                 dv = dot_tn(probs[cut], dos[j])
                 stage[:, ats[j], :] = jnp.concatenate([dq, dk, dv], 1).reshape(blocks, 8, 3 * HEAD)
 
-        def mix(i):
-            b0 = i * chunk
-            at = pl.ds(b0, chunk)
-            dkv = own_s[pl.ds(b0 + 1, chunk)]
+        def mixed(i):
+            at = pl.ds(i * chunk, chunk)
+            dkv = own_s[pl.ds(i * chunk + 1, chunk)]
             for k in range(group - 1):
                 dkv = dkv + back_s[l % 2, k, at].astype(F32)
             d1 = stage[at]
-            dqkv = jnp.concatenate(
+            return jnp.concatenate(
                 [
                     dq0_s[at],
                     d1[..., :HEAD].astype(BF),
@@ -515,18 +542,36 @@
                 ],
                 -1,
             ).reshape(rows, 6 * HEAD)
-            unit, rstd = normalise(x_s[l, at].reshape(rows, D))
-            gain = norm_s[4 * l]
-            h = (unit * (1.0 + gain) + norm_s[4 * l + 1]).astype(BF)
+
+        def mix_grad(i, dqkv=None, unit=None):
+            dqkv = mixed(i) if dqkv is None else dqkv
+            if unit is None:
+                unit, _ = normalise(x_s[l, pl.ds(i * chunk, chunk)].reshape(rows, D))
+            h = (unit * (1.0 + norm_s[4 * l]) + norm_s[4 * l + 1]).astype(BF)
             add_to(grads, C_IN, dot_tn(h, dqkv))
+
+        def mix_state(i, dqkv=None, both=None):
+            at = pl.ds(i * chunk, chunk)
+            dqkv = mixed(i) if dqkv is None else dqkv
+            unit, rstd = normalise(x_s[l, at].reshape(rows, D)) if both is None else both
             dh = dot_nt(dqkv, layer_table(l, C_IN))
-            dx, g_gain, g_bias = normalise_back(dh, unit, rstd, gain)
+            dx, g_gain, g_bias = normalise_back(dh, unit, rstd, norm_s[4 * l])
             gnorm[4 * l] += g_gain
             gnorm[4 * l + 1] += g_bias
             dx_s[at] += dx.reshape(chunk, res, D)
 
-        loop(chunks, feed)
-        after_feed()
+        def mix(i):
+            dqkv = mixed(i)
+            both = normalise(x_s[l, pl.ds(i * chunk, chunk)].reshape(rows, D))
+            mix_grad(i, dqkv, both[0])
+            mix_state(i, dqkv, both)
+
+        def take(point):
+            for step in points.get(point, ()):
+                step()
+
+        loop(chunks, feed, points.get("feed", ()))
+        take("window")
         edge_s[...] = jnp.zeros_like(edge_s)
         loop(blocks // batch, window)
         last = edge_s[...].reshape(group, res, 2 * HEAD)
@@ -536,147 +581,174 @@
         copies = [give(l, k) for k in range(group - 1)]
         for copy in copies:
             copy.start()
-        after_window()
+        take("strided")
         loop(n_groups // pack, strided)
-        after_strided()
         for copy in copies:
             copy.wait()
-        loop(chunks, mix)
-
-    def section(index, ref, cols, base):
-        width = cols[1] - cols[0]
-        cut = slice(base, base + width)
+        take("mix")
+        if l > 0:
+            loop(chunks, mix)
+            take("end")
+        else:
+            loop(chunks, mix_grad)
+            take("end")
+            loop(chunks, mix_state)
+
+    def section(index, ref, cols, base, at_once=False):
+        cut = slice(base + cols[0], base + cols[1])
         grad = ref.at[..., cols[0] : cols[1]]
-        first = push(s1.at[..., cut], r1.at[..., cut], rs_send.at[index, 0], rs_recv.at[index, 0], sibling)
-        second = push(s2.at[..., cut], r2.at[..., cut], rs_send.at[index, 1], rs_recv.at[index, 1], beside)
-        third = [
-            push(
-                s3.at[lax.rem(z + k, depth), :, cut],
-                r3.at[k - 1, :, cut],
-                rs_send.at[index, 1 + k],
-                rs_recv.at[index, 1 + k],
-                peers[k - 1],
-            )
-            for k in range(1, depth)
-        ]
-        fourth = [
-            push(
-                r4.at[x_img, :, cut],
-                r4.at[x_img, :, cut],
-                rs_send.at[index, depth + 1 + k],
-                rs_recv.at[index, depth + 1 + k],
-                across[k],
-            )
-            for k in range(m - 1)
+
+        def way(k, src, dst, device):
+            return push(src, dst, rs_send.at[index, k], rs_recv.at[index, k], device)
+
+        one = way(0, s1.at[..., cut], r1.at[..., cut], sibling)
+        if at_once:
+            direct = [
+                way(1 + k, s1.at[q // 2, q % 2, :, cut], r2.at[k, :, cut], seq_id(q // 2, q % 2, core))
+                for k, q in enumerate(plane)
+            ]
+        else:
+            two = way(1, s1.at[every, 0, :, cut], r2.at[every, :, cut], beside)
+            three = [
+                way(1 + k, s1.at[lax.rem(z + k, depth), 1, :, cut], r2.at[depth + k - 1, :, cut], peers[k - 1])
+                for k in range(1, depth)
+            ]
+        last = [
+            way(columns + k, r4.at[x_img, :, cut], r4.at[x_img, :, cut], across[k]) for k in range(m - 1)
         ]
 
         def go_core():
             s1[..., cut] = grad[every, pair, 1 - core].astype(BF)
-            first.start()
+            one.start()
 
         def go_y():
-            first.wait()
+            one.wait()
             total = grad[every, 1 - y, core] + r1[every, 1 - y, :, cut].astype(F32)
-            s2[..., cut] = total.astype(BF)
-            second.start()
+            s1[every, 0, :, cut] = total.astype(BF)
+            two.start()
 
         def go_z():
-            second.wait()
-            total = grad[every, y, core] + r1[every, y, :, cut].astype(F32) + r2[..., cut].astype(F32)
-            s3[..., cut] = total.astype(BF)
-            for copy in third:
+            two.wait()
+            total = grad[every, y, core] + r1[every, y, :, cut].astype(F32) + r2[every, :, cut].astype(F32)
+            s1[every, 1, :, cut] = total.astype(BF)
+            for copy in three:
                 copy.start()
 
+        def go_plane():
+            one.wait()
+            total = grad[every, pair, core] + r1[..., cut].astype(F32)
+            s1[..., cut] = total.astype(BF)
+            for copy in direct:
+                copy.start()
+
+        def to_img(copies, mine, first):
+            for copy in copies:
+                copy.wait()
+            total = mine.astype(F32)
+            for k in range(len(copies)):
+                total = total + r2[first + k, :, cut].astype(F32)
+            r4[x_img, :, cut] = total.astype(BF)
+            for copy in last:
+                copy.start()
+
         def go_img():
-            for copy in third:
-                copy.wait()
-            total = s3[z, :, cut].astype(F32)
-            for k in range(1, depth):
-                total = total + r3[k - 1, :, cut].astype(F32)
-            r4[x_img, :, cut] = total.astype(BF)
-            for copy in fourth:
-                copy.start()
+            to_img(three, s1[z, 1, :, cut], depth)
+
+        def from_plane():
+            to_img(direct, s1[z, y, :, cut], 0)
 
         def end():
-            for copy in fourth:
+            for copy in last:
                 copy.wait()
             total = r4[0, :, cut].astype(F32)
             for k in range(1, m):
                 total = total + r4[k, :, cut].astype(F32)
             sums[:, cut] = total
-            return jnp.sum(jnp.sum(total * total, 0, keepdims=True), 1, keepdims=True)
-
-        return go_core, go_y, go_z, go_img, end
-
-    two = section(0, g_layers.at[0], (0, C_LAYER), 2 * C_LAYER)
-    one = section(1, g_layers.at[1], (0, C_LAYER), C_LAYER)
-    zero_rest = section(2, g_layers.at[0], (C_OUT[0], C_LAYER), C_OUT[0])
-    zero_in = section(3, g_layers.at[0], C_IN, 0)
-    other = section(4, g_rest, (0, C_REST), LAYERS * C_LAYER)
-
-    def run(*steps):
-        def inner():
-            for step in steps:
-                step()
-
-        return inner
-
-    nothing = run()
-    backward(2, nothing, nothing, nothing)
-    two[0]()
-    backward(1, two[1], two[2], two[3])
-    squares = two[4]()
-    one[0]()
+            square = jnp.sum(jnp.sum(total * total, 0, keepdims=True), 1, keepdims=True)
+            squares[...] += jnp.broadcast_to(square, squares.shape)
+
+        return (go_core, go_plane, from_plane, end) if at_once else (go_core, go_y, go_z, go_img, end)
+
+    def of_layer(l):
+        grads, base = g_layers.at[l % 2], l * C_LAYER
+        return section(2 * l, grads, (C_OUT[0], C_LAYER), base), section(2 * l + 1, grads, C_IN, base, l == 0)
+
+    (feed_two, mix_two), (feed_one, mix_one), (feed_zero, mix_zero) = (of_layer(l) for l in (2, 1, 0))
+    head_sum = section(6, g_rest, C_HEAD, LAYERS * C_LAYER)
+    first_sum = section(7, g_rest, (C_TOK[0], C_POS[1]), LAYERS * C_LAYER, True)
+
+    squares[...] = jnp.zeros_like(squares)
+    head_sum[0]()
+    backward(
+        2,
+        {
+            "window": [head_sum[1], feed_two[0]],
+            "strided": [feed_two[1]],
+            "mix": [head_sum[2]],
+            "end": [mix_two[0]],
+        },
+    )
+    backward(
+        1,
+        {
+            "feed": [mix_two[1]],
+            "window": [feed_two[2], feed_one[0]],
+            "strided": [head_sum[3], feed_one[1]],
+            "mix": [mix_two[2]],
+            "end": [feed_two[3], head_sum[4], mix_one[0]],
+        },
+    )
     g_layers[0] = jnp.zeros(g_layers.shape[1:], F32)
-    backward(0, run(zero_rest[0], one[1]), run(zero_rest[1], one[2]), run(zero_rest[2], one[3]))
-    zero_in[0]()
-    zero_rest[3]()
-    squares = squares + one[4]()
+    backward(
+        0,
+        {
+            "feed": [mix_one[1]],
+            "window": [feed_one[2], feed_zero[0], mix_two[3]],
+            "strided": [feed_zero[1], feed_two[4]],
+            "mix": [mix_one[2]],
+            "end": [mix_zero[0], mix_two[4]],
+        },
+    )
+    mix_zero[1]()
 
     def embed_back(i):
         b0 = i * chunk
         hot = jnp.concatenate([one_hot(ids_s, b0), place_hot(b0)], 1).astype(BF)
         dx = dx_s[pl.ds(b0, chunk)].reshape(rows, D)
-        high = dx.astype(BF)
-        low = (dx - high.astype(F32)).astype(BF)
-        add_to(g_rest, (C_TOK[0], C_POS[1]), dot_tn(high, hot) + dot_tn(low, hot))
+        add_to(g_rest, (C_TOK[0], C_POS[1]), dot_tn(dx.astype(BF), hot))
 
     loop(chunks, embed_back)
     for i in range(2 * NORMS):
-        wide[i : i + 1, :] = jnp.sum(gnorm[i], 0, keepdims=True)
-    add_to(g_rest, C_NORM, jnp.transpose(wide[...]))
-    other[0]()
-    zero_in[1]()
-    other[1]()
-    zero_in[2]()
-    other[2]()
-    squares = squares + zero_rest[4]()
-    zero_in[3]()
-    other[3]()
-    squares = squares + zero_in[4]()
-    squares = squares + other[4]()
+        wide[POS + i : POS + i + 1, :] = jnp.sum(gnorm[i], 0, keepdims=True)
+    add_to(g_rest, C_POS, jnp.transpose(wide[...]))
+    first_sum[0]()
+    feed_zero[2]()
+    first_sum[1]()
+    feed_one[3]()
+    mix_one[3]()
+    mix_zero[2]()
+    feed_zero[3]()
+    first_sum[2]()
+    for part_sum in (feed_one, mix_one, mix_zero, feed_zero, first_sum):
+        part_sum[-1]()
 
     for copy in st_across:
         copy.wait()
     told = st_img[0]
     for k in range(1, m):
         told = told + st_img[k]
-    told = jnp.where(line == 2, squares, told)
+    told = jnp.where(line == 2, squares[...], told)
+    st_plane[column] = told
     base = m - 1
-
-    def swap(told, buffer, index, where, device):
-        buffer[where] = told
-        copy = push(buffer.at[where], buffer.at[where], st_send.at[base + index], st_recv.at[base + index], device)
-        copy.start()
-        copy.wait()
-        return buffer[0] + buffer[1]
-
-    told = swap(told, st_core, 0, core, sibling)
-    told = swap(told, st_y, 1, y, beside)
-    st_z[z] = told
     copies = [
-        push(st_z.at[z], st_z.at[z], st_send.at[base + 1 + k], st_recv.at[base + 1 + k], peers[k - 1])
-        for k in range(1, depth)
+        push(
+            st_plane.at[column],
+            st_plane.at[column],
+            st_send.at[base + k],
+            st_recv.at[base + k],
+            seq_id(q // 2, q % 2, core),
+        )
+        for k, q in enumerate(plane)
     ]
     for copy in copies:
         copy.start()
@@ -687,9 +759,16 @@
         gather_core(a).wait_send()
     for copy in copies:
         copy.wait()
-    told = st_z[0]
-    for k in range(1, depth):
-        told = told + st_z[k]
+    told = st_plane[0]
+    for k in range(1, columns):
+        told = told + st_plane[k]
+    st_core[core] = told
+    copy = push(
+        st_core.at[core], st_core.at[core], st_send.at[base + columns], st_recv.at[base + columns], sibling
+    )
+    copy.start()
+    copy.wait()
+    told = st_core[0] + st_core[1]
     count = told[1:2, :1]
     norm = jnp.sqrt(told[2:3, :1]) / count
     factor = jnp.minimum(1.0, CLIP_NORM / norm) / count
@@ -719,9 +798,9 @@
     put(0, ..., sums[:, base + C_TOK[0] : base + C_TOK[1]])
     put(1, ..., sums[:, base + C_POS[0] : base + C_POS[0] + POS])
     put(6, ..., sums[:, base + C_HEAD[0] : base + C_HEAD[1]])
-    turned[...] = jnp.transpose(sums[:, base + C_NORM[0] : base + C_NORM[1]])
+    turned[...] = jnp.transpose(sums[:, base + C_POS[0] : base + C_POS[1]])
     for i in range(NORMS):
-        put(7, i, turned[2 * i : 2 * i + 2, :])
+        put(7, i, turned[POS + 2 * i : POS + 2 * i + 2, :])
     for l in range(LAYERS):
         for index, cols in ((2, C_IN), (3, C_OUT), (4, C_UP), (5, C_DOWN)):
             put(index, l, sums[:, l * C_LAYER + cols[0] : l * C_LAYER + cols[1]])
@@ -782,25 +861,22 @@
             pltpu.VMEM((16, 1, D), F32),
             pltpu.VMEM((2 * NORMS, 8, D), F32),
             pltpu.VMEM((128, D), F32),
+            pltpu.VMEM((8, 128), F32),
             pltpu.VMEM((depth, 2, n_rows, C_ALL), BF),
             pltpu.VMEM((depth, 2, n_rows, C_ALL), BF),
-            pltpu.VMEM((depth, n_rows, C_ALL), BF),
-            pltpu.VMEM((depth, n_rows, C_ALL), BF),
-            pltpu.VMEM((depth, n_rows, C_ALL), BF),
-            pltpu.VMEM((depth - 1, n_rows, C_ALL), BF),
+            pltpu.VMEM((2 * depth - 1, n_rows, C_ALL), BF),
             pltpu.VMEM((m, n_rows, C_ALL), BF),
             pltpu.VMEM((m, 8, 128), F32),
             pltpu.VMEM((2, 8, 128), F32),
-            pltpu.VMEM((2, 8, 128), F32),
-            pltpu.VMEM((depth, 8, 128), F32),
-            pltpu.SemaphoreType.DMA((4 + LAYERS, depth + 1)),
-            pltpu.SemaphoreType.DMA((4 + LAYERS, depth + 1)),
+            pltpu.VMEM((2 * depth, 8, 128), F32),
+            pltpu.SemaphoreType.DMA((3 + 2 * LAYERS, depth + 1)),
+            pltpu.SemaphoreType.DMA((3 + 2 * LAYERS, depth + 1)),
             pltpu.SemaphoreType.DMA((group - 1,)),
             pltpu.SemaphoreType.DMA((2 * LAYERS, group - 1)),
-            pltpu.SemaphoreType.DMA((5, depth + m)),
-            pltpu.SemaphoreType.DMA((5, depth + m)),
-            pltpu.SemaphoreType.DMA((m + depth,)),
-            pltpu.SemaphoreType.DMA((m + depth,)),
+            pltpu.SemaphoreType.DMA((2 * LAYERS + 2, 2 * depth + m)),
+            pltpu.SemaphoreType.DMA((2 * LAYERS + 2, 2 * depth + m)),
+            pltpu.SemaphoreType.DMA((2 * depth + m,)),
+            pltpu.SemaphoreType.DMA((2 * depth + m,)),
         ],
         compiler_params=pltpu.CompilerParams(
             collective_id=0, has_side_effects=True, vmem_limit_bytes=VMEM_LIMIT

time: 142 us -> 114 us (0.80)
  Pallas kernels: 139 us -> 112 us
    pallas_call x1, Pallas kernels: 136 us -> 109 us  [on_device(): pl.pallas_call(functools.partial(step_kernel, geo, chunk, batch, pack), o...]
where the time goes in v4:
time: 114 us
  Pallas kernels  112 us (98%)
  local copies, waits for them, and re-layouts  1.31 us (1%)
    pallas_call x1, Pallas kernels, on_device(): pl.pallas_call(functools.partial(step_kernel, geo, chunk, batch, pack), o...  109 us
    pallas_call x1, Pallas kernels, on_device(): pl.pallas_call(functools.partial(update_kernel, n_rows), out_shape=shapes...  2.95 us

profile of v4, /device:TPU:0, one launch (start us, length us, event | category | flops | bytes accessed | tf_op | source)
XLA Modules:
  0.0 114.1 jit_solution(6732294441264879737)
XLA Ops:
  0.7 109.1 %step.1 = (f32[16,6784]{1,0:T(8,128)}, f32[8,128]{1,0:T(8,128)}) custom-call(s32[8,8,24]{2,1,0:T(8,128)} %bitcast.31, s32[8,8,24]{2,1,0:T(8,128)} %bitcast.32, f32[16,256]{1,0:T(8,128)} %bitcast.27, f32[16,67]{1,0:T(8,128)} %bitcast.29, f32[3,16,768]{2,1,0:T(8,128)} %refs_4_.1, f32[3,16,256]{2,1,0:T(8,128)} %refs_5_.1, f32[3,16,512]{2,1,0:T(8,128)} %refs_6_.1, ...), custom_call_target="tpu_custom_call" | custom-call | tf_op jit(solution)/shard_map/step/pallas_call | solution.py:823
  109.8 2.9 %update.1 = (f32[16,256]{1,0:T(8,128)}, f32[16,67]{1,0:T(8,128)}, f32[3,16,768]{2,1,0:T(8,128)}, f32[3,16,256]{2,1,0:T(8,128)}, f32[3,16,512]{2,1,0:T(8,128)}, /...) custom-call(f32[16,6784]{1,0:T(8,128)} %get-tuple-element.54.refs_0_, ...), custom_call_target="tpu_custom_call" | custom-call | tf_op jit(solution)/shard_map/update/pallas_call | solution.py:888
  112.8 1.3 %fusion = (f32[1,1]{1,0:T(1,128)}, f32[1,1]{1,0:T(1,128)}, f32[1,1]{1,0:T(1,128)}) fusion(f32[8,128]{1,0:T(8,128)} %get-tuple-element.53.refs_1_), kind=kLoop, calls=%fused_computation | loop fusion | bytes 24 | tf_op jit(solution)/shard_map/slice | solution.py:899

commit v5 on v4

--- a/solution.py
+++ b/solution.py
@@ -111,10 +111,10 @@
 
 def gelu_both(u):
     c = math.sqrt(2.0 / math.pi)
-    w = c + (0.044715 * c) * (u * u)
-    half = 0.5 + 0.5 * jnp.tanh(u * w)
+    square = u * u
+    half = 0.5 + 0.5 * jnp.tanh(u * (c + (0.044715 * c) * square))
     a = u * half
-    return a, half + a * (1.0 - half) * (6.0 * w - 4.0 * c)
+    return a, half + a * (1.0 - half) * (2.0 * c + (6.0 * 0.044715 * c) * square)
 
 
 def softmax(scores):
@@ -127,7 +127,7 @@
     pixels, mask, tok, pos, w_in, w_out, w_up, w_down, head, norms,
     sums, totals,
     px, rest, layers, g_rest, g_layers,
-    x_s, x1_s, q0_s, kv_s, qkv1_s, p0_s, p1_s, o_s, a_s, slope_s, stage, o1_s, do0_s, dq0_s,
+    x_s, unit_s, rstd_s, own_s, q0_s, kv_s, qkv1_s, p0_s, p1_s, o_s, a_s, slope_s, stage, o1_s, do0_s, dq0_s,
     away_s, back_s, edge_s, ids_s, tgt_s, msk_s, prev_s, pack_s, bias0, bias1, norm_s, gnorm, wide, squares,
     s1, r1, r2, r4, st_img, st_core, st_plane,
     g_send, g_recv, kv_send, kv_recv, rs_send, rs_recv, st_send, st_recv,
@@ -304,17 +304,32 @@
             body(i)
             return carry
 
-        lax.fori_loop(0, count, inner, 0)
+        if count == 1:
+            inner(0, None)
+        else:
+            lax.fori_loop(0, count, inner, 0)
 
     def embed(i):
         b0 = i * chunk
         hot = jnp.concatenate([one_hot(ids_s, b0), place_hot(b0)], 1).astype(BF)
         x = dot_nt(hot, table(rest, (C_TOK[0], C_POS[1])))
-        x_s[0, pl.ds(b0, chunk)] = x.reshape(chunk, res, D)
+        x_s[pl.ds(b0, chunk)] = x.reshape(chunk, res, D)
 
     loop(chunks, embed)
     to_core(2)
     to_y(4)
+
+    def keep(k, at, x):
+        unit, rstd = normalise(x)
+        unit = unit.astype(BF)
+        unit_s[k, at] = unit.reshape(x.shape[0] // res, res, D)
+        rstd_s[at, :, k : k + 1] = rstd.reshape(x.shape[0] // res, res, 1)
+        return (unit.astype(F32) * (1.0 + norm_s[2 * k]) + norm_s[2 * k + 1]).astype(BF)
+
+    def kept(k, at):
+        unit = unit_s[k, at].reshape(rows, D).astype(F32)
+        h = (unit * (1.0 + norm_s[2 * k]) + norm_s[2 * k + 1]).astype(BF)
+        return h, unit, rstd_s[at, :, k : k + 1].reshape(rows, 1)
 
     def exchange(l, k):
         mine = kv_s.at[l, pl.ds(1, blocks), 0]
@@ -325,8 +340,7 @@
         def mix(i):
             b0 = i * chunk
             at = pl.ds(b0, chunk)
-            unit, _ = normalise(x_s[l, at].reshape(rows, D))
-            h = (unit * (1.0 + norm_s[4 * l]) + norm_s[4 * l + 1]).astype(BF)
+            h = keep(2 * l, at, x_s[at].reshape(rows, D))
             qkv = dot(h, layer_table(l, C_IN)).reshape(chunk, res, 6 * HEAD)
             q0_s[l, at] = qkv[..., :HEAD].astype(BF)
             kv_s[l, pl.ds(b0 + 1, chunk), 0, :, :HEAD] = qkv[..., 2 * HEAD : 3 * HEAD].astype(BF)
@@ -368,16 +382,13 @@
             b0 = i * chunk
             at = pl.ds(b0, chunk)
             o_s[l, at, :, HEAD:] = o1_s[at].astype(BF)
-            x1 = x_s[l, at].reshape(rows, D) + dot(o_s[l, at].reshape(rows, D), layer_table(l, C_OUT))
-            x1_s[l, at] = x1.reshape(chunk, res, D)
-            unit, _ = normalise(x1)
-            h = (unit * (1.0 + norm_s[4 * l + 2]) + norm_s[4 * l + 3]).astype(BF)
-            a, slope = gelu_both(dot(h, layer_table(l, C_UP)))
-            a = a.astype(BF)
+            x1 = x_s[at].reshape(rows, D) + dot(o_s[l, at].reshape(rows, D), layer_table(l, C_OUT))
+            h = keep(2 * l + 1, at, x1)
+            a, slope = gelu_both(dot(h, layer_table(l, C_UP)).astype(BF))
             a_s[l, at] = a.reshape(chunk, res, FF)
-            slope_s[l, at] = slope.astype(BF).reshape(chunk, res, FF)
+            slope_s[l, at] = slope.reshape(chunk, res, FF)
             x2 = x1 + dot_nt(a, layer_table(l, C_DOWN))
-            x_s[l + 1, at] = x2.reshape(chunk, res, D)
+            x_s[at] = x2.reshape(chunk, res, D)
 
         arrived(2 + 2 * l)
         loop(chunks, mix)
@@ -411,12 +422,12 @@
         forward(l)
     arrived(8)
 
-    dx_s = x_s.at[LAYERS]
+    dx_s = x_s
 
     def finish(i, loss):
         b0 = i * chunk
         at = pl.ds(b0, chunk)
-        unit, rstd = normalise(x_s[LAYERS, at].reshape(rows, D))
+        unit, rstd = normalise(x_s[at].reshape(rows, D))
         gain = norm_s[4 * LAYERS]
         h = (unit * (1.0 + gain) + norm_s[4 * LAYERS + 1]).astype(BF)
         table_head = table(rest, C_HEAD)
@@ -426,14 +437,11 @@
         e = jnp.exp(shift)
         total = jnp.sum(e, -1, keepdims=True)
         weight = spread(msk_s, b0)
-        per = (
-            jnp.log(total)
-            - (1.0 - SMOOTHING) * jnp.sum(hot * shift, -1, keepdims=True)
-            - SMOOTHING * jnp.mean(shift, -1, keepdims=True)
-        )
+        goal = (1.0 - SMOOTHING) * hot + SMOOTHING / V
+        per = jnp.log(total) - jnp.sum(goal * shift, -1, keepdims=True)
         loss = loss + jnp.sum(weight[:, :1] * per, 0, keepdims=True)
         weight = jnp.concatenate([weight, weight], 1)
-        d_logits = weight * (e * (1.0 / total) - (1.0 - SMOOTHING) * hot - SMOOTHING / V)
+        d_logits = weight * (e * (1.0 / total) - goal)
         d_logits = d_logits.astype(BF)
         add_to(g_rest, C_HEAD, dot_tn(h, d_logits))
         dx, g_gain, g_bias = normalise_back(dot_nt(d_logits, table_head), unit, rstd, gain)
@@ -459,7 +467,6 @@
 
     def backward(l, points):
         grads = g_layers.at[l % 2]
-        own_s = x1_s.at[l]
 
         def feed(i):
             b0 = i * chunk
@@ -468,14 +475,11 @@
             g2 = dx2.astype(BF)
             a = a_s[l, at].reshape(rows, FF)
             add_to(grads, C_DOWN, dot_tn(g2, a))
-            du = slope_s[l, at].reshape(rows, FF).astype(F32) * dot(g2, layer_table(l, C_DOWN))
-            du = du.astype(BF)
-            unit, rstd = normalise(x1_s[l, at].reshape(rows, D))
-            gain = norm_s[4 * l + 2]
-            h = (unit * (1.0 + gain) + norm_s[4 * l + 3]).astype(BF)
+            du = slope_s[l, at].reshape(rows, FF) * dot(g2, layer_table(l, C_DOWN)).astype(BF)
+            h, unit, rstd = kept(2 * l + 1, at)
             add_to(grads, C_UP, dot_tn(h, du))
             dh = dot_nt(du, layer_table(l, C_UP))
-            dx, g_gain, g_bias = normalise_back(dh, unit, rstd, gain)
+            dx, g_gain, g_bias = normalise_back(dh, unit, rstd, norm_s[4 * l + 2])
             gnorm[4 * l + 2] += g_gain
             gnorm[4 * l + 3] += g_bias
             dx = dx + dx2
@@ -543,17 +547,16 @@
                 -1,
             ).reshape(rows, 6 * HEAD)
 
-        def mix_grad(i, dqkv=None, unit=None):
+        def mix_grad(i, dqkv=None, h=None):
             dqkv = mixed(i) if dqkv is None else dqkv
-            if unit is None:
-                unit, _ = normalise(x_s[l, pl.ds(i * chunk, chunk)].reshape(rows, D))
-            h = (unit * (1.0 + norm_s[4 * l]) + norm_s[4 * l + 1]).astype(BF)
+            if h is None:
+                h, _, _ = kept(2 * l, pl.ds(i * chunk, chunk))
             add_to(grads, C_IN, dot_tn(h, dqkv))
 
         def mix_state(i, dqkv=None, both=None):
             at = pl.ds(i * chunk, chunk)
             dqkv = mixed(i) if dqkv is None else dqkv
-            unit, rstd = normalise(x_s[l, at].reshape(rows, D)) if both is None else both
+            unit, rstd = kept(2 * l, at)[1:] if both is None else both
             dh = dot_nt(dqkv, layer_table(l, C_IN))
             dx, g_gain, g_bias = normalise_back(dh, unit, rstd, norm_s[4 * l])
             gnorm[4 * l] += g_gain
@@ -562,9 +565,9 @@
 
         def mix(i):
             dqkv = mixed(i)
-            both = normalise(x_s[l, pl.ds(i * chunk, chunk)].reshape(rows, D))
-            mix_grad(i, dqkv, both[0])
-            mix_state(i, dqkv, both)
+            h, unit, rstd = kept(2 * l, pl.ds(i * chunk, chunk))
+            mix_grad(i, dqkv, h)
+            mix_state(i, dqkv, (unit, rstd))
 
         def take(point):
             for step in points.get(point, ()):
@@ -786,8 +789,10 @@
     sums, totals = refs[:2]
     masters, firsts, seconds = refs[2:10], refs[10:18], refs[18:26]
     outs = (refs[26:34], refs[34:42], refs[42:50])
-    turned = refs[50]
+    scalars, turned = refs[50:53], refs[53]
     factor = totals[3:4, :1]
+    for k in range(3):
+        scalars[k][0, 0] = totals[k, 0]
 
     def put(index, at, gradient):
         result = adam(masters[index][at], gradient * factor, firsts[index][at], seconds[index][at])
@@ -816,7 +821,7 @@
     m = geo.m
     vmem = pl.BlockSpec(memory_space=pltpu.VMEM)
     chunk = 12
-    batch = 12
+    batch = 24
     pack = 4
     n_groups = res // 8
     side = 8 * blocks
@@ -834,8 +839,10 @@
             pltpu.VMEM((LAYERS, depth, 2, 2, n_rows, C_LAYER), BF),
             pltpu.VMEM((depth, 2, 2, n_rows, C_REST), F32),
             pltpu.VMEM((2, depth, 2, 2, n_rows, C_LAYER), F32),
-            pltpu.VMEM((LAYERS + 1, blocks, res, D), F32),
-            pltpu.VMEM((LAYERS, blocks + 1, res, D), F32),
+            pltpu.VMEM((blocks, res, D), F32),
+            pltpu.VMEM((2 * LAYERS, blocks, res, D), BF),
+            pltpu.VMEM((blocks, res, 128), F32),
+            pltpu.VMEM((blocks + 1, res, 2 * HEAD), F32),
             pltpu.VMEM((LAYERS, blocks, res, HEAD), BF),
             pltpu.VMEM((LAYERS, blocks + 1, group, res, 2 * HEAD), BF),
             pltpu.VMEM((LAYERS, n_groups, side, 3 * HEAD), BF),
@@ -887,19 +894,17 @@
     shapes = [jax.ShapeDtypeStruct(item.shape, F32) for item in masters]
     outs = pl.pallas_call(
         functools.partial(update_kernel, n_rows),
-        out_shape=shapes * 3,
+        out_shape=shapes * 3 + [jax.ShapeDtypeStruct((1, 1), F32)] * 3,
         in_specs=[vmem] * 26,
-        out_specs=[vmem] * 24,
+        out_specs=[vmem] * 24 + [pl.BlockSpec(memory_space=pltpu.SMEM)] * 3,
         scratch_shapes=[pltpu.VMEM((128, n_rows), F32)],
         name="update",
     )(sums, totals, *masters, *firsts, *seconds)
     return (
-        totals[0, 0],
-        totals[1, 0],
-        totals[2, 0],
+        *(item.reshape(()) for item in outs[24:]),
         *turned(*outs[:8]),
         *turned(*outs[8:16]),
-        *turned(*outs[16:]),
+        *turned(*outs[16:24]),
     )
 
 

time: 114 us -> 106 us (0.930)
  Pallas kernels: 112 us -> 105 us
  local copies, waits for them, and re-layouts: 1.31 us -> 0 us
    pallas_call x1, Pallas kernels: 109 us -> 102 us  [on_device(): pl.pallas_call(functools.partial(step_kernel, geo, chunk, batch, pack), o...]
    slice x1 -> x0, local copies, waits for them, and re-layouts: 1.31 us -> none  [on_device(): totals[2, 0]]
where the time goes in v5:
time: 106 us
  Pallas kernels  105 us (99%)
    pallas_call x1, Pallas kernels, on_device(): pl.pallas_call(functools.partial(step_kernel, geo, chunk, batch, pack), o...  102 us
    pallas_call x1, Pallas kernels, on_device(): pl.pallas_call(functools.partial(update_kernel, n_rows), out_shape=shapes...  2.96 us

profile of v5, /device:TPU:0, one launch (start us, length us, event | category | flops | bytes accessed | tf_op | source)
XLA Modules:
  0.0 106.2 jit_solution(2212959573931694942)
XLA Ops:
  0.7 102.4 %step.1 = (f32[16,6784]{1,0:T(8,128)}, f32[8,128]{1,0:T(8,128)}) custom-call(s32[8,8,24]{2,1,0:T(8,128)} %bitcast.31, s32[8,8,24]{2,1,0:T(8,128)} %bitcast.32, f32[16,256]{1,0:T(8,128)} %bitcast.27, f32[16,67]{1,0:T(8,128)} %bitcast.29, f32[3,16,768]{2,1,0:T(8,128)} %refs_4_.1, f32[3,16,256]{2,1,0:T(8,128)} %refs_5_.1, f32[3,16,512]{2,1,0:T(8,128)} %refs_6_.1, ...), custom_call_target="tpu_custom_call" | custom-call | tf_op jit(solution)/shard_map/step/pallas_call | solution.py:828
  103.0 3.0 %update.1 = (f32[16,256]{1,0:T(8,128)}, f32[16,67]{1,0:T(8,128)}, f32[3,16,768]{2,1,0:T(8,128)}, f32[3,16,256]{2,1,0:T(8,128)}, f32[3,16,512]{2,1,0:T(8,128)}, /...) custom-call(f32[16,6784]{1,0:T(8,128)} %get-tuple-element.56.refs_0_, ...), custom_call_target="tpu_custom_call" | custom-call | tf_op jit(solution)/shard_map/update/pallas_call | solution.py:895

commit v6 on v5

--- a/solution.py
+++ b/solution.py
@@ -129,8 +129,8 @@
     px, rest, layers, g_rest, g_layers,
     x_s, unit_s, rstd_s, own_s, q0_s, kv_s, qkv1_s, p0_s, p1_s, o_s, a_s, slope_s, stage, o1_s, do0_s, dq0_s,
     away_s, back_s, edge_s, ids_s, tgt_s, msk_s, prev_s, pack_s, bias0, bias1, norm_s, gnorm, wide, squares,
-    s1, r1, r2, r4, st_img, st_core, st_plane,
-    g_send, g_recv, kv_send, kv_recv, rs_send, rs_recv, st_send, st_recv,
+    s1, r1, r2, r4, r_cross, r_first, st_core, st_all,
+    g_send, g_recv, kv_send, kv_recv, rs_send, rs_recv, c_send, c_recv, cb_send, cb_recv, f_send, f_recv, b_send, b_recv, st_send, st_recv,
 ):
     z, y, core = geo.place()
     me, x_img = lax.axis_index("seq"), lax.axis_index("img")
@@ -143,7 +143,8 @@
     column = z * 2 + y
     plane = [lax.rem(column + k, columns) for k in range(1, columns)]
     across = [{"img": lax.rem(x_img + k, m)} for k in range(1, m)]
-    others = [seq_id(q // 2, q % 2, core) for q in plane] + across + [sibling]
+    off_plane = [{**seq_id(q // 2, q % 2, core), "img": lax.rem(x_img + k, m)} for k in range(1, m) for q in plane]
+    others = [seq_id(q // 2, q % 2, core) for q in plane] + across + [sibling] + off_plane
     if group > 2:
         others.append(seq_id(z, 1 - y, 1 - core))
     greet(others)
@@ -453,12 +454,7 @@
     loss = lax.fori_loop(0, chunks, finish, jnp.zeros((1, 1), F32))
     count = jnp.sum(jnp.sum(msk_s[...], 0, keepdims=True), 1, keepdims=True)
     line = lax.broadcasted_iota(jnp.int32, (8, 128), 0)
-    st_img[x_img] = jnp.where(line == 0, loss, jnp.where(line == 1, count, 0.0))
-    st_across = [
-        push(st_img.at[x_img], st_img.at[x_img], st_send.at[k], st_recv.at[k], across[k]) for k in range(m - 1)
-    ]
-    for copy in st_across:
-        copy.start()
+    told = jnp.where(line == 0, loss, jnp.where(line == 1, count, 0.0))
 
     def give(l, k):
         return push(
@@ -474,12 +470,12 @@
             dx2 = dx_s[at].reshape(rows, D)
             g2 = dx2.astype(BF)
             a = a_s[l, at].reshape(rows, FF)
-            add_to(grads, C_DOWN, dot_tn(g2, a))
             du = slope_s[l, at].reshape(rows, FF) * dot(g2, layer_table(l, C_DOWN)).astype(BF)
             h, unit, rstd = kept(2 * l + 1, at)
+            dh = dot_nt(du, layer_table(l, C_UP))
+            add_to(grads, C_DOWN, dot_tn(g2, a))
+            dx, g_gain, g_bias = normalise_back(dh, unit, rstd, norm_s[4 * l + 2])
             add_to(grads, C_UP, dot_tn(h, du))
-            dh = dot_nt(du, layer_table(l, C_UP))
-            dx, g_gain, g_bias = normalise_back(dh, unit, rstd, norm_s[4 * l + 2])
             gnorm[4 * l + 2] += g_gain
             gnorm[4 * l + 3] += g_bias
             dx = dx + dx2
@@ -605,20 +601,18 @@
             return push(src, dst, rs_send.at[index, k], rs_recv.at[index, k], device)
 
         one = way(0, s1.at[..., cut], r1.at[..., cut], sibling)
-        if at_once:
-            direct = [
-                way(1 + k, s1.at[q // 2, q % 2, :, cut], r2.at[k, :, cut], seq_id(q // 2, q % 2, core))
-                for k, q in enumerate(plane)
-            ]
-        else:
-            two = way(1, s1.at[every, 0, :, cut], r2.at[every, :, cut], beside)
-            three = [
-                way(1 + k, s1.at[lax.rem(z + k, depth), 1, :, cut], r2.at[depth + k - 1, :, cut], peers[k - 1])
-                for k in range(1, depth)
-            ]
-        last = [
-            way(columns + k, r4.at[x_img, :, cut], r4.at[x_img, :, cut], across[k]) for k in range(m - 1)
-        ]
+        def two():
+            return way(1, s1.at[every, 0, :, cut], r2.at[every, :, cut], beside)
+
+        def three(k):
+            return way(1 + k, s1.at[lax.rem(z + k, depth), 1, :, cut], r2.at[depth + k - 1, :, cut], peers[k - 1])
+
+        def direct(k):
+            q = plane[k - 1]
+            return way(k, s1.at[q // 2, q % 2, :, cut], r2.at[k - 1, :, cut], seq_id(q // 2, q % 2, core))
+
+        def last(k):
+            return way(columns + k - 1, r4.at[x_img, :, cut], r4.at[x_img, :, cut], across[k - 1])
 
         def go_core():
             s1[..., cut] = grad[every, pair, 1 - core].astype(BF)
@@ -628,41 +622,42 @@
             one.wait()
             total = grad[every, 1 - y, core] + r1[every, 1 - y, :, cut].astype(F32)
             s1[every, 0, :, cut] = total.astype(BF)
-            two.start()
+            two().start()
 
         def go_z():
-            two.wait()
+            two().wait()
             total = grad[every, y, core] + r1[every, y, :, cut].astype(F32) + r2[every, :, cut].astype(F32)
             s1[every, 1, :, cut] = total.astype(BF)
-            for copy in three:
-                copy.start()
-
-        def go_plane():
+            for k in range(1, depth):
+                three(k).start()
+
+        def go_plane(start=True):
             one.wait()
             total = grad[every, pair, core] + r1[..., cut].astype(F32)
             s1[..., cut] = total.astype(BF)
-            for copy in direct:
-                copy.start()
-
-        def to_img(copies, mine, first):
-            for copy in copies:
-                copy.wait()
+            if start:
+                for k in range(1, columns):
+                    direct(k).start()
+
+        def to_img(copy, number, mine, first):
+            for k in range(1, number):
+                copy(k).wait()
             total = mine.astype(F32)
-            for k in range(len(copies)):
-                total = total + r2[first + k, :, cut].astype(F32)
+            for k in range(1, number):
+                total = total + r2[first + k - 1, :, cut].astype(F32)
             r4[x_img, :, cut] = total.astype(BF)
-            for copy in last:
-                copy.start()
+            for k in range(1, m):
+                last(k).start()
 
         def go_img():
-            to_img(three, s1[z, 1, :, cut], depth)
+            to_img(three, depth, s1[z, 1, :, cut], depth)
 
         def from_plane():
-            to_img(direct, s1[z, y, :, cut], 0)
+            to_img(direct, columns, s1[z, y, :, cut], 0)
 
         def end():
-            for copy in last:
-                copy.wait()
+            for k in range(1, m):
+                last(k).wait()
             total = r4[0, :, cut].astype(F32)
             for k in range(1, m):
                 total = total + r4[k, :, cut].astype(F32)
@@ -672,13 +667,170 @@
 
         return (go_core, go_plane, from_plane, end) if at_once else (go_core, go_y, go_z, go_img, end)
 
+    def crossed(index, ref, cols, base):
+        tiles = (cols[1] - cols[0]) // 128
+        cut = slice(base + cols[0], base + cols[1])
+        grad = ref.at[..., cols[0] : cols[1]]
+        ends = [128 * (tiles * p // m) for p in range(m + 1)]
+        shares = [slice(cut.start + ends[p], cut.start + ends[p + 1]) for p in range(m)]
+        widths = [ends[p + 1] - ends[p] for p in range(m)]
+        one = push(s1.at[..., cut], r1.at[..., cut], rs_send.at[index, 0], rs_recv.at[index, 0], sibling)
+
+        def over(p, group_at):
+            there = r_cross.at[group_at, every, pair, :, 0 : widths[p]]
+            return push(s1.at[..., shares[p]], there, c_send.at[p], c_recv.at[group_at], {"img": p})
+
+        def direct(p, k):
+            q = plane[k - 1]
+            return push(
+                s1.at[q // 2, q % 2, :, shares[p]],
+                r2.at[k - 1, :, shares[p]],
+                rs_send.at[index, k],
+                rs_recv.at[index, k],
+                seq_id(q // 2, q % 2, core),
+            )
+
+        def share(p, k):
+            there = sums.at[:, shares[p]]
+            return push(there, there, cb_send.at[k], cb_recv.at[p], across[k])
+
+        def mine(p, step):
+            if widths[p]:
+                pl.when(x_img == p)(step)
+
+        def not_mine(p, step):
+            if widths[p]:
+                pl.when(x_img != p)(step)
+
+        def go_core():
+            s1[..., cut] = grad[every, pair, 1 - core].astype(BF)
+            one.start()
+
+        def go_img():
+            one.wait()
+            total = grad[every, pair, core] + r1[..., cut].astype(F32)
+            s1[..., cut] = total.astype(BF)
+            for p in range(m):
+                not_mine(p, lambda: over(p, x_img).start())
+
+        def go_plane():
+            for p in range(m):
+
+                def step():
+                    total = s1[..., shares[p]].astype(F32)
+                    for group_at in range(m):
+                        if group_at != p:
+                            over(p, group_at).wait_recv()
+                            total = total + r_cross[group_at, ..., 0 : widths[p]].astype(F32)
+                    s1[..., shares[p]] = total.astype(BF)
+                    for k in range(1, columns):
+                        direct(p, k).start()
+
+                mine(p, step)
+
+        def end():
+            for p in range(m):
+
+                def step():
+                    total = s1[z, y, :, shares[p]].astype(F32)
+                    for k in range(1, columns):
+                        direct(p, k).wait()
+                        total = total + r2[k - 1, :, shares[p]].astype(F32)
+                    sums[:, shares[p]] = total
+                    for k in range(m - 1):
+                        share(p, k).start()
+                    square = jnp.sum(jnp.sum(total * total, 0, keepdims=True), 1, keepdims=True)
+                    squares[...] += jnp.broadcast_to(square, squares.shape)
+
+                mine(p, step)
+
+        def drain():
+            for p in range(m):
+
+                def sent():
+                    over(p, x_img).wait_send()
+                    share(p, 0).wait_recv()
+
+                def shared():
+                    for k in range(m - 1):
+                        share(p, k).wait_send()
+
+                not_mine(p, sent)
+                mine(p, shared)
+
+        return go_core, go_img, go_plane, end, drain
+
     def of_layer(l):
         grads, base = g_layers.at[l % 2], l * C_LAYER
-        return section(2 * l, grads, (C_OUT[0], C_LAYER), base), section(2 * l + 1, grads, C_IN, base, l == 0)
+        kind = crossed if l == 0 else section
+        return kind(2 * l, grads, (C_OUT[0], C_LAYER), base), section(2 * l + 1, grads, C_IN, base, l == 0)
 
     (feed_two, mix_two), (feed_one, mix_one), (feed_zero, mix_zero) = (of_layer(l) for l in (2, 1, 0))
     head_sum = section(6, g_rest, C_HEAD, LAYERS * C_LAYER)
     first_sum = section(7, g_rest, (C_TOK[0], C_POS[1]), LAYERS * C_LAYER, True)
+
+    first_base = LAYERS * C_LAYER
+    first_cuts = [slice(first_base + 128 * b, first_base + 128 * (b + 1)) for b in range(C_POS[1] // 128)]
+
+    def first_send(b, k):
+        own_place = k == columns - 1
+        q = column if own_place else plane[k]
+        device = {"img": b % m} if own_place else {**seq_id(q // 2, q % 2, core), "img": b % m}
+        here = s1.at[q // 2, q % 2, :, first_cuts[b]]
+        there = r_first.at[x_img, k, :, 128 * b : 128 * (b + 1)]
+        return push(here, there, f_send.at[b, k], f_recv.at[b, x_img, k], device)
+
+    def first_came(b, group_at, k):
+        there = r_first.at[group_at, k, :, 128 * b : 128 * (b + 1)]
+        return push(there, there, f_send.at[b, k], f_recv.at[b, group_at, k], sibling)
+
+    def first_share(b, k):
+        there = sums.at[:, first_cuts[b]]
+        return push(there, there, b_send.at[b, k], b_recv.at[b], across[k])
+
+    def first_start():
+        first_sum[1](start=False)
+        for b in range(len(first_cuts)):
+            for k in range(columns - 1):
+                first_send(b, k).start()
+
+            @pl.when(x_img != b % m)
+            def _():
+                first_send(b, columns - 1).start()
+
+    def first_end():
+        for b in range(len(first_cuts)):
+
+            @pl.when(x_img == b % m)
+            def _():
+                total = s1[z, y, :, first_cuts[b]].astype(F32)
+                for group_at in range(m):
+                    for k in range(columns - 1):
+                        first_came(b, group_at, k).wait_recv()
+                        total = total + r_first[group_at, k, :, 128 * b : 128 * (b + 1)].astype(F32)
+                    if group_at != b % m:
+                        first_came(b, group_at, columns - 1).wait_recv()
+                        total = total + r_first[group_at, columns - 1, :, 128 * b : 128 * (b + 1)].astype(F32)
+                sums[:, first_cuts[b]] = total
+                for k in range(m - 1):
+                    first_share(b, k).start()
+                square = jnp.sum(jnp.sum(total * total, 0, keepdims=True), 1, keepdims=True)
+                squares[...] += jnp.broadcast_to(square, squares.shape)
+
+    def first_drain():
+        for b in range(len(first_cuts)):
+            for k in range(columns - 1):
+                first_send(b, k).wait_send()
+
+            @pl.when(x_img != b % m)
+            def _():
+                first_send(b, columns - 1).wait_send()
+                first_share(b, 0).wait_recv()
+
+            @pl.when(x_img == b % m)
+            def _():
+                for k in range(m - 1):
+                    first_share(b, k).wait_send()
 
     squares[...] = jnp.zeros_like(squares)
     head_sum[0]()
@@ -725,34 +877,27 @@
         wide[POS + i : POS + i + 1, :] = jnp.sum(gnorm[i], 0, keepdims=True)
     add_to(g_rest, C_POS, jnp.transpose(wide[...]))
     first_sum[0]()
+    first_start()
     feed_zero[2]()
-    first_sum[1]()
     feed_one[3]()
     mix_one[3]()
     mix_zero[2]()
+    for part_sum in (feed_one, mix_one, mix_zero):
+        part_sum[-1]()
+    squares[...] = jnp.where(x_img == 0, squares[...], 0.0)
+    first_end()
     feed_zero[3]()
-    first_sum[2]()
-    for part_sum in (feed_one, mix_one, mix_zero, feed_zero, first_sum):
-        part_sum[-1]()
-
-    for copy in st_across:
-        copy.wait()
-    told = st_img[0]
-    for k in range(1, m):
-        told = told + st_img[k]
+
     told = jnp.where(line == 2, squares[...], told)
-    st_plane[column] = told
-    base = m - 1
-    copies = [
-        push(
-            st_plane.at[column],
-            st_plane.at[column],
-            st_send.at[base + k],
-            st_recv.at[base + k],
-            seq_id(q // 2, q % 2, core),
-        )
-        for k, q in enumerate(plane)
-    ]
+    st_all[x_img, column] = told
+    mine = st_all.at[x_img, column]
+    plane_places = [(x_img, q) for q in plane]
+    plane_places += [(lax.rem(x_img + k, m), lax.rem(column + j, columns)) for k in range(1, m) for j in range(columns)]
+    copies = []
+    for k, (group_at, q) in enumerate(plane_places, 1):
+        spot = (k // columns, k % columns)
+        device = {**seq_id(q // 2, q % 2, core), "img": group_at}
+        copies.append(push(mine, mine, st_send.at[spot], st_recv.at[spot], device))
     for copy in copies:
         copy.start()
     for a in range(len(parts)):
@@ -762,14 +907,15 @@
         gather_core(a).wait_send()
     for copy in copies:
         copy.wait()
-    told = st_plane[0]
-    for k in range(1, columns):
-        told = told + st_plane[k]
+    told = jnp.zeros((8, 128), F32)
+    for group_at in range(m):
+        for q in range(columns):
+            told = told + st_all[group_at, q]
     st_core[core] = told
-    copy = push(
-        st_core.at[core], st_core.at[core], st_send.at[base + columns], st_recv.at[base + columns], sibling
-    )
+    copy = push(st_core.at[core], st_core.at[core], st_send.at[0, 0], st_recv.at[0, 0], sibling)
     copy.start()
+    first_drain()
+    feed_zero[4]()
     copy.wait()
     told = st_core[0] + st_core[1]
     count = told[1:2, :1]
@@ -873,17 +1019,26 @@
             pltpu.VMEM((depth, 2, n_rows, C_ALL), BF),
             pltpu.VMEM((2 * depth - 1, n_rows, C_ALL), BF),
             pltpu.VMEM((m, n_rows, C_ALL), BF),
-            pltpu.VMEM((m, 8, 128), F32),
+            pltpu.VMEM((m, depth, 2, n_rows, 128 * -(-(C_LAYER - C_OUT[0]) // 128 // m)), BF),
+            pltpu.VMEM((m, 2 * depth, n_rows, C_POS[1]), BF),
             pltpu.VMEM((2, 8, 128), F32),
-            pltpu.VMEM((2 * depth, 8, 128), F32),
+            pltpu.VMEM((m, 2 * depth, 8, 128), F32),
             pltpu.SemaphoreType.DMA((3 + 2 * LAYERS, depth + 1)),
             pltpu.SemaphoreType.DMA((3 + 2 * LAYERS, depth + 1)),
             pltpu.SemaphoreType.DMA((group - 1,)),
             pltpu.SemaphoreType.DMA((2 * LAYERS, group - 1)),
             pltpu.SemaphoreType.DMA((2 * LAYERS + 2, 2 * depth + m)),
             pltpu.SemaphoreType.DMA((2 * LAYERS + 2, 2 * depth + m)),
-            pltpu.SemaphoreType.DMA((2 * depth + m,)),
-            pltpu.SemaphoreType.DMA((2 * depth + m,)),
+            pltpu.SemaphoreType.DMA((m,)),
+            pltpu.SemaphoreType.DMA((m,)),
+            pltpu.SemaphoreType.DMA((m,)),
+            pltpu.SemaphoreType.DMA((m,)),
+            pltpu.SemaphoreType.DMA((C_POS[1] // 128, 2 * depth)),
+            pltpu.SemaphoreType.DMA((C_POS[1] // 128, m, 2 * depth)),
+            pltpu.SemaphoreType.DMA((C_POS[1] // 128, m)),
+            pltpu.SemaphoreType.DMA((C_POS[1] // 128,)),
+            pltpu.SemaphoreType.DMA((m, 2 * depth)),
+            pltpu.SemaphoreType.DMA((m, 2 * depth)),
         ],
         compiler_params=pltpu.CompilerParams(
             collective_id=0, has_side_effects=True, vmem_limit_bytes=VMEM_LIMIT

time: 106 us -> 103 us (0.972)
  Pallas kernels: 105 us -> 102 us
    pallas_call x1, Pallas kernels: 102 us -> 98.7 us  [on_device(): pl.pallas_call(functools.partial(step_kernel, geo, chunk, batch, pack), o...]
where the time goes in v6:
time: 103 us
  Pallas kernels  102 us (99%)
    pallas_call x1, Pallas kernels, on_device(): pl.pallas_call(functools.partial(step_kernel, geo, chunk, batch, pack), o...  98.7 us
    pallas_call x1, Pallas kernels, on_device(): pl.pallas_call(functools.partial(update_kernel, n_rows), out_shape=shapes...  2.96 us

profile of v6, /device:TPU:0, one launch (start us, length us, event | category | flops | bytes accessed | tf_op | source)
XLA Modules:
  0.0 102.5 jit_solution(3133284075350599827)
XLA Ops:
  0.7 98.7 %step.1 = (f32[16,6784]{1,0:T(8,128)}, f32[8,128]{1,0:T(8,128)}) custom-call(s32[8,8,24]{2,1,0:T(8,128)} %bitcast.31, s32[8,8,24]{2,1,0:T(8,128)} %bitcast.32, f32[16,256]{1,0:T(8,128)} %bitcast.27, f32[16,67]{1,0:T(8,128)} %bitcast.29, f32[3,16,768]{2,1,0:T(8,128)} %refs_4_.1, f32[3,16,256]{2,1,0:T(8,128)} %refs_5_.1, f32[3,16,512]{2,1,0:T(8,128)} %refs_6_.1, ...), custom_call_target="tpu_custom_call" | custom-call | tf_op jit(solution)/shard_map/step/pallas_call | solution.py:974
  99.4 3.0 %update.1 = (f32[16,256]{1,0:T(8,128)}, f32[16,67]{1,0:T(8,128)}, f32[3,16,768]{2,1,0:T(8,128)}, f32[3,16,256]{2,1,0:T(8,128)}, f32[3,16,512]{2,1,0:T(8,128)}, /...) custom-call(f32[16,6784]{1,0:T(8,128)} %get-tuple-element.56.refs_0_, ...), custom_call_target="tpu_custom_call" | custom-call | tf_op jit(solution)/shard_map/update/pallas_call | solution.py:1050

commit v7 on v6

--- a/solution.py
+++ b/solution.py
@@ -210,13 +210,12 @@
     to_z(1)
     for l in range(LAYERS):
         layers[l, z, y, core, :, C_IN[0] : C_IN[1]] = w_in[l].astype(BF)
-        to_z(2 + 2 * l)
+        if l == 0:
+            to_z(2)
         layers[l, z, y, core, :, C_OUT[0] : C_OUT[1]] = w_out[l].astype(BF)
         layers[l, z, y, core, :, C_UP[0] : C_UP[1]] = w_up[l].astype(BF)
         layers[l, z, y, core, :, C_DOWN[0] : C_DOWN[1]] = w_down[l].astype(BF)
-        to_z(3 + 2 * l)
     rest[z, y, core, :, C_HEAD[0] : C_HEAD[1]] = head[...].astype(BF)
-    to_z(8)
 
     def table(ref, cols):
         piece = ref[..., cols[0] : cols[1]]
@@ -250,7 +249,9 @@
 
     to_y(0)
     to_y(1)
+    to_z(3)
     to_y(2)
+    to_z(4)
     to_core(0)
     to_core(1)
     arrived(0)
@@ -276,6 +277,7 @@
         norm_s[i] = wide[POS + i : POS + i + 1, :]
     wide[...] = jnp.zeros_like(wide)
     to_y(3)
+    to_z(5)
 
     def spread(ref, b0):
         values = ref[...].astype(BF)
@@ -319,6 +321,7 @@
     loop(chunks, embed)
     to_core(2)
     to_y(4)
+    to_z(6)
 
     def keep(k, at, x):
         unit, rstd = normalise(x)
@@ -396,6 +399,8 @@
         copies = [exchange(l, k) for k in range(group - 1)]
         for copy in copies:
             copy.start()
+        if l == 0:
+            to_z(7)
         if l == 1:
             to_core(5)
             to_y(7)
@@ -403,6 +408,7 @@
         if l == 0:
             to_core(3)
             to_y(5)
+            to_z(8)
         if l == 1:
             to_core(6)
         if l == 2:

time: 103 us -> 99.4 us (0.965)
  Pallas kernels: 102 us -> 98.3 us
    pallas_call x1, Pallas kernels: 98.7 us -> 95.4 us  [on_device(): pl.pallas_call(functools.partial(step_kernel, geo, chunk, batch, pack), o...]
where the time goes in v7:
time: 99.4 us; the launch traced here: 99.2 us
  Pallas kernels  98.3 us (99%)
    pallas_call x1, Pallas kernels, on_device(): pl.pallas_call(functools.partial(step_kernel, geo, chunk, batch, pack), o...  95.4 us
    pallas_call x1, Pallas kernels, on_device(): pl.pallas_call(functools.partial(update_kernel, n_rows), out_shape=shapes...  2.96 us

profile of v7, /device:TPU:0, one launch (start us, length us, event | category | flops | bytes accessed | tf_op | source)
XLA Modules:
  0.0 99.2 jit_solution(3340883511232972285)
XLA Ops:
  0.7 95.4 %step.1 = (f32[16,6784]{1,0:T(8,128)}, f32[8,128]{1,0:T(8,128)}) custom-call(s32[8,8,24]{2,1,0:T(8,128)} %bitcast.31, s32[8,8,24]{2,1,0:T(8,128)} %bitcast.32, f32[16,256]{1,0:T(8,128)} %bitcast.27, f32[16,67]{1,0:T(8,128)} %bitcast.29, f32[3,16,768]{2,1,0:T(8,128)} %refs_4_.1, f32[3,16,256]{2,1,0:T(8,128)} %refs_5_.1, f32[3,16,512]{2,1,0:T(8,128)} %refs_6_.1, ...), custom_call_target="tpu_custom_call" | custom-call | tf_op jit(solution)/shard_map/step/pallas_call | solution.py:980
  96.0 3.0 %update.1 = (f32[16,256]{1,0:T(8,128)}, f32[16,67]{1,0:T(8,128)}, f32[3,16,768]{2,1,0:T(8,128)}, f32[3,16,256]{2,1,0:T(8,128)}, f32[3,16,512]{2,1,0:T(8,128)}, /...) custom-call(f32[16,6784]{1,0:T(8,128)} %get-tuple-element.56.refs_0_, ...), custom_call_target="tpu_custom_call" | custom-call | tf_op jit(solution)/shard_map/update/pallas_call | solution.py:1056

commit v8 on v7

--- a/solution.py
+++ b/solution.py
@@ -117,8 +117,8 @@
     return a, half + a * (1.0 - half) * (2.0 * c + (6.0 * 0.044715 * c) * square)
 
 
-def softmax(scores):
-    e = jnp.exp(scores - jnp.max(scores, -1, keepdims=True))
+def softmax(raw):
+    e = jnp.exp2((raw - jnp.max(raw, -1, keepdims=True)) * (SCALE * math.log2(math.e)))
     return e * (1.0 / jnp.sum(e, -1, keepdims=True))
 
 
@@ -286,10 +286,10 @@
             [dot(values, (at == b0 + j).astype(F32).astype(BF)) for j in range(chunk)], 0
         )
 
-    def one_hot(ref, b0):
+    def one_hot(ref, b0, on=1.0, off=0.0):
         value = spread(ref, b0)
         lane = lax.broadcasted_iota(jnp.int32, (rows, 128), 1).astype(F32)
-        return jnp.concatenate([(value == lane).astype(F32), (value == lane + 128.0).astype(F32)], 1)
+        return jnp.concatenate([jnp.where(value == lane, on, off), jnp.where(value == lane + 128.0, on, off)], 1)
 
     def place_hot(b0):
         r = lax.broadcasted_iota(jnp.int32, (rows, 128), 0)
@@ -360,7 +360,7 @@
                 qkv = stage[:, at, :].reshape(side, 3 * HEAD).astype(BF)
                 qkv1_s[l, i * pack + j] = qkv
                 qkvs.append(qkv)
-            raw = [dot_nt(qkv[:, :HEAD], qkv[:, HEAD : 2 * HEAD]) * SCALE + bias1[...] for qkv in qkvs]
+            raw = [dot_nt(qkv[:, :HEAD], qkv[:, HEAD : 2 * HEAD]) + bias1[...] for qkv in qkvs]
             probs = softmax(jnp.concatenate(raw, 0)).astype(BF)
             p1_s[l, pl.ds(i * pack, pack)] = probs.reshape(pack, side, side)
             for j in range(pack):
@@ -372,7 +372,7 @@
             b0 = i * batch
             kv = kv_s[l, pl.ds(b0, batch + 1)].reshape((batch + 1) * STRIDE, 2 * HEAD)
             raw = [
-                dot_nt(q0_s[l, b0 + j], kv[j * STRIDE : (j + 2) * STRIDE, :HEAD]) * SCALE
+                dot_nt(q0_s[l, b0 + j], kv[j * STRIDE : (j + 2) * STRIDE, :HEAD])
                 + bias0[jnp.minimum(b0 + j, 1)]
                 for j in range(batch)
             ]
@@ -439,12 +439,11 @@
         h = (unit * (1.0 + gain) + norm_s[4 * LAYERS + 1]).astype(BF)
         table_head = table(rest, C_HEAD)
         logits = dot(h, table_head)
-        hot = one_hot(tgt_s, b0)
         shift = logits - jnp.max(logits, -1, keepdims=True)
         e = jnp.exp(shift)
         total = jnp.sum(e, -1, keepdims=True)
         weight = spread(msk_s, b0)
-        goal = (1.0 - SMOOTHING) * hot + SMOOTHING / V
+        goal = one_hot(tgt_s, b0, 1.0 - SMOOTHING + SMOOTHING / V, SMOOTHING / V)
         per = jnp.log(total) - jnp.sum(goal * shift, -1, keepdims=True)
         loss = loss + jnp.sum(weight[:, :1] * per, 0, keepdims=True)
         weight = jnp.concatenate([weight, weight], 1)

time: 99.4 us -> 99.1 us (level)
  no operation moved by 1% of the time
where the time goes in v8:
time: 99.1 us; the launch traced here: 98.9 us
  Pallas kernels  98.1 us (99%)
    pallas_call x1, Pallas kernels, on_device(): pl.pallas_call(functools.partial(step_kernel, geo, chunk, batch, pack), o...  95.1 us
    pallas_call x1, Pallas kernels, on_device(): pl.pallas_call(functools.partial(update_kernel, n_rows), out_shape=shapes...  2.96 us

profile of v8, /device:TPU:0, one launch (start us, length us, event | category | flops | bytes accessed | tf_op | source)
XLA Modules:
  0.0 98.9 jit_solution(4154314310970665908)
XLA Ops:
  0.7 95.1 %step.1 = (f32[16,6784]{1,0:T(8,128)}, f32[8,128]{1,0:T(8,128)}) custom-call(s32[8,8,24]{2,1,0:T(8,128)} %bitcast.31, s32[8,8,24]{2,1,0:T(8,128)} %bitcast.32, f32[16,256]{1,0:T(8,128)} %bitcast.27, f32[16,67]{1,0:T(8,128)} %bitcast.29, f32[3,16,768]{2,1,0:T(8,128)} %refs_4_.1, f32[3,16,256]{2,1,0:T(8,128)} %refs_5_.1, f32[3,16,512]{2,1,0:T(8,128)} %refs_6_.1, ...), custom_call_target="tpu_custom_call" | custom-call | tf_op jit(solution)/shard_map/step/pallas_call | solution.py:979
  95.8 3.0 %update.1 = (f32[16,256]{1,0:T(8,128)}, f32[16,67]{1,0:T(8,128)}, f32[3,16,768]{2,1,0:T(8,128)}, f32[3,16,256]{2,1,0:T(8,128)}, f32[3,16,512]{2,1,0:T(8,128)}, /...) custom-call(f32[16,6784]{1,0:T(8,128)} %get-tuple-element.56.refs_0_, ...), custom_call_target="tpu_custom_call" | custom-call | tf_op jit(solution)/shard_map/update/pallas_call | solution.py:1055
